TPU v7x, 32 devices: a whole 2x2x4 slice. The times are simulated.
32 devices in a mesh: section: 2 (over x), dp: 4 (over z), expert: 4 (over y, core).
Axes of the slice: x: 2, y: 2, z: 4, core: 2. Of those that a mesh axis runs over, the one named last changes fastest.
Arguments:
- tokens: bfloat16 [2, 4096, 3584], P('section', ('dp', 'expert')), may hold values from -0.75 to 0.75
- routes: int32 [2, 4096, 2], P('section', ('dp', 'expert')), may hold values from 0 to 3, all different within a row; in each aligned block of 256 rows (0 to 255, 256 to 511, ..., all dimensions but the last counted through in order) at most 160 rows name the same one
- hidden_grad: bfloat16 [2, 4, 4, 640, 1024], P('section', 'dp', 'expert'), may hold values from -1.5 to 1.5
- w_gate: bfloat16 [2, 4, 3584, 1024], P('section', 'expert'), may hold values from -0.75 to 0.75
- w_up: bfloat16 [2, 4, 3584, 1024], P('section', 'expert'), may hold values from -0.75 to 0.75
Outputs:
- passed_grad: bfloat16 [2, 4096, 3584], P('section', ('dp', 'expert'))
- grad_gate: bfloat16 [2, 4, 3584, 1024], P('section', 'expert', 'dp')
- grad_up: bfloat16 [2, 4, 3584, 1024], P('section', 'expert', 'dp')
Inputs may be any that keep to these rules, and one draw needn't show every extreme that they name: `routes`: each token names 2 different experts. Among the 256 tokens of one device at most 160 name the same expert, and in every draw some device's tokens name some expert exactly 160 times.
All inputs are finite; a program needn't handle non-finite values.
Results may differ from a plain program's by a relative error of at most 0.019.
Values may be sent and summed in bfloat16 or wider, within the bound.
No kernel may reach another device: no remote copies, remote signals or barrier semaphores. Data moves between devices by JAX's collectives and lax.ppermute only.
A program may use at most 192 MiB of HBM per device.

v0:
```python
import jax
import jax.numpy as jnp
from jax import lax
from jax.sharding import PartitionSpec as P


def from_behind(value, axis, by):
    count = lax.axis_size(axis)
    return lax.ppermute(value, axis, [(i, (i + by) % count) for i in range(count)])


def slot_numbers(route_rows, experts, capacity):
    marked = (route_rows[:, :, None] == jnp.arange(experts, dtype=jnp.int32)[None, None, :]).astype(
        jnp.int32
    )
    per_token = jnp.sum(marked, axis=1)
    earlier = jnp.cumsum(per_token, axis=0) - per_token
    within = jnp.sum(marked * earlier[:, None, :], axis=2)
    return route_rows * capacity + within


def sender_rows(token_rows, slots, slot_total):
    token_count = token_rows.shape[0]
    top_slots = slots.shape[1]
    owner = jnp.full((slot_total,), token_count, jnp.int32)
    owner = owner.at[slots.reshape(-1)].set(
        jnp.repeat(jnp.arange(token_count, dtype=jnp.int32), top_slots)
    )
    padded = jnp.concatenate(
        [token_rows, jnp.zeros((1, token_rows.shape[1]), token_rows.dtype)], axis=0
    )
    return padded[owner]


def swiglu_grads(grad_hidden, gate_pre, up_pre):
    sigmoid_gate = jax.nn.sigmoid(gate_pre)
    grad_gate_pre = grad_hidden * up_pre * sigmoid_gate * (1.0 + gate_pre * (1.0 - sigmoid_gate))
    grad_up_pre = grad_hidden * gate_pre * sigmoid_gate
    return (grad_gate_pre.astype(jnp.bfloat16), grad_up_pre.astype(jnp.bfloat16))


def shards(tokens, routes, hidden_grad, w_gate, w_up):
    experts = lax.axis_size("expert")
    slot_total = hidden_grad.shape[3]
    capacity = slot_total // experts
    width = tokens.shape[2]
    slots = slot_numbers(routes[0], experts, capacity)
    outgoing = sender_rows(tokens[0], slots, slot_total)
    received = lax.all_to_all(
        outgoing.reshape(experts, capacity, width),
        "expert",
        split_axis=0,
        concat_axis=0,
        tiled=True,
    )
    received = received.reshape(slot_total, width)
    gate_w = w_gate[0, 0]
    up_w = w_up[0, 0]
    hidden = gate_w.shape[1]
    gate_pre = jnp.dot(received, gate_w, preferred_element_type=jnp.float32)
    up_pre = jnp.dot(received, up_w, preferred_element_type=jnp.float32)
    grad_gate_pre, grad_up_pre = swiglu_grads(
        hidden_grad[0, 0, 0].astype(jnp.float32), gate_pre, up_pre
    )
    along_hidden = (((1,), (1,)), ((), ()))
    slot_grad = (
        lax.dot_general(grad_gate_pre, gate_w, along_hidden, preferred_element_type=jnp.float32)
        + lax.dot_general(grad_up_pre, up_w, along_hidden, preferred_element_type=jnp.float32)
    ).astype(jnp.bfloat16)
    returned = lax.all_to_all(
        slot_grad.reshape(experts, capacity, width),
        "expert",
        split_axis=0,
        concat_axis=0,
        tiled=True,
    )
    returned = returned.reshape(slot_total, width)
    token_grad = jnp.sum(returned[slots].astype(jnp.float32), axis=1).astype(jnp.bfloat16)
    passed_grad = from_behind(token_grad[None], "section", -1)
    both_grads = jnp.concatenate([grad_gate_pre, grad_up_pre], axis=1)
    along_slots = (((0,), (0,)), ((), ()))
    summed = lax.psum_scatter(
        lax.dot_general(
            received, both_grads, along_slots, preferred_element_type=jnp.float32
        ).astype(jnp.bfloat16),
        "dp",
        scatter_dimension=0,
        tiled=True,
    ).astype(jnp.float32)
    grad_gate = summed[:, :hidden].astype(jnp.bfloat16)[None, None]
    grad_up = summed[:, hidden:].astype(jnp.bfloat16)[None, None]
    return (passed_grad, grad_gate, grad_up)


def solution(mesh):
    placed = (
        P("section", ("dp", "expert"), None),
        P("section", ("dp", "expert"), None),
        P("section", "dp", "expert", None, None),
        P("section", "expert", None, None),
        P("section", "expert", None, None),
    )
    return jax.shard_map(
        shards,
        mesh=mesh,
        in_specs=placed,
        out_specs=(
            P("section", ("dp", "expert"), None),
            P("section", "expert", "dp", None),
            P("section", "expert", "dp", None),
        ),
        check_vma=False,
    )
```

profile of v0, /device:TPU:0, one launch (start us, length us, event | category | flops | bytes accessed | tf_op | source)
XLA Modules:
  0.0 365.4 jit_solution(17693831958353100302)
XLA Ops:
  7.2 0.0 reduce-scatter.2.cloned.1.call-start
  7.2 0.7 broadcast_multiply_fusion
  7.9 0.7 convert_reduce_fusion
  8.6 1.2 reduce-window.6
  9.8 0.1 slice.22
  9.9 0.1 copy.20
  10.0 0.1 copy.21
  10.1 0.1 add_bitcast_fusion
  10.2 0.7 select_reduce_fusion
  10.9 0.1 copy.22
  11.1 0.1 reduce_sum.36
  11.2 0.1 copy.19
  11.4 0.1 mul.55
  11.5 0.1 reshape.125
  11.7 2.4 scatter_custom_fusion
  14.2 1.6 concatenate.6
  15.8 5.1 %gather_fusion = bf16[640,3584]{1,0:T(8,128)(2,1)} fusion(bf16[257,3584]{1,0:T(8,128)(2,1)S(1)} %concatenate.6, s32[1024]{0:T(1024)S(1)} %pad_clamp_fusion.1), kind=kCustom, calls=%fused_computation | custom fusion | bytes 9177600 | tf_op jit(solution)/shard_map/gather | solution.py:32
  20.9 0.0 copy-start.1
  20.9 0.0 slice-start
  20.9 57.4 %all_to_all.10 = bf16[4,160,3584]{2,1,0:T(8,128)(2,1)S(1)} all-to-all(bf16[4,160,3584]{2,1,0:T(8,128)(2,1)} %bitcast.57), channel_id=1, replica_groups=mesh['section'=2,'dp'=4,'expert'=4] {'expert'}, dimensions={0} | all-to-all | bytes 9175040 | tf_op jit(solution)/shard_map/all_to_all | solution.py:49
  78.3 0.0 copy-done.1
  78.3 0.0 slice-start.1
  78.3 7.7 %fusion.14 = (bf16[640,1024]{1,0:T(8,128)(2,1)S(1)}, f32[640,1024]{1,0:T(8,128)S(1)}) fusion(bf16[1,1,1,640,1024]{4,3,2,1,0:T(8,128)(2,1)S(1)} %copy-done.1, bf16[640,3584]{1,0:T(8,128)(2,1)S(1)} %bitcast.59, bf16[1,1,3584,1024]{3,2,1,0:T(8,128)(2,1)} %param.8), kind=kOutput, calls=%fused_computation.19 | convolution fusion | flops 4702208000 | bytes 17170432 | tf_op jit(solution)/shard_map/dot_general | solution.py:60
  86.0 0.0 slice-done
  86.0 0.0 slice-done.1
  86.0 5.5 %fusion.12 = bf16[640,1024]{1,0:T(8,128)(2,1)S(1)} fusion(f32[640,1024]{1,0:T(8,128)S(1)} %get-tuple-element.6, bf16[640,3584]{1,0:T(8,128)(2,1)S(1)} %bitcast.60, bf16[1,1,3584,1024]{3,2,1,0:T(8,128)(2,1)S(1)} %bitcast.70, bf16[1,1,1,640,1024]{4,3,2,1,0:T(8,128)(2,1)S(1)} %copy-done.1), kind=kOutput, calls=%fused_computation.17 | convolution fusion | flops 4704829440 | bytes 17170432 | tf_op jit(solution)/shard_map/dot_general | solution.py:61
  91.5 14.7 %convolution_convert_fusion = bf16[3584,2048]{1,0:T(8,128)(2,1)} fusion(bf16[640,3584]{1,0:T(8,128)(2,1)S(1)} %bitcast.61, bf16[640,1024]{1,0:T(8,128)(2,1)S(1)} %get-tuple-element.5, bf16[640,1024]{1,0:T(8,128)(2,1)S(1)} %fusion.12), kind=kOutput, calls=%fused_computation.3 | convolution fusion | flops 9407823872 | bytes 21889024 | tf_op jit(solution)/shard_map/dot_general | solution.py:83
  106.2 0.0 reduce-scatter.2.cloned.1.call-update
  106.2 10.5 %fusion = f32[640,3584]{1,0:T(8,128)} fusion(bf16[640,1024]{1,0:T(8,128)(2,1)S(1)} %fusion.12, bf16[1,1,3584,1024]{3,2,1,0:T(8,128)(2,1)} %param.8), kind=kOutput, calls=%fused_computation.5 | convolution fusion | flops 4697620480 | bytes 17825792 | tf_op jit(solution)/shard_map/dot_general | solution.py:67
  116.8 11.0 %add_convert_fusion = bf16[640,3584]{1,0:T(8,128)(2,1)} fusion(f32[640,3584]{1,0:T(8,128)} %fusion, bf16[640,1024]{1,0:T(8,128)(2,1)S(1)} %get-tuple-element.5, bf16[1,1,3584,1024]{3,2,1,0:T(8,128)(2,1)} %param.9), kind=kOutput, calls=%fused_computation.4 | convolution fusion | flops 4702208000 | bytes 22413312 | tf_op jit(solution)/shard_map/dot_general | solution.py:68
  127.8 0.0 copy-start
  127.8 5.1 %all-to-all-start.1 = ((bf16[4,160,3584]{2,1,0:T(8,128)(2,1)}), bf16[4,160,3584]{2,1,0:T(8,128)(2,1)}, u32[]{:S(2)}, u32[]{:S(2)}) async-start(bf16[4,160,3584]{2,1,0:T(8,128)(2,1)} %bitcast.58), calls=%async_computation.1 | async-start | bytes 9175040 | tf_op jit(solution)/shard_map/all_to_all | solution.py:70
  132.9 0.0 copy-done
  132.9 0.1 copy.23
  133.1 0.1 reshape.115
  133.2 52.1 %all-to-all-done.1 = bf16[4,160,3584]{2,1,0:T(8,128)(2,1)} async-done(((bf16[4,160,3584]{2,1,0:T(8,128)(2,1)}), bf16[4,160,3584]{2,1,0:T(8,128)(2,1)}, u32[]{:S(2)}, u32[]{:S(2)}) %all-to-all-start.1) | async-done | bytes 4587552 | tf_op jit(solution)/shard_map/all_to_all | solution.py:70
  185.3 10.8 %gather_fusion.1 = bf16[512,3584]{1,0:T(8,128)(2,1)} fusion(bf16[640,3584]{1,0:T(8,128)(2,1)} %bitcast.13, s32[1024]{0:T(1024)S(1)} %pad_clamp_fusion), kind=kCustom, calls=%fused_computation.1 | custom fusion | bytes 7342080 | tf_op jit(solution)/shard_map/gather | solution.py:78
  196.2 8.1 %reshape.118 = bf16[256,2,3584]{2,1,0:T(2,128)(2,1)} reshape(bf16[512,3584]{1,0:T(8,128)(2,1)} %gather_fusion.1) | data formatting | bytes 7340032 | tf_op jit(solution)/shard_map/gather | solution.py:78
  204.3 11.3 %reduce_sum.38 = bf16[256,3584]{1,0:T(8,128)(2,1)} reduce(bf16[256,2,3584]{2,1,0:T(2,128)(2,1)} %reshape.118, bf16[]{:T(256)} %constant.7.clone.1), dimensions={1}, to_apply=%region_5.6 | reduce | flops 917504 | bytes 5505026 | tf_op jit(solution)/shard_map/reduce_sum | solution.py:78
  215.6 2.2 collective-permute-start
  217.8 40.0 %collective-permute-done = bf16[1,256,3584]{2,1,0:T(8,128)(2,1)S(1)} collective-permute-done((bf16[1,256,3584]{2,1,0:T(8,128)(2,1)}, bf16[1,256,3584]{2,1,0:T(8,128)(2,1)S(1)}, u32[]{:S(2)}, u32[]{:S(2)}) %collective-permute-start) | collective-permute-done | bytes 1835040 | tf_op jit(solution)/shard_map/ppermute | solution.py:9
  257.8 95.2 %reduce-scatter.2.cloned.1.call-done = bf16[896,2048]{1,0:T(8,128)(2,1)} async-done(((bf16[3584,2048]{1,0:T(8,128)(2,1)}), bf16[896,2048]{1,0:T(8,128)(2,1)}) %reduce-scatter.2.cloned.1.call-update) | async-done | bytes 3670032 | tf_op jit(solution)/shard_map/reduce_scatter | solution.py:82
  353.0 4.3 %slice_bitcast_fusion = (bf16[1,1,896,1024]{3,2,1,0:T(8,128)(2,1)}, bf16[1,1,896,1024]{3,2,1,0:T(8,128)(2,1)}) fusion(bf16[896,2048]{1,0:T(8,128)(2,1)} %reduce-scatter.2.cloned.1.call-done), kind=kLoop, calls=%fused_computation.24 | loop fusion | bytes 7340032 | tf_op jit(solution)/shard_map/broadcast_in_dim | solution.py:91
  357.3 1.2 copy.27
  (11 shorter events, 0.1 us)
Async XLA Ops:
  7.2 345.9 %reduce-scatter.2.cloned.1.call-start = ((), (), s32[]{:S(2)}) async-start(), calls=%async_computation.3 | async-start | bytes 18350080 | tf_op jit(solution)/shard_map/reduce_scatter | solution.py:82
  20.9 57.4 %copy-start.1 = (bf16[1,1,1,640,1024]{4,3,2,1,0:T(8,128)(2,1)S(1)}, bf16[1,1,1,640,1024]{4,3,2,1,0:T(8,128)(2,1)}, u32[]{:S(2)}) copy-start(bf16[1,1,1,640,1024]{4,3,2,1,0:T(8,128)(2,1)} %param.7) | copy-start | bytes 3932164
  20.9 65.1 %slice-start = ((s8[7340032]{0:T(1024)(128)(4,1)}), s8[4194304]{0:T(1024)(128)(4,1)S(1)}, s32[]{:S(2)}) async-start(s8[7340032]{0:T(1024)(128)(4,1)} %bitcast.69), calls=%async_computation.4 | async-start | bytes 8388608
  78.3 7.7 %slice-start.1 = ((s8[7340032]{0:T(1024)(128)(4,1)}), s8[3145728]{0:T(1024)(128)(4,1)S(1)}, s32[]{:S(2)}) async-start(s8[7340032]{0:T(1024)(128)(4,1)} %bitcast.69), calls=%async_computation.5 | async-start | bytes 6291456
  127.8 5.1 %copy-start = (s32[1,256,2]{1,2,0:T(2,128)S(1)}, s32[1,256,2]{1,2,0:T(2,128)}, u32[]{:S(2)}) copy-start(s32[1,256,2]{1,2,0:T(2,128)} %param.6) | copy-start | bytes 6148
  127.8 57.5 %all-to-all-start.1 = ((bf16[4,160,3584]{2,1,0:T(8,128)(2,1)}), bf16[4,160,3584]{2,1,0:T(8,128)(2,1)}, u32[]{:S(2)}, u32[]{:S(2)}) async-start(bf16[4,160,3584]{2,1,0:T(8,128)(2,1)} %bitcast.58), calls=%async_computation.1 | async-start | bytes 9175040 | tf_op jit(solution)/shard_map/all_to_all | solution.py:70
  215.6 42.2 %collective-permute-start = (bf16[1,256,3584]{2,1,0:T(8,128)(2,1)}, bf16[1,256,3584]{2,1,0:T(8,128)(2,1)S(1)}, u32[]{:S(2)}, u32[]{:S(2)}) collective-permute-start(bf16[1,256,3584]{2,1,0:T(8,128)(2,1)} %bitcast.63), channel_id=1, source_target_pairs={{0,16},{16,0},{1,17},{17,1},{2,18},{18,2},{3,19},{19,3},{4,20},{20... | collective-permute-start | bytes 5505032 | tf_op jit(solution)/shard_map/ppermute | solution.py:9
Sparse Core Ops, SparseCore 0:
  106.4 246.6 reduce-scatter.1
where the time goes:
time: 366 us; the launch traced here: 365 us
  waiting for transfers between devices  187 us (51%)
  blocking collectives  57.4 us (16%)
  matrix products  49.5 us (14%)
  local copies, waits for them, and re-layouts  34.9 us (10%)
  other arithmetic  14.8 us (4%)
  between operations  14.2 us (4%)
  starting transfers between devices  7.29 us (2%)
    reduce_scatter x1, waiting for transfers between devices, shards(): lax.psum_scatter(lax.dot_general(received, both_grads, along_slots, prefe...  95.2 us
    all_to_all x1, blocking collectives, shards(): lax.all_to_all(outgoing.reshape(experts, capacity, width), 'expert', spli...  57.4 us
    all_to_all x1, waiting for transfers between devices, shards(): lax.all_to_all(slot_grad.reshape(experts, capacity, width), 'expert', spl...  52.1 us
    ppermute x1, waiting for transfers between devices, from_behind(): lax.ppermute(value, axis, [(i, (i + by) % count) for i in range(count)])  40 us
    gather x2, local copies, waits for them, and re-layouts, shards(): returned[slots].astype(jnp.float32)  18.9 us
    dot_general x1, matrix products, shards(): lax.dot_general(received, both_grads, along_slots, preferred_element_type...  14.7 us
    reduce_sum x1, other arithmetic, shards(): jnp.sum(returned[slots].astype(jnp.float32), axis=1).astype(jnp.bfloat16)  11.3 us
    dot_general x1, matrix products, shards(): lax.dot_general(grad_up_pre, up_w, along_hidden, preferred_element_type=j...  11 us
  transfers between devices with their start and end apart: 3, of which 3 were waited for; matrix products, arithmetic and copies ran while one was open for 14% of the time, Pallas kernels for 0%

commit v1 on v0

v1 whole, which is shorter than its diff:
```python
import jax
import jax.numpy as jnp
from jax import lax
from jax.experimental import pallas as pl
from jax.experimental.pallas import tpu as pltpu
from jax.sharding import PartitionSpec as P

BF16 = jnp.bfloat16
F32 = jnp.float32
VMEM_LIMIT = 56 * 1024 * 1024


def dot(a, b, contract=((1,), (0,))):
    return lax.dot_general(a, b, (contract, ((), ())), preferred_element_type=F32)


def grouped_pairs(count):
    first, last = 0, count - 1
    sets = []
    inner = range(1, last)
    for j, i in sorted(((j, i) for j in inner for i in inner if j != i), key=lambda p: (abs(p[0] - p[1]), p)):
        for chosen in sets:
            if all(j != a and i != b for a, b in chosen):
                chosen.append((j, i))
                break
        else:
            sets.append([(j, i)])
    out = [[(first, 1), (last, last - 1)]]
    for chosen in sets:
        out.append(chosen)
        out.append([({1: first, last - 1: last}[j], i) for j, i in chosen if j in (1, last - 1)])
    return out


def target_in(pairs, index):
    found = jnp.int32(0)
    for source, target in pairs:
        found = jnp.where(index == source, target, found)
    return found


def call(body, name, scalars, ins, in_specs, outs, out_specs, grid, scratch=(), after=(), aliases=None):
    count, skip = len(ins), len(after)

    def kernel(scalar_ref, *refs):
        body(scalar_ref, refs[:count], refs[count + skip :])

    return pl.pallas_call(
        kernel,
        name=name,
        out_shape=[jax.ShapeDtypeStruct(shape, dtype) for shape, dtype in outs],
        grid_spec=pltpu.PrefetchScalarGridSpec(
            num_scalar_prefetch=1,
            grid=grid,
            in_specs=list(in_specs) + [pl.BlockSpec(memory_space=pl.ANY)] * skip,
            out_specs=list(out_specs),
            scratch_shapes=list(scratch),
        ),
        input_output_aliases=aliases or {},
        compiler_params=pltpu.CompilerParams(
            dimension_semantics=("arbitrary",) * len(grid), vmem_limit_bytes=VMEM_LIMIT
        ),
        cost_estimate=pl.CostEstimate(flops=1, bytes_accessed=1, transcendentals=0),
    )(jnp.stack(scalars).astype(jnp.int32), *ins, *after)


def whole(shape):
    return pl.BlockSpec(shape, lambda j, s: (0,) * len(shape))


def earlier_mask(token_count):
    first = lax.broadcasted_iota(jnp.int32, (token_count, token_count), 0)
    second = lax.broadcasted_iota(jnp.int32, (token_count, token_count), 1)
    return jnp.where(first < second, 1.0, 0.0).astype(BF16)


def pair_in(ref, token_count):
    return ref[token_count:, :token_count].astype(F32).astype(jnp.int32)


def slot_marks(pair, expert, capacity, earlier):
    token_count = pair.shape[1]
    named = (pair[0:1] == expert) | (pair[1:2] == expert)
    named = jnp.broadcast_to(jnp.where(named, 1.0, 0.0), (capacity, token_count))
    rank = dot(named.astype(BF16), earlier)
    slot = lax.broadcasted_iota(jnp.int32, (capacity, token_count), 0).astype(F32)
    return jnp.where(rank == slot, named, 0.0).astype(BF16)


ROUTE_ROWS = 16


def cut_columns(rows, pair, group, targets, groups, block):
    def end_of(index):
        return jnp.where(index < groups // 2, 0, groups - 1)

    token_count, width = rows.shape
    lines = token_count + ROUTE_ROWS
    if block % 128:
        wide = -(-block // 128) * 128

        def tail(columns):
            return jnp.pad(pair.astype(BF16), ((0, ROUTE_ROWS - 2), (0, columns - token_count)))

        def cut(index):
            return jnp.concatenate([cut_padded(rows, [index], block, wide), tail(wide)], axis=0)

        return [jnp.concatenate([rows, tail(width)], axis=0)] + [
            jnp.concatenate([cut(t)] + ([cut(end_of(t))] if k else []), axis=1) for k, t in enumerate(targets)
        ]
    scalars = targets + [end_of(t) for t in targets[1:]]
    count = len(targets)

    def body(s, ins, outs):
        held = jnp.concatenate([ins[0][...].astype(F32), jnp.zeros((ROUTE_ROWS - 2, token_count), F32)], axis=0)
        for i, o in zip(ins[1:], outs):
            o[:token_count] = i[...]
            o[token_count:] = jnp.zeros((ROUTE_ROWS, block), BF16)
            o[token_count:, :token_count] = held.astype(BF16)

    def from_block(k):
        if k == 0:
            return lambda j, s: (0, s[0])
        return lambda j, s: (0, jnp.where(j == 0, s[k], s[count + k - 1]))

    return call(
        body,
        "cut_columns",
        scalars,
        [pair] + [rows] * (count + 1),
        [whole(pair.shape), pl.BlockSpec((token_count, block), lambda j, s: (0, j))]
        + [pl.BlockSpec((token_count, block), from_block(k)) for k in range(count)],
        [((lines, width), BF16)] + [((lines, block * (1 if k == 0 else 2)), BF16) for k in range(count)],
        [pl.BlockSpec((lines, block), lambda j, s: (0, j))]
        + [
            pl.BlockSpec(
                (lines, block), (lambda j, s: (0, 0)) if k == 0 else (lambda j, s: (0, jnp.minimum(j, 1)))
            )
            for k in range(count)
        ],
        (groups,),
    )


def cut_padded(rows, indices, block, wide):
    pieces = [lax.dynamic_slice_in_dim(rows, i * block, block, axis=1) for i in indices]
    return jnp.concatenate([jnp.pad(p, ((0, 0), (0, wide - block))) for p in pieces], axis=1)


def forward(expert, places, rows, upstream, gate_w, up_w, up_parts, first=None, after=()):
    sources = len(rows)
    lines, width = rows[0].shape
    token_count = lines - ROUTE_ROWS
    slots, hidden = upstream.shape
    capacity = slots // len(places)
    skip = 0 if first is None else len(places) - sources
    used = places[skip : skip + sources]
    step = 256 if hidden % 256 == 0 else hidden
    count = sources * capacity
    lead = skip * capacity
    spans, at = [], 0
    for size in up_parts:
        spans.append((at // step, (at + size) // step))
        at += size

    def body(s, ins, refs):
        tok = ins[:sources]
        up_ref, wg, wu = ins[sources : sources + 3]
        gate_out, up_outs, received = refs[0], refs[1:-1], refs[-1]
        j = pl.program_id(0)

        @pl.when(pl.program_id(0) == 0)
        def _():
            earlier = earlier_mask(token_count)
            for r in range(sources):
                mark = slot_marks(pair_in(tok[r], token_count), s[0], capacity, earlier)
                received[r * capacity : (r + 1) * capacity] = dot(mark, tok[r][:token_count]).astype(BF16)

        gate = dot(received[...], wg[...])
        up = dot(received[...], wu[...])
        for r in range(sources):
            here = slice(r * capacity, (r + 1) * capacity)
            g = gate[here]
            h = up_ref[pl.ds(pl.multiple_of(s[1 + r] * capacity, 16), capacity), :].astype(F32)
            sig = jax.nn.sigmoid(g)
            gate_out[here] = (h * up[here] * sig * (1.0 + g * (1.0 - sig))).astype(BF16)
            up_grad = (h * g * sig).astype(BF16)
            for (low, high), out in zip(spans, up_outs):

                @pl.when((j >= low) & (j < high))
                def _():
                    out[lead + r * capacity : lead + (r + 1) * capacity] = up_grad

        if first is not None:
            for (low, high), out in zip(spans, up_outs):

                @pl.when((j >= low) & (j < high))
                def _():
                    out[:lead] = ins[sources + 3][...]

    ins = list(rows) + [upstream, gate_w, up_w]
    specs = [whole((lines, width))] * sources
    specs += [pl.BlockSpec((slots, step), lambda j, s: (0, j))]
    specs += [pl.BlockSpec((width, step), lambda j, s: (0, j))] * 2
    if first is not None:
        ins.append(first)
        specs.append(pl.BlockSpec((lead, step), lambda j, s: (0, j)))
    return call(
        body,
        "forward_first" if first is None else "forward_rest",
        [expert] + used,
        ins,
        specs,
        [((count, hidden), BF16)] + [((lead + count, size), BF16) for size in up_parts],
        [pl.BlockSpec((count, step), lambda j, s: (0, j))]
        + [
            pl.BlockSpec((lead + count, step), lambda j, s, a=low, b=high: (0, jnp.clip(j - a, 0, b - a - 1)))
            for low, high in spans
        ],
        (hidden // step,),
        scratch=[pltpu.VMEM((count, width), BF16)],
        after=after,
    )


def halves_of(width):
    step = 512 if width % 512 == 0 else 128
    steps = width // step
    return step, steps, (steps + 1) // 2


def slot_gradients(places, gate_parts, up_parts, gate_w, up_w, after=()):
    width, hidden = gate_w.shape
    slots = up_parts[0].shape[0]
    capacity = slots // len(places)
    gates = len(gate_parts)
    step, steps, lead = halves_of(width)

    def body(s, ins, outs):
        j = pl.program_id(0)
        wg, wu = ins[-2], ins[-1]
        across = ((1,), (1,))
        total = jnp.concatenate([dot(g[...], wg[...], across) for g in ins[:gates]], axis=0)
        at = 0
        for g in ins[gates:-2]:
            size = g.shape[1]
            total = total + dot(g[...], wu[:, at : at + size], across)
            at += size
        total = total.astype(BF16)

        def put(out):
            for r in range(len(places)):
                at = pl.ds(pl.multiple_of(s[r] * capacity, 16), capacity)
                out[at, :] = total[r * capacity : (r + 1) * capacity]

        @pl.when(j < lead)
        def _():
            put(outs[0])

        @pl.when(j >= lead)
        def _():
            put(outs[1])

    return call(
        body,
        "slot_gradients",
        places,
        list(gate_parts) + list(up_parts) + [gate_w, up_w],
        [whole(g.shape) for g in list(gate_parts) + list(up_parts)]
        + [pl.BlockSpec((step, hidden), lambda j, s: (j, 0))] * 2,
        [((slots, lead * step), BF16), ((slots, width - lead * step), BF16)],
        [
            pl.BlockSpec((slots, step), lambda j, s: (0, jnp.minimum(j, lead - 1))),
            pl.BlockSpec((slots, step), lambda j, s: (0, jnp.maximum(j - lead, 0))),
        ],
        (steps,),
        after=after,
    )


def combine(pair, returned, experts, after=()):
    token_count = pair.shape[1]
    slots, width = returned.shape
    capacity = slots // experts
    step = 512 if width % 512 == 0 else 128

    def body(s, ins, refs):
        marks = refs[-1]

        @pl.when(pl.program_id(0) == 0)
        def _():
            earlier = earlier_mask(token_count)
            for r in range(experts):
                marks[r * capacity : (r + 1) * capacity] = slot_marks(ins[0][...], r, capacity, earlier)

        refs[0][...] = dot(marks[...], ins[1][...], ((0,), (0,))).astype(BF16)

    return call(
        body,
        "combine",
        [jnp.int32(0)],
        [pair, returned],
        [whole(pair.shape), pl.BlockSpec((slots, step), lambda j, s: (0, j))],
        [((token_count, width), BF16)],
        [pl.BlockSpec((token_count, step), lambda j, s: (0, j))],
        (width // step,),
        scratch=[pltpu.VMEM((slots, token_count), BF16)],
        after=after,
    )[0]


def pick_rows(expert, blocks, rows, capacity, block, routes=None, after=()):
    sources = len(rows)
    lines = rows[0].shape[0]
    token_count = lines - ROUTE_ROWS
    count = len(blocks)

    def body(s, ins, outs):
        earlier = earlier_mask(token_count)
        picked = []
        for r in range(sources):
            pair = pair_in(ins[r], token_count) if routes is None else ins[sources + r][...]
            pair = pair.astype(F32).astype(jnp.int32)
            mark = slot_marks(pair, s[0], capacity, earlier)
            picked.append(dot(mark, ins[r][:token_count]))
        outs[0][...] = jnp.concatenate(picked, axis=0).astype(BF16).T

    ins, specs = list(rows), []
    for r in range(sources):
        specs.append(pl.BlockSpec((lines, block), lambda j, s: (0, s[1 + j])))
    if routes is not None:
        ins += list(routes)
        specs += [
            pl.BlockSpec((ROUTE_ROWS, token_count), lambda j, s: (token_count // ROUTE_ROWS, 0)) for _ in routes
        ]
    return call(
        body,
        "pick_rows",
        [expert] + list(blocks),
        ins,
        specs,
        [((count * block, sources * capacity), BF16)],
        [pl.BlockSpec((block, sources * capacity), lambda j, s: (j, 0))],
        (count,),
        after=after,
    )[0]


def products(terms, block, part, dtype, name, extras=(), total=None, after=()):
    slots = terms[0][0].shape[1]
    split = 2 if block % 32 == 0 else 1
    lines = block // split

    def body(s, ins, outs):
        at, result = len(terms), None
        for k, (_, _, parts) in enumerate(terms):
            row = 0
            for _ in parts:
                g = ins[at]
                new = dot(ins[k][:, row : row + g.shape[0]] if len(parts) > 1 else ins[k][...], g[...])
                result = new if result is None else result + new
                row += g.shape[0]
                at += 1
        if extras:
            result = result + jnp.concatenate([e[...].astype(F32) for e in ins[at:]], axis=1)
        outs[0][...] = result.astype(dtype)

    ins = [p for p, _, _ in terms]
    specs = [pl.BlockSpec((lines, slots), lambda j, s, i=i: (i * split + j, 0)) for _, i, _ in terms]
    for _, _, parts in terms:
        for array, column in parts:
            ins.append(array)
            specs.append(pl.BlockSpec((array.shape[0], part), lambda j, s, c=column: (0, c)))
    for e in extras:
        ins.append(e)
        specs.append(pl.BlockSpec((lines, e.shape[1]), lambda j, s: (j, 0)))
    return call(
        body,
        name,
        [jnp.int32(0)],
        ins,
        specs,
        [((block, total or part), dtype)],
        [pl.BlockSpec((lines, part), lambda j, s: (j, 0))],
        (split,),
        after=after,
    )[0]


def finish(own, extra, target, place, total, after=()):
    block, part = own.shape
    ins = [own, extra]
    specs = [whole((block, part))] * 2
    if target is not None:
        ins.append(target)
        specs.append(pl.BlockSpec(memory_space=pl.ANY))

    def body(s, refs, outs):
        outs[0][...] = (refs[0][...] + refs[1][...].astype(F32)).astype(BF16)

    return call(
        body,
        "finish",
        [jnp.int32(0)],
        ins,
        specs,
        [((block, total), BF16)],
        [pl.BlockSpec((block, part), lambda j, s: (0, place))],
        (1,),
        after=after,
        aliases={3: 0} if target is not None else None,
    )[0]


def tied(value, *others):
    return lax.optimization_barrier((value,) + others)[0]


def shards(tokens, routes, hidden_grad, w_gate, w_up):
    groups = lax.axis_size("dp")
    experts = lax.axis_size("expert")
    sections = lax.axis_size("section")
    group = lax.axis_index("dp")
    expert = lax.axis_index("expert")
    rows = tokens[0]
    token_count, width = rows.shape
    slots = hidden_grad.shape[3]
    capacity = slots // experts
    hidden = w_gate.shape[3]
    block = width // groups
    gate_w = w_gate[0, 0]
    up_w = w_up[0, 0]
    upstream = hidden_grad[0, 0, 0]
    sets = grouped_pairs(groups)
    up_parts = [hidden // 2, hidden // 2]
    wide = -(-block // 128) * 128
    own_blocks = [group, jnp.where(group < groups // 2, 0, groups - 1)]

    def swap(value):
        return lax.ppermute(value, "expert", [(s, s ^ 1) for s in range(experts)])

    def shift(value, by):
        return lax.ppermute(value, "expert", [(s, (s + 2 * by) % experts) for s in range(experts)])

    def over_groups(value, pairs):
        return lax.ppermute(value, "dp", pairs)

    def to_sources(value):
        back = lax.all_to_all(
            value.reshape(experts, capacity, value.shape[1]), "expert", split_axis=0, concat_axis=0, tiled=True
        )
        return back.reshape(value.shape)

    def passed_on(value):
        return lax.ppermute(value, "section", [(s, (s - 1) % sections) for s in range(sections)])

    def to_ends(value):
        return lax.ppermute(value, "dp", [(1, 0), (groups - 2, groups - 1)])

    chips = range(1, experts // 2)
    places = [jnp.bitwise_xor((expert - 2 * (r // 2)) % experts, r % 2) for r in range(experts)]
    targets = [target_in(pairs, group) for pairs in sets]
    order = list(range(1, len(sets))) + [0]

    pair = routes[0].T
    own, *cut = cut_columns(rows, pair, group, targets, groups, block)
    far_even = [shift(own, by) for by in chips]
    others = {k: over_groups(cut[k], sets[k]) for k in order}
    partner = swap(own)
    near_gate, near_up = forward(expert, places, [own, partner], upstream, gate_w, up_w, [hidden])
    epoch = [others[k] for k in order] + far_even + [near_gate]

    near_sent = {k: over_groups(tied(near_gate, *epoch), sets[k]) for k in order}
    far = []
    for value in far_even:
        far += [value, swap(tied(value, *epoch))]
    end_columns = jnp.concatenate([others[k][:, wide:] for k in range(1, len(sets))], axis=1)
    own_part = jnp.concatenate([others[k][:, :wide] for k in range(len(sets))], axis=1)
    end_columns = tied(end_columns, *epoch)
    end_far = [shift(end_columns, by) for by in chips]
    far_gate, *ups = forward(
        expert,
        places,
        far,
        upstream,
        gate_w,
        up_w,
        up_parts,
        first=near_up,
        after=[near_gate, end_columns],
    )
    end_rows = [end_columns, swap(tied(end_columns, *far))]
    epoch = [near_sent[k] for k in order] + end_far + [far_gate, end_rows[1]]

    far_sent = {k: over_groups(tied(far_gate, *epoch), sets[k]) for k in order}
    for value in end_far:
        end_rows += [value, swap(tied(value, *epoch))]
    own_part = tied(own_part, *epoch)
    column_rows = [own_part]
    column_far = [shift(own_part, by) for by in chips]
    first_back, second_back = slot_gradients(
        places, [near_gate, far_gate], ups, gate_w, up_w, after=[end_rows[-1]]
    )
    first_back = to_sources(first_back)
    own_columns = [own, partner] + far
    own_lines = own_columns
    if wide != block:
        own_columns = [cut_padded(v, own_blocks, block, wide) for v in own_columns]
        own_blocks = [jnp.int32(0), jnp.int32(1)]
    own_picked = pick_rows(
        expert, own_blocks, own_columns, capacity, wide, routes=own_lines, after=[second_back]
    )
    column_rows.append(swap(tied(own_part, *end_rows)))
    end_picked = pick_rows(
        expert, [jnp.int32(k) for k in range(len(sets) - 1)], end_rows, capacity, wide, after=[own_picked]
    )
    epoch = [far_sent[k] for k in order] + [end_picked] + column_far + column_rows

    def parts_of(c):
        if c < 2:
            out = [[(near_gate, c), (far_gate, c)]]
            out += [[(near_sent[k], c), (far_sent[k], c)] for k in range(len(sets))]
        else:
            out = [[(ups[c - 2], 0)]] + [[(up_sent[c - 2][k], 0)] for k in range(len(sets))]
        return out

    def for_end(c, after):
        parts = parts_of(c)
        part = hidden // 2 if c < 2 else up_parts[c - 2]
        terms = [(own_picked, 1, parts[0])]
        terms += [(end_picked, k - 1, parts[1 + k]) for k in range(1, len(sets))]
        return products(terms, wide, part, BF16, "for_end", after=after)

    def for_own(c, part, dtype, after, extras=(), total=None):
        parts = parts_of(c)
        terms = [(own_picked, 0, parts[0])]
        terms += [(picked, k, parts[1 + k]) for k in range(len(sets))]
        return products(terms, wide, part, dtype, "for_own", extras=extras, total=total, after=after)

    up_sent = []

    def send_up(c):
        up_sent.append({k: over_groups(tied(ups[c], *epoch), sets[k]) for k in order})
        return [up_sent[c][k] for k in order]

    arriving = send_up(0)
    for value in column_far:
        column_rows += [value, swap(tied(value, *epoch))]
    end0 = for_end(0, epoch[:1])
    extra0 = to_ends(end0)
    end1 = for_end(1, [end0])
    extra1 = to_ends(tied(end1, *column_rows))
    picked = pick_rows(
        expert, [jnp.int32(k) for k in range(len(sets))], column_rows, capacity, wide, after=[end1]
    )
    epoch = arriving + [picked, extra0]

    arriving = send_up(1)
    second_back = to_sources(tied(second_back, first_back, *epoch))
    end2 = for_end(2, epoch[:1])
    extra2 = to_ends(end2)
    first_tok = combine(pair, first_back, experts, after=[end2])
    first_passed = passed_on(tied(first_tok, extra1))
    gate = for_own(0, hidden, BF16, [first_tok], extras=[extra0, extra1])
    epoch = arriving + [gate]

    end3 = for_end(3, epoch)
    extra3 = to_ends(end3)
    second_tok = combine(pair, second_back, experts, after=[end3])
    second_passed = passed_on(second_tok)
    up0 = for_own(2, up_parts[0], BF16, [second_tok], extras=[extra2], total=hidden)
    own3 = for_own(3, up_parts[1], F32, [up0])
    passed = jnp.concatenate([tied(first_passed, own3), second_passed], axis=1)
    up1 = finish(own3, extra3, up0, up_parts[0] // up_parts[1], hidden)
    return (passed[None], gate[None, None, :block], up1[None, None, :block])


def solution(mesh):
    placed = (
        P("section", ("dp", "expert"), None),
        P("section", ("dp", "expert"), None),
        P("section", "dp", "expert", None, None),
        P("section", "expert", None, None),
        P("section", "expert", None, None),
    )
    return jax.shard_map(
        shards,
        mesh=mesh,
        in_specs=placed,
        out_specs=(
            P("section", ("dp", "expert"), None),
            P("section", "expert", "dp", None),
            P("section", "expert", "dp", None),
        ),
        check_vma=False,
    )
```

time: 366 us -> 273 us (0.75)
  waiting for transfers between devices: 187 us -> 50.5 us
  Pallas kernels: 0 us -> 129 us
  starting transfers between devices: 7.29 us -> 73.2 us
  blocking collectives: 57.4 us -> 0 us
  matrix products: 49.5 us -> 0 us
  local copies, waits for them, and re-layouts: 34.9 us -> 9.61 us
  between operations: 14.2 us -> 1.13 us
  other arithmetic: 14.8 us -> 8.56 us
    pallas_call x0 -> x17, Pallas kernels: none -> 129 us  [call(): pl.pallas_call(kernel, name=name, out_shape=[jax.ShapeDtypeStruct(shape,...]
    reduce_scatter x1 -> x0, waiting for transfers between devices: 95.2 us -> none  [shards(): lax.psum_scatter(lax.dot_general(received, both_grads, along_slots, prefe...]
    ppermute x1 -> x30, starting transfers between devices: 2.18 us -> 64.9 us  [the longest x15 50.6 us: over_groups(): return lax.ppermute(value, 'dp', pairs)]
    all_to_all x1 -> x0, blocking collectives: 57.4 us -> none  [shards(): lax.all_to_all(outgoing.reshape(experts, capacity, width), 'expert', spli...]
    all_to_all x1 -> x2, waiting for transfers between devices: 52.1 us -> 0.01 us  [to_sources(): lax.all_to_all(value.reshape(experts, capacity, value.shape[1]), 'expert'...]
    dot_general x5 -> x0, matrix products: 49.5 us -> none  [the longest x1 14.7 us: shards(): lax.dot_general(received, both_grads, along_slots, preferred_element_type...]
    gather x3 -> x0, local copies, waits for them, and re-layouts: 24 us -> none  [the longest x2 18.9 us: shards(): returned[slots].astype(jnp.float32)]
    reduce_sum x3 -> x0, other arithmetic: 12.7 us -> none  [the longest x1 11.3 us: shards(): jnp.sum(returned[slots].astype(jnp.float32), axis=1).astype(jnp.bfloat16)]
  transfers between devices with their start and end apart: 3 -> 32, of which waited for: 3 -> 6; matrix products, arithmetic and copies ran while one was open for 14% -> 3% of each run, Pallas kernels for 0% -> 45%
where the time goes in v1:
time: 273 us; the launch traced here: 272 us
  Pallas kernels  129 us (47%)
  starting transfers between devices  73.2 us (27%)
  waiting for transfers between devices  50.5 us (18%)
  local copies, waits for them, and re-layouts  9.61 us (4%)
  other arithmetic  8.56 us (3%)
    pallas_call x17, Pallas kernels, call(): pl.pallas_call(kernel, name=name, out_shape=[jax.ShapeDtypeStruct(shape,...  129 us
    ppermute x15, starting transfers between devices, over_groups(): return lax.ppermute(value, 'dp', pairs)  50.6 us
    ppermute x15, waiting for transfers between devices, over_groups(): return lax.ppermute(value, 'dp', pairs)  37.9 us
    all_to_all x2, starting transfers between devices, to_sources(): lax.all_to_all(value.reshape(experts, capacity, value.shape[1]), 'expert'...  8.3 us
    ppermute x4, waiting for transfers between devices, to_ends(): return lax.ppermute(value, 'dp', [(1, 0), (groups - 2, groups - 1)])  8.25 us
    unnamed x54, local copies, waits for them, and re-layouts  6.26 us
    ppermute x3, starting transfers between devices, shift(): lax.ppermute(value, 'expert', [(s, (s + 2 * by) % experts) for s in range...  5.82 us
  transfers between devices with their start and end apart: 32, of which 6 were waited for; matrix products, arithmetic and copies ran while one was open for 3% of the time, Pallas kernels for 45%

profile of v1, /device:TPU:0, one launch (start us, length us, event | category | flops | bytes accessed | tf_op | source)
XLA Modules:
  0.0 271.5 jit_solution(16668897708805156756)
XLA Ops:
  0.7 0.6 stack.77.scalar_ref
  1.3 5.7 %cut_columns.1 = (bf16[272,3584]{1,0:T(8,128)(2,1)}, bf16[272,896]{1,0:T(8,128)(2,1)}, bf16[272,1792]{1,0:T(8,128)(2,1)}, bf16[272,1792]{1,0:T(8,128)(2,1)}) custom-call(s32[5]{0:T(128)} %stack.77.scalar_ref, s32[2,256]{1,0:T(2,128)} %bitcast.44, bf16[256,3584]{1,0:T(8,128)(2,1)} %bitcast.33, bf16[256,3584]{1,0:T(8,128)(2,1)} %bitcast.34, ...), custom_call_target="tpu_custom_call" | custom-call | flops 1 | bytes 1 | tf_op jit(solution)/shard_map/cut_columns/pallas_call | solution.py:48
  7.4 2.6 collective-permute-start.1
  10.0 0.7 collective-permute-start.2
  10.8 7.4 %collective-permute-start.3 = (bf16[272,1792]{1,0:T(8,128)(2,1)}, bf16[272,1792]{1,0:T(8,128)(2,1)}, u32[]{:S(2)}, u32[]{:S(2)}) collective-permute-start(bf16[272,1792]{1,0:T(8,128)(2,1)} %get-tuple-element.32), channel_id=1, source_target_pairs={{0,8},{12,4},{1,9},{13,5},{2,10},{14,6},{3,11},{15,7},{16,24},{28,... | collective-permute-start | bytes 2924552 | tf_op jit(solution)/shard_map/ppermute | solution.py:446
  18.2 1.3 collective-permute-start.4
  19.5 0.6 pad_add_fusion.1.scalar_ref
  20.1 13.2 %forward_first.1 = (bf16[320,1024]{1,0:T(8,128)(2,1)}, bf16[320,1024]{1,0:T(8,128)(2,1)}) custom-call(s32[3]{0:T(128)} %pad_add_fusion.1.scalar_ref, bf16[272,3584]{1,0:T(8,128)(2,1)} %get-tuple-element.29.refs_0_.refs_4_, bf16[272,3584]{1,0:T(8,128)(2,1)} %collective-permute-done.refs_1_.refs_5_, bf16[640,1024]{1,0:T(8,128)(2,1)} %bitcast.41, ...), custom_call_target="tpu_custom_call" | custom-call | flops 1 | bytes 1 | tf_op jit(solution)/shard_map/forward_first/pallas_call | solution.py:48
  33.2 15.8 %collective-permute-done.4 = bf16[272,896]{1,0:T(8,128)(2,1)S(1)} collective-permute-done((bf16[272,896]{1,0:T(8,128)(2,1)}, bf16[272,896]{1,0:T(8,128)(2,1)S(1)}, u32[]{:S(2)}, u32[]{:S(2)}) %collective-permute-start.4) | collective-permute-done | bytes 487456 | tf_op jit(solution)/shard_map/ppermute | solution.py:446
  49.0 4.3 %collective-permute-done.1.refs_0_.refs_2_.refs_6_ = bf16[272,3584]{1,0:T(8,128)(2,1)S(1)} collective-permute-done((bf16[272,3584]{1,0:T(8,128)(2,1)}, bf16[272,3584]{1,0:T(8,128)(2,1)S(1)}, u32[]{:S(2)}, u32[]{:S(2)}) %collective-permute-start.1) | collective-permute-done | bytes 1949728 | tf_op jit(solution)/shard_map/ppermute | solution.py:443
  53.4 1.9 fusion.1
  55.5 0.9 fusion
  56.4 1.0 pad_maximum_fusion.1.refs_7_.refs_0_
  57.4 1.7 collective-permute-start.6
  59.1 1.2 copy-done.1
  60.4 0.7 collective-permute-start.7
  61.1 9.2 %collective-permute-start.8 = (bf16[320,1024]{1,0:T(8,128)(2,1)S(1)}, bf16[320,1024]{1,0:T(8,128)(2,1)S(1)}, u32[]{:S(2)}, u32[]{:S(2)}) collective-permute-start(bf16[320,1024]{1,0:T(8,128)(2,1)S(1)} %copy-done.2), channel_id=1, source_target_pairs={{0,8},{12,4},{1,9},{13,5},{2,10},{14,6},{3,11},{15,7},{16,24},{28,... | collective-permute-start | bytes 1966088 | tf_op jit(solution)/shard_map/ppermute | solution.py:446
  70.3 2.4 collective-permute-start.9
  73.2 13.7 %forward_rest.1 = (bf16[320,1024]{1,0:T(8,128)(2,1)}, bf16[640,512]{1,0:T(8,128)(2,1)}, bf16[640,512]{1,0:T(8,128)(2,1)}) custom-call(s32[3]{0:T(128)} %pad_add_fusion.2.scalar_ref, bf16[272,3584]{1,0:T(8,128)(2,1)} %copy-done, bf16[272,3584]{1,0:T(8,128)(2,1)} %copy-done.1, bf16[640,1024]{1,0:T(8,128)(2,1)} %bitcast.42, bf16[3584,1024]{1,0:T(8,128)(2,1)} %bitcast.28, ...), custom_call_target="tpu_custom_call" | custom-call | flops 1 | bytes 1 | tf_op jit(solution)/shard_map/forward_rest/pallas_call | solution.py:48
  86.9 11.6 %collective-permute-done.9.refs_6_ = bf16[320,1024]{1,0:T(8,128)(2,1)} collective-permute-done((bf16[320,1024]{1,0:T(8,128)(2,1)S(1)}, bf16[320,1024]{1,0:T(8,128)(2,1)}, u32[]{:S(2)}, u32[]{:S(2)}) %collective-permute-start.9) | collective-permute-done | bytes 655392 | tf_op jit(solution)/shard_map/ppermute | solution.py:446
  98.6 1.2 pad_maximum_fusion.refs_0_
  99.8 1.5 collective-permute-start.15
  101.6 0.7 collective-permute-start.12
  102.3 7.2 %collective-permute-start.13 = (bf16[320,1024]{1,0:T(8,128)(2,1)S(1)}, bf16[320,1024]{1,0:T(8,128)(2,1)S(1)}, u32[]{:S(2)}, u32[]{:S(2)}) collective-permute-start(bf16[320,1024]{1,0:T(8,128)(2,1)S(1)} %copy-done.3), channel_id=1, source_target_pairs={{0,8},{12,4},{1,9},{13,5},{2,10},{14,6},{3,11},{15,7},{16,24},{28,... | collective-permute-start | bytes 1966088 | tf_op jit(solution)/shard_map/ppermute | solution.py:446
  109.5 1.6 collective-permute-start.14
  111.1 0.7 pad_add_fusion.scalar_ref
  111.7 16.0 %slot_gradients.1 = (bf16[640,2048]{1,0:T(8,128)(2,1)}, bf16[640,1536]{1,0:T(8,128)(2,1)}) custom-call(s32[4]{0:T(128)} %pad_add_fusion.scalar_ref, bf16[320,1024]{1,0:T(8,128)(2,1)} %get-tuple-element.40.refs_6_.refs_0_.refs_3_.refs_4_, bf16[320,1024]{1,0:T(8,128)(2,1)} %get-tuple-element.45.refs_1_.refs_4_.refs_5_, ...), custom_call_target="tpu_custom_call" | custom-call | flops 1 | bytes 1 | tf_op jit(solution)/shard_map/slot_gradients/pallas_call | solution.py:48
  127.7 4.6 %all-to-all-start = ((bf16[4,160,2048]{2,1,0:T(8,128)(2,1)}), bf16[4,160,2048]{2,1,0:T(8,128)(2,1)}, u32[]{:S(2)}, u32[]{:S(2)}) async-start(bf16[4,160,2048]{2,1,0:T(8,128)(2,1)} %bitcast.43), calls=%async_computation | async-start | bytes 5242880 | tf_op jit(solution)/shard_map/all_to_all | solution.py:449
  132.3 0.7 pad_add_fusion.4.scalar_ref
  132.9 0.7 pad_add_fusion.3.scalar_ref
  133.6 5.6 %pick_rows.3.refs_4_.refs_0_ = bf16[1792,640]{1,0:T(8,128)(2,1)} custom-call(s32[3]{0:T(128)} %pad_add_fusion.3.scalar_ref, bf16[272,3584]{1,0:T(8,128)(2,1)} %get-tuple-element.29.refs_0_.refs_4_, bf16[272,3584]{1,0:T(8,128)(2,1)} %collective-permute-done.refs_1_.refs_5_, bf16[272,3584]{1,0:T(8,128)(2,1)} %copy-done, bf16[272,3584]{1,0:T(8,128)(2,1)} %copy-done.1, ...), custom_call_target="tpu_custom_call" | custom-call | flops 1 | bytes 1 | tf_op jit(solution)/shard_map/pick_rows/pallas_call | solution.py:48
  139.2 5.5 %pick_rows.4.refs_1_.refs_2_ = bf16[1792,640]{1,0:T(8,128)(2,1)} custom-call(s32[3]{0:T(128)} %pad_add_fusion.4.scalar_ref, bf16[272,1792]{1,0:T(8,128)(2,1)} %pad_maximum_fusion.1.refs_7_.refs_0_, bf16[272,1792]{1,0:T(8,128)(2,1)} %collective-permute-done.10.refs_1_, bf16[272,1792]{1,0:T(8,128)(2,1)} %collective-permute-done.6.refs_2_, ...), custom_call_target="tpu_custom_call" | custom-call | flops 1 | bytes 1 | tf_op jit(solution)/shard_map/pick_rows/pallas_call | solution.py:48
  145.8 6.2 %for_end.5.refs_9_ = bf16[896,512]{1,0:T(8,128)(2,1)} custom-call(s32[1]{0:T(128)} %constant.31.clone.1.scalar_ref, bf16[1792,640]{1,0:T(8,128)(2,1)} %pick_rows.3.refs_4_.refs_0_, bf16[1792,640]{1,0:T(8,128)(2,1)} %pick_rows.4.refs_1_.refs_2_, bf16[1792,640]{1,0:T(8,128)(2,1)} %pick_rows.4.refs_1_.refs_2_, ...), custom_call_target="tpu_custom_call" | custom-call | flops 1 | bytes 1 | tf_op jit(solution)/shard_map/for_end/pallas_call | solution.py:48
  152.1 1.3 collective-permute-start.23
  153.4 0.7 collective-permute-start.17
  154.1 7.3 %collective-permute-start.18 = (bf16[640,512]{1,0:T(8,128)(2,1)S(1)}, bf16[640,512]{1,0:T(8,128)(2,1)S(1)}, u32[]{:S(2)}, u32[]{:S(2)}) collective-permute-start(bf16[640,512]{1,0:T(8,128)(2,1)S(1)} %copy-done.10), channel_id=1, source_target_pairs={{0,8},{12,4},{1,9},{13,5},{2,10},{14,6},{3,11},{15,7},{16,24},{28,... | collective-permute-start | bytes 1966088 | tf_op jit(solution)/shard_map/ppermute | solution.py:446
  161.4 2.1 collective-permute-start.22
  163.5 0.7 pad_add_fusion.5.scalar_ref
  164.2 6.2 %for_end.6.refs_4_ = bf16[896,512]{1,0:T(8,128)(2,1)} custom-call(s32[1]{0:T(128)} %constant.31.clone.1.scalar_ref, bf16[1792,640]{1,0:T(8,128)(2,1)} %pick_rows.3.refs_4_.refs_0_, bf16[1792,640]{1,0:T(8,128)(2,1)} %pick_rows.4.refs_1_.refs_2_, bf16[1792,640]{1,0:T(8,128)(2,1)} %pick_rows.4.refs_1_.refs_2_, ...), custom_call_target="tpu_custom_call" | custom-call | flops 1 | bytes 1 | tf_op jit(solution)/shard_map/for_end/pallas_call | solution.py:48
  170.4 1.1 copy-done.19
  171.5 7.4 %pick_rows.5.refs_1_.refs_2_.refs_3_ = bf16[2688,640]{1,0:T(8,128)(2,1)} custom-call(s32[4]{0:T(128)} %pad_add_fusion.5.scalar_ref, bf16[272,2688]{1,0:T(8,128)(2,1)} %pad_maximum_fusion.refs_0_, bf16[272,2688]{1,0:T(8,128)(2,1)} %collective-permute-done.16.refs_1_, bf16[272,2688]{1,0:T(8,128)(2,1)} %collective-permute-done.15.refs_2_, ...), custom_call_target="tpu_custom_call" | custom-call | flops 1 | bytes 1 | tf_op jit(solution)/shard_map/pick_rows/pallas_call | solution.py:48
  179.0 10.5 %collective-permute-done.22.refs_5_ = bf16[640,512]{1,0:T(8,128)(2,1)} collective-permute-done((bf16[640,512]{1,0:T(8,128)(2,1)S(1)}, bf16[640,512]{1,0:T(8,128)(2,1)}, u32[]{:S(2)}, u32[]{:S(2)}) %collective-permute-start.22) | collective-permute-done | bytes 655392 | tf_op jit(solution)/shard_map/ppermute | solution.py:446
  189.5 3.7 %all-to-all-start.1 = ((bf16[4,160,1536]{2,1,0:T(8,128)(2,1)}), bf16[4,160,1536]{2,1,0:T(8,128)(2,1)S(1)}, u32[]{:S(2)}, u32[]{:S(2)}) async-start(bf16[4,160,1536]{2,1,0:T(8,128)(2,1)} %bitcast.39), calls=%async_computation.1 | async-start | bytes 3932160 | tf_op jit(solution)/shard_map/all_to_all | solution.py:449
  193.2 1.3 collective-permute-start.20
  194.5 0.7 collective-permute-start.25
  195.2 7.3 %collective-permute-start.26 = (bf16[640,512]{1,0:T(8,128)(2,1)S(1)}, bf16[640,512]{1,0:T(8,128)(2,1)S(1)}, u32[]{:S(2)}, u32[]{:S(2)}) collective-permute-start(bf16[640,512]{1,0:T(8,128)(2,1)S(1)} %copy-done.9), channel_id=1, source_target_pairs={{0,8},{12,4},{1,9},{13,5},{2,10},{14,6},{3,11},{15,7},{16,24},{28,... | collective-permute-start | bytes 1966088 | tf_op jit(solution)/shard_map/ppermute | solution.py:446
  202.6 1.3 collective-permute-start.24
  203.9 5.5 %for_end.4.refs_2_ = bf16[896,512]{1,0:T(8,128)(2,1)} custom-call(s32[1]{0:T(128)} %constant.31.clone.1.scalar_ref, bf16[1792,640]{1,0:T(8,128)(2,1)} %pick_rows.3.refs_4_.refs_0_, bf16[1792,640]{1,0:T(8,128)(2,1)} %pick_rows.4.refs_1_.refs_2_, bf16[1792,640]{1,0:T(8,128)(2,1)} %pick_rows.4.refs_1_.refs_2_, ...), custom_call_target="tpu_custom_call" | custom-call | flops 1 | bytes 1 | tf_op jit(solution)/shard_map/for_end/pallas_call | solution.py:48
  209.4 4.8 %combine.2.refs_14_ = bf16[256,2048]{1,0:T(8,128)(2,1)} custom-call(s32[1]{0:T(128)} %constant.31.clone.1.scalar_ref, s32[2,256]{1,0:T(2,128)} %bitcast.45, bf16[640,2048]{1,0:T(8,128)(2,1)} %bitcast.18.refs_1_, bf16[896,512]{1,0:T(8,128)(2,1)} %for_end.4.refs_2_), custom_call_target="tpu_custom_call" | custom-call | flops 1 | bytes 1 | tf_op jit(solution)/shard_map/combine/pallas_call | solution.py:48
  214.2 4.1 %collective-permute-done.20.refs_13_ = bf16[896,512]{1,0:T(8,128)(2,1)S(1)} collective-permute-done((bf16[896,512]{1,0:T(8,128)(2,1)}, bf16[896,512]{1,0:T(8,128)(2,1)S(1)}, u32[]{:S(2)}, u32[]{:S(2)}) %collective-permute-start.20) | collective-permute-done | bytes 917536 | tf_op jit(solution)/shard_map/ppermute | solution.py:458
  218.3 1.5 collective-permute-start.21
  219.8 1.3 collective-permute-start.27
  221.1 12.8 %for_own.3.refs_9_ = bf16[896,1024]{1,0:T(8,128)(2,1)} custom-call(s32[1]{0:T(128)} %constant.31.clone.1.scalar_ref, bf16[1792,640]{1,0:T(8,128)(2,1)} %pick_rows.3.refs_4_.refs_0_, bf16[2688,640]{1,0:T(8,128)(2,1)} %pick_rows.5.refs_1_.refs_2_.refs_3_, bf16[2688,640]{1,0:T(8,128)(2,1)} %pick_rows.5.refs_1_.refs_2_.refs_3_, ...), custom_call_target="tpu_custom_call" | custom-call | flops 1 | bytes 1 | tf_op jit(solution)/shard_map/for_own/pallas_call | solution.py:48
  233.9 0.8 copy-done.12
  234.9 0.8 copy-done.17
  235.8 5.4 %for_end.7.refs_2_ = bf16[896,512]{1,0:T(8,128)(2,1)} custom-call(s32[1]{0:T(128)} %constant.31.clone.1.scalar_ref, bf16[1792,640]{1,0:T(8,128)(2,1)} %pick_rows.3.refs_4_.refs_0_, bf16[1792,640]{1,0:T(8,128)(2,1)} %pick_rows.4.refs_1_.refs_2_, bf16[1792,640]{1,0:T(8,128)(2,1)} %pick_rows.4.refs_1_.refs_2_, ...), custom_call_target="tpu_custom_call" | custom-call | flops 1 | bytes 1 | tf_op jit(solution)/shard_map/for_end/pallas_call | solution.py:48
  241.2 1.3 collective-permute-start.29
  242.5 1.3 copy-done.5
  243.8 4.0 %combine.3.refs_9_ = bf16[256,1536]{1,0:T(8,128)(2,1)} custom-call(s32[1]{0:T(128)} %constant.31.clone.1.scalar_ref, s32[2,256]{1,0:T(2,128)} %bitcast.46, bf16[640,1536]{1,0:T(8,128)(2,1)} %bitcast.38, bf16[896,512]{1,0:T(8,128)(2,1)} %for_end.7.refs_2_), custom_call_target="tpu_custom_call" | custom-call | flops 1 | bytes 1 | tf_op jit(solution)/shard_map/combine/pallas_call | solution.py:48
  248.4 6.9 %for_own.4.refs_8_.refs_2_ = bf16[896,1024]{1,0:T(8,128)(2,1)} custom-call(s32[1]{0:T(128)} %constant.31.clone.1.scalar_ref, bf16[1792,640]{1,0:T(8,128)(2,1)} %pick_rows.3.refs_4_.refs_0_, bf16[2688,640]{1,0:T(8,128)(2,1)} %pick_rows.5.refs_1_.refs_2_.refs_3_, bf16[2688,640]{1,0:T(8,128)(2,1)} %pick_rows.5.refs_1_.refs_2_.refs_3_, ...), custom_call_target="tpu_custom_call" | custom-call | flops 1 | bytes 1 | tf_op jit(solution)/shard_map/for_own/pallas_call | solution.py:48
  255.2 6.7 %for_own.5.refs_0_ = f32[896,512]{1,0:T(8,128)} custom-call(s32[1]{0:T(128)} %constant.31.clone.1.scalar_ref, bf16[1792,640]{1,0:T(8,128)(2,1)} %pick_rows.3.refs_4_.refs_0_, bf16[2688,640]{1,0:T(8,128)(2,1)} %pick_rows.5.refs_1_.refs_2_.refs_3_, bf16[2688,640]{1,0:T(8,128)(2,1)} %pick_rows.5.refs_1_.refs_2_.refs_3_, ...), custom_call_target="tpu_custom_call" | custom-call | flops 1 | bytes 1 | tf_op jit(solution)/shard_map/for_own/pallas_call | solution.py:48
  261.9 4.2 %collective-permute-done.29.refs_1_ = bf16[896,512]{1,0:T(8,128)(2,1)} collective-permute-done((bf16[896,512]{1,0:T(8,128)(2,1)}, bf16[896,512]{1,0:T(8,128)(2,1)}, u32[]{:S(2)}, u32[]{:S(2)}) %collective-permute-start.29) | collective-permute-done | bytes 917536 | tf_op jit(solution)/shard_map/ppermute | solution.py:458
  266.1 2.8 %finish.1 = bf16[896,1024]{1,0:T(8,128)(2,1)} custom-call(s32[1]{0:T(128)} %constant.31.clone.1.scalar_ref, f32[896,512]{1,0:T(8,128)} %for_own.5.refs_0_, bf16[896,512]{1,0:T(8,128)(2,1)} %collective-permute-done.29.refs_1_, bf16[896,1024]{1,0:T(8,128)(2,1)} %for_own.4.refs_8_.refs_2_), custom_call_target="tpu_custom_call", output_to_operand_aliasing={{}: (3, {})} | custom-call | flops 1 | bytes 1 | tf_op jit(solution)/shard_map/finish/pallas_call | solution.py:48
  268.9 2.6 maximum_bitcast_fusion
  (83 shorter events, 3.5 us)
Async XLA Ops:
  7.0 13.1 %collective-permute-start = (bf16[272,3584]{1,0:T(8,128)(2,1)}, bf16[272,3584]{1,0:T(8,128)(2,1)}, u32[]{:S(2)}, u32[]{:S(2)}) collective-permute-start(bf16[272,3584]{1,0:T(8,128)(2,1)} %get-tuple-element.29.refs_0_.refs_4_), channel_id=1, source_target_pairs={{0,1},{1,0},{2,3},{3,2},{4,5},{5,4},{6,7},{7,6},{8,9},{9,8},{10,11... | collective-permute-start | bytes 5849096 | tf_op jit(solution)/shard_map/ppermute | solution.py:440
  7.4 45.9 %collective-permute-start.1 = (bf16[272,3584]{1,0:T(8,128)(2,1)}, bf16[272,3584]{1,0:T(8,128)(2,1)S(1)}, u32[]{:S(2)}, u32[]{:S(2)}) collective-permute-start(bf16[272,3584]{1,0:T(8,128)(2,1)} %get-tuple-element.29.refs_0_.refs_4_), channel_id=1, source_target_pairs={{0,2},{1,3},{2,0},{3,1},{4,6},{5,7},{6,4},{7,5},{8,10},{9,11},{10,... | collective-permute-start | bytes 5849096 | tf_op jit(solution)/shard_map/ppermute | solution.py:443
  10.0 39.0 %collective-permute-start.2 = (bf16[272,1792]{1,0:T(8,128)(2,1)}, bf16[272,1792]{1,0:T(8,128)(2,1)S(1)}, u32[]{:S(2)}, u32[]{:S(2)}) collective-permute-start(bf16[272,1792]{1,0:T(8,128)(2,1)} %get-tuple-element.31), channel_id=1, source_target_pairs={{4,8},{8,4},{5,9},{9,5},{6,10},{10,6},{7,11},{11,7},{20,24},{24,20... | collective-permute-start | bytes 2924552 | tf_op jit(solution)/shard_map/ppermute | solution.py:446
  10.8 38.3 %collective-permute-start.3 = (bf16[272,1792]{1,0:T(8,128)(2,1)}, bf16[272,1792]{1,0:T(8,128)(2,1)}, u32[]{:S(2)}, u32[]{:S(2)}) collective-permute-start(bf16[272,1792]{1,0:T(8,128)(2,1)} %get-tuple-element.32), channel_id=1, source_target_pairs={{0,8},{12,4},{1,9},{13,5},{2,10},{14,6},{3,11},{15,7},{16,24},{28,... | collective-permute-start | bytes 2924552 | tf_op jit(solution)/shard_map/ppermute | solution.py:446
  18.2 30.8 %collective-permute-start.4 = (bf16[272,896]{1,0:T(8,128)(2,1)}, bf16[272,896]{1,0:T(8,128)(2,1)S(1)}, u32[]{:S(2)}, u32[]{:S(2)}) collective-permute-start(bf16[272,896]{1,0:T(8,128)(2,1)} %get-tuple-element.33), channel_id=1, source_target_pairs={{0,4},{12,8},{1,5},{13,9},{2,6},{14,10},{3,7},{15,11},{16,20},{28,... | collective-permute-start | bytes 1462280 | tf_op jit(solution)/shard_map/ppermute | solution.py:446
  49.0 4.3 %copy-start.25 = (bf16[272,896]{1,0:T(8,128)(2,1)}, bf16[272,896]{1,0:T(8,128)(2,1)S(1)}, u32[]{:S(2)}) copy-start(bf16[272,896]{1,0:T(8,128)(2,1)S(1)} %collective-permute-done.4) | copy-start | bytes 1462276
  49.0 4.3 %copy-start.20 = (bf16[272,1792]{1,0:T(8,128)(2,1)}, bf16[272,1792]{1,0:T(8,128)(2,1)S(1)}, u32[]{:S(2)}) copy-start(bf16[272,1792]{1,0:T(8,128)(2,1)S(1)} %collective-permute-done.2) | copy-start | bytes 2924548
  53.3 3.1 %copy-start = (bf16[272,3584]{1,0:T(8,128)(2,1)}, bf16[272,3584]{1,0:T(8,128)(2,1)S(1)}, u32[]{:S(2)}) copy-start(bf16[272,3584]{1,0:T(8,128)(2,1)S(1)} %collective-permute-done.1.refs_0_.refs_2_.refs_6_) | copy-start | bytes 5849092
  53.3 5.8 %collective-permute-start.5 = (bf16[272,3584]{1,0:T(8,128)(2,1)S(1)}, bf16[272,3584]{1,0:T(8,128)(2,1)S(1)}, u32[]{:S(2)}, u32[]{:S(2)}) collective-permute-start(bf16[272,3584]{1,0:T(8,128)(2,1)S(1)} %collective-permute-done.1.refs_0_.refs_2_.refs_6_), channel_id=1, source_target_pairs={{0,1},{1,0},{2,3},{3,2},{4,5},{5,4},{6,7},{7,6},{8,9},{9,8},{10,11... | collective-permute-start | bytes 5849096 | tf_op jit(solution)/shard_map/ppermute | solution.py:440
  53.4 2.1 copy-start.21
  55.5 4.9 %copy-start.2 = (bf16[320,1024]{1,0:T(8,128)(2,1)S(1)}, bf16[320,1024]{1,0:T(8,128)(2,1)}, u32[]{:S(2)}) copy-start(bf16[320,1024]{1,0:T(8,128)(2,1)} %get-tuple-element.40.refs_6_.refs_0_.refs_3_.refs_4_) | copy-start | bytes 1966084
  57.4 41.2 %collective-permute-start.6 = (bf16[272,1792]{1,0:T(8,128)(2,1)}, bf16[272,1792]{1,0:T(8,128)(2,1)}, u32[]{:S(2)}, u32[]{:S(2)}) collective-permute-start(bf16[272,1792]{1,0:T(8,128)(2,1)} %pad_maximum_fusion.1.refs_7_.refs_0_), channel_id=1, source_target_pairs={{0,2},{1,3},{2,0},{3,1},{4,6},{5,7},{6,4},{7,5},{8,10},{9,11},{10,... | collective-permute-start | bytes 2924552 | tf_op jit(solution)/shard_map/ppermute | solution.py:443
  59.1 1.2 copy-start.1
  60.4 38.2 %collective-permute-start.10 = (bf16[272,1792]{1,0:T(8,128)(2,1)}, bf16[272,1792]{1,0:T(8,128)(2,1)}, u32[]{:S(2)}, u32[]{:S(2)}) collective-permute-start(bf16[272,1792]{1,0:T(8,128)(2,1)} %pad_maximum_fusion.1.refs_7_.refs_0_), channel_id=1, source_target_pairs={{0,1},{1,0},{2,3},{3,2},{4,5},{5,4},{6,7},{7,6},{8,9},{9,8},{10,11... | collective-permute-start | bytes 2924552 | tf_op jit(solution)/shard_map/ppermute | solution.py:440
  60.4 26.5 %collective-permute-start.7 = (bf16[320,1024]{1,0:T(8,128)(2,1)S(1)}, bf16[320,1024]{1,0:T(8,128)(2,1)S(1)}, u32[]{:S(2)}, u32[]{:S(2)}) collective-permute-start(bf16[320,1024]{1,0:T(8,128)(2,1)S(1)} %copy-done.2), channel_id=1, source_target_pairs={{4,8},{8,4},{5,9},{9,5},{6,10},{10,6},{7,11},{11,7},{20,24},{24,20... | collective-permute-start | bytes 1966088 | tf_op jit(solution)/shard_map/ppermute | solution.py:446
  61.1 25.8 %collective-permute-start.8 = (bf16[320,1024]{1,0:T(8,128)(2,1)S(1)}, bf16[320,1024]{1,0:T(8,128)(2,1)S(1)}, u32[]{:S(2)}, u32[]{:S(2)}) collective-permute-start(bf16[320,1024]{1,0:T(8,128)(2,1)S(1)} %copy-done.2), channel_id=1, source_target_pairs={{0,8},{12,4},{1,9},{13,5},{2,10},{14,6},{3,11},{15,7},{16,24},{28,... | collective-permute-start | bytes 1966088 | tf_op jit(solution)/shard_map/ppermute | solution.py:446
  70.3 28.3 %collective-permute-start.9 = (bf16[320,1024]{1,0:T(8,128)(2,1)S(1)}, bf16[320,1024]{1,0:T(8,128)(2,1)}, u32[]{:S(2)}, u32[]{:S(2)}) collective-permute-start(bf16[320,1024]{1,0:T(8,128)(2,1)S(1)} %copy-done.2), channel_id=1, source_target_pairs={{0,4},{12,8},{1,5},{13,9},{2,6},{14,10},{3,7},{15,11},{16,20},{28,... | collective-permute-start | bytes 1966088 | tf_op jit(solution)/shard_map/ppermute | solution.py:446
  73.2 25.4 %copy-start.18 = (bf16[272,896]{1,0:T(8,128)(2,1)S(1)}, bf16[272,896]{1,0:T(8,128)(2,1)}, u32[]{:S(2)}) copy-start(bf16[272,896]{1,0:T(8,128)(2,1)} %get-tuple-element.55) | copy-start | bytes 1462276
  73.2 25.4 %copy-start.26 = (bf16[272,896]{1,0:T(8,128)(2,1)S(1)}, bf16[272,896]{1,0:T(8,128)(2,1)}, u32[]{:S(2)}) copy-start(bf16[272,896]{1,0:T(8,128)(2,1)} %copy-done.25) | copy-start | bytes 1462276
  86.9 14.7 %copy-start.3 = (bf16[320,1024]{1,0:T(8,128)(2,1)S(1)}, bf16[320,1024]{1,0:T(8,128)(2,1)}, u32[]{:S(2)}) copy-start(bf16[320,1024]{1,0:T(8,128)(2,1)} %get-tuple-element.45.refs_1_.refs_4_.refs_5_) | copy-start | bytes 1966084
  86.9 40.8 %copy-start.6 = (bf16[320,1024]{1,0:T(8,128)(2,1)}, bf16[320,1024]{1,0:T(8,128)(2,1)S(1)}, u32[]{:S(2)}) copy-start(bf16[320,1024]{1,0:T(8,128)(2,1)S(1)} %collective-permute-done.7.refs_5_.refs_8_) | copy-start | bytes 1966084
  86.9 14.4 %copy-start.7 = (bf16[320,1024]{1,0:T(8,128)(2,1)}, bf16[320,1024]{1,0:T(8,128)(2,1)S(1)}, u32[]{:S(2)}) copy-start(bf16[320,1024]{1,0:T(8,128)(2,1)S(1)} %collective-permute-done.8.refs_7_.refs_10_) | copy-start | bytes 1966084
  98.6 2.8 %collective-permute-start.11 = (bf16[272,1792]{1,0:T(8,128)(2,1)}, bf16[272,1792]{1,0:T(8,128)(2,1)S(1)}, u32[]{:S(2)}, u32[]{:S(2)}) collective-permute-start(bf16[272,1792]{1,0:T(8,128)(2,1)} %collective-permute-done.6.refs_2_), channel_id=1, source_target_pairs={{0,1},{1,0},{2,3},{3,2},{4,5},{5,4},{6,7},{7,6},{8,9},{9,8},{10,11... | collective-permute-start | bytes 2924552 | tf_op jit(solution)/shard_map/ppermute | solution.py:440
  99.8 45.0 %collective-permute-start.15 = (bf16[272,2688]{1,0:T(8,128)(2,1)}, bf16[272,2688]{1,0:T(8,128)(2,1)}, u32[]{:S(2)}, u32[]{:S(2)}) collective-permute-start(bf16[272,2688]{1,0:T(8,128)(2,1)} %pad_maximum_fusion.refs_0_), channel_id=1, source_target_pairs={{0,2},{1,3},{2,0},{3,1},{4,6},{5,7},{6,4},{7,5},{8,10},{9,11},{10,... | collective-permute-start | bytes 4386824 | tf_op jit(solution)/shard_map/ppermute | solution.py:443
  101.3 10.4 %copy-start.14 = (bf16[272,1792]{1,0:T(8,128)(2,1)}, bf16[272,1792]{1,0:T(8,128)(2,1)S(1)}, u32[]{:S(2)}) copy-start(bf16[272,1792]{1,0:T(8,128)(2,1)S(1)} %collective-permute-done.11.refs_6_.refs_3_) | copy-start | bytes 2924548
  101.3 43.5 %collective-permute-start.16 = (bf16[272,2688]{1,0:T(8,128)(2,1)}, bf16[272,2688]{1,0:T(8,128)(2,1)}, u32[]{:S(2)}, u32[]{:S(2)}) collective-permute-start(bf16[272,2688]{1,0:T(8,128)(2,1)} %pad_maximum_fusion.refs_0_), channel_id=1, source_target_pairs={{0,1},{1,0},{2,3},{3,2},{4,5},{5,4},{6,7},{7,6},{8,9},{9,8},{10,11... | collective-permute-start | bytes 4386824 | tf_op jit(solution)/shard_map/ppermute | solution.py:440
  101.6 43.2 %collective-permute-start.12 = (bf16[320,1024]{1,0:T(8,128)(2,1)S(1)}, bf16[320,1024]{1,0:T(8,128)(2,1)S(1)}, u32[]{:S(2)}, u32[]{:S(2)}) collective-permute-start(bf16[320,1024]{1,0:T(8,128)(2,1)S(1)} %copy-done.3), channel_id=1, source_target_pairs={{4,8},{8,4},{5,9},{9,5},{6,10},{10,6},{7,11},{11,7},{20,24},{24,20... | collective-permute-start | bytes 1966088 | tf_op jit(solution)/shard_map/ppermute | solution.py:446
  102.3 42.5 %collective-permute-start.13 = (bf16[320,1024]{1,0:T(8,128)(2,1)S(1)}, bf16[320,1024]{1,0:T(8,128)(2,1)S(1)}, u32[]{:S(2)}, u32[]{:S(2)}) collective-permute-start(bf16[320,1024]{1,0:T(8,128)(2,1)S(1)} %copy-done.3), channel_id=1, source_target_pairs={{0,8},{12,4},{1,9},{13,5},{2,10},{14,6},{3,11},{15,7},{16,24},{28,... | collective-permute-start | bytes 1966088 | tf_op jit(solution)/shard_map/ppermute | solution.py:446
  109.5 35.3 %collective-permute-start.14 = (bf16[320,1024]{1,0:T(8,128)(2,1)S(1)}, bf16[320,1024]{1,0:T(8,128)(2,1)S(1)}, u32[]{:S(2)}, u32[]{:S(2)}) collective-permute-start(bf16[320,1024]{1,0:T(8,128)(2,1)S(1)} %copy-done.3), channel_id=1, source_target_pairs={{0,4},{12,8},{1,5},{13,9},{2,6},{14,10},{3,7},{15,11},{16,20},{28,... | collective-permute-start | bytes 1966088 | tf_op jit(solution)/shard_map/ppermute | solution.py:446
  127.7 51.2 %all-to-all-start = ((bf16[4,160,2048]{2,1,0:T(8,128)(2,1)}), bf16[4,160,2048]{2,1,0:T(8,128)(2,1)}, u32[]{:S(2)}, u32[]{:S(2)}) async-start(bf16[4,160,2048]{2,1,0:T(8,128)(2,1)} %bitcast.43), calls=%async_computation | async-start | bytes 5242880 | tf_op jit(solution)/shard_map/all_to_all | solution.py:449
  144.7 8.6 %copy-start.10 = (bf16[640,512]{1,0:T(8,128)(2,1)S(1)}, bf16[640,512]{1,0:T(8,128)(2,1)}, u32[]{:S(2)}) copy-start(bf16[640,512]{1,0:T(8,128)(2,1)} %get-tuple-element.48.refs_2_.refs_3_.refs_4_) | copy-start | bytes 1966084
  144.8 0.9 copy-start.4
  144.8 1.1 copy-start.8
  144.8 7.3 %copy-start.24 = (bf16[320,1024]{1,0:T(8,128)(2,1)}, bf16[320,1024]{1,0:T(8,128)(2,1)S(1)}, u32[]{:S(2)}) copy-start(bf16[320,1024]{1,0:T(8,128)(2,1)S(1)} %collective-permute-done.14.refs_7_) | copy-start | bytes 1966084
  144.8 25.6 %collective-permute-start.19 = (bf16[272,2688]{1,0:T(8,128)(2,1)}, bf16[272,2688]{1,0:T(8,128)(2,1)S(1)}, u32[]{:S(2)}, u32[]{:S(2)}) collective-permute-start(bf16[272,2688]{1,0:T(8,128)(2,1)} %collective-permute-done.15.refs_2_), channel_id=1, source_target_pairs={{0,1},{1,0},{2,3},{3,2},{4,5},{5,4},{6,7},{7,6},{8,9},{9,8},{10,11... | collective-permute-start | bytes 4386824 | tf_op jit(solution)/shard_map/ppermute | solution.py:440
  152.1 26.9 %collective-permute-start.23 = (bf16[896,512]{1,0:T(8,128)(2,1)}, bf16[896,512]{1,0:T(8,128)(2,1)S(1)}, u32[]{:S(2)}, u32[]{:S(2)}) collective-permute-start(bf16[896,512]{1,0:T(8,128)(2,1)} %for_end.5.refs_9_), channel_id=1, source_target_pairs={{4,0},{8,12},{5,1},{9,13},{6,2},{10,14},{7,3},{11,15},{20,16},{24,... | collective-permute-start | bytes 2752520 | tf_op jit(solution)/shard_map/ppermute | solution.py:458
  153.4 25.6 %collective-permute-start.17 = (bf16[640,512]{1,0:T(8,128)(2,1)S(1)}, bf16[640,512]{1,0:T(8,128)(2,1)S(1)}, u32[]{:S(2)}, u32[]{:S(2)}) collective-permute-start(bf16[640,512]{1,0:T(8,128)(2,1)S(1)} %copy-done.10), channel_id=1, source_target_pairs={{4,8},{8,4},{5,9},{9,5},{6,10},{10,6},{7,11},{11,7},{20,24},{24,20... | collective-permute-start | bytes 1966088 | tf_op jit(solution)/shard_map/ppermute | solution.py:446
  154.1 24.9 %collective-permute-start.18 = (bf16[640,512]{1,0:T(8,128)(2,1)S(1)}, bf16[640,512]{1,0:T(8,128)(2,1)S(1)}, u32[]{:S(2)}, u32[]{:S(2)}) collective-permute-start(bf16[640,512]{1,0:T(8,128)(2,1)S(1)} %copy-done.10), channel_id=1, source_target_pairs={{0,8},{12,4},{1,9},{13,5},{2,10},{14,6},{3,11},{15,7},{16,24},{28,... | collective-permute-start | bytes 1966088 | tf_op jit(solution)/shard_map/ppermute | solution.py:446
  161.4 28.1 %collective-permute-start.22 = (bf16[640,512]{1,0:T(8,128)(2,1)S(1)}, bf16[640,512]{1,0:T(8,128)(2,1)}, u32[]{:S(2)}, u32[]{:S(2)}) collective-permute-start(bf16[640,512]{1,0:T(8,128)(2,1)S(1)} %copy-done.10), channel_id=1, source_target_pairs={{0,4},{12,8},{1,5},{13,9},{2,6},{14,10},{3,7},{15,11},{16,20},{28,... | collective-permute-start | bytes 1966088 | tf_op jit(solution)/shard_map/ppermute | solution.py:446
  170.4 1.1 copy-start.19
  179.0 10.5 %copy-start.22 = (bf16[896,512]{1,0:T(8,128)(2,1)}, bf16[896,512]{1,0:T(8,128)(2,1)S(1)}, u32[]{:S(2)}) copy-start(bf16[896,512]{1,0:T(8,128)(2,1)S(1)} %collective-permute-done.23.refs_12_) | copy-start | bytes 2752516
  179.0 10.5 %copy-start.11 = (bf16[640,512]{1,0:T(8,128)(2,1)}, bf16[640,512]{1,0:T(8,128)(2,1)S(1)}, u32[]{:S(2)}) copy-start(bf16[640,512]{1,0:T(8,128)(2,1)S(1)} %collective-permute-done.17.refs_4_.refs_6_) | copy-start | bytes 1966084
  179.0 10.5 %copy-start.16 = (bf16[640,512]{1,0:T(8,128)(2,1)}, bf16[640,512]{1,0:T(8,128)(2,1)S(1)}, u32[]{:S(2)}) copy-start(bf16[640,512]{1,0:T(8,128)(2,1)S(1)} %collective-permute-done.18.refs_5_.refs_7_) | copy-start | bytes 1966084
  189.5 5.1 %copy-start.9 = (bf16[640,512]{1,0:T(8,128)(2,1)S(1)}, bf16[640,512]{1,0:T(8,128)(2,1)}, u32[]{:S(2)}) copy-start(bf16[640,512]{1,0:T(8,128)(2,1)} %get-tuple-element.52.refs_3_.refs_4_) | copy-start | bytes 1966084
  189.5 53.0 %all-to-all-start.1 = ((bf16[4,160,1536]{2,1,0:T(8,128)(2,1)}), bf16[4,160,1536]{2,1,0:T(8,128)(2,1)S(1)}, u32[]{:S(2)}, u32[]{:S(2)}) async-start(bf16[4,160,1536]{2,1,0:T(8,128)(2,1)} %bitcast.39), calls=%async_computation.1 | async-start | bytes 3932160 | tf_op jit(solution)/shard_map/all_to_all | solution.py:449
  193.2 25.0 %collective-permute-start.20 = (bf16[896,512]{1,0:T(8,128)(2,1)}, bf16[896,512]{1,0:T(8,128)(2,1)S(1)}, u32[]{:S(2)}, u32[]{:S(2)}) collective-permute-start(bf16[896,512]{1,0:T(8,128)(2,1)} %for_end.6.refs_4_), channel_id=1, source_target_pairs={{4,0},{8,12},{5,1},{9,13},{6,2},{10,14},{7,3},{11,15},{20,16},{24,... | collective-permute-start | bytes 2752520 | tf_op jit(solution)/shard_map/ppermute | solution.py:458
  194.5 39.3 %collective-permute-start.25 = (bf16[640,512]{1,0:T(8,128)(2,1)S(1)}, bf16[640,512]{1,0:T(8,128)(2,1)S(1)}, u32[]{:S(2)}, u32[]{:S(2)}) collective-permute-start(bf16[640,512]{1,0:T(8,128)(2,1)S(1)} %copy-done.9), channel_id=1, source_target_pairs={{4,8},{8,4},{5,9},{9,5},{6,10},{10,6},{7,11},{11,7},{20,24},{24,20... | collective-permute-start | bytes 1966088 | tf_op jit(solution)/shard_map/ppermute | solution.py:446
  195.2 38.6 %collective-permute-start.26 = (bf16[640,512]{1,0:T(8,128)(2,1)S(1)}, bf16[640,512]{1,0:T(8,128)(2,1)S(1)}, u32[]{:S(2)}, u32[]{:S(2)}) collective-permute-start(bf16[640,512]{1,0:T(8,128)(2,1)S(1)} %copy-done.9), channel_id=1, source_target_pairs={{0,8},{12,4},{1,9},{13,5},{2,10},{14,6},{3,11},{15,7},{16,24},{28,... | collective-permute-start | bytes 1966088 | tf_op jit(solution)/shard_map/ppermute | solution.py:446
  202.6 31.3 %collective-permute-start.24 = (bf16[640,512]{1,0:T(8,128)(2,1)S(1)}, bf16[640,512]{1,0:T(8,128)(2,1)S(1)}, u32[]{:S(2)}, u32[]{:S(2)}) collective-permute-start(bf16[640,512]{1,0:T(8,128)(2,1)S(1)} %copy-done.9), channel_id=1, source_target_pairs={{0,4},{12,8},{1,5},{13,9},{2,6},{14,10},{3,7},{15,11},{16,20},{28,... | collective-permute-start | bytes 1966088 | tf_op jit(solution)/shard_map/ppermute | solution.py:446
  209.4 10.4 %copy-start.15 = (bf16[896,512]{1,0:T(8,128)(2,1)S(1)}, bf16[896,512]{1,0:T(8,128)(2,1)}, u32[]{:S(2)}) copy-start(bf16[896,512]{1,0:T(8,128)(2,1)} %for_end.4.refs_2_) | copy-start | bytes 2752516
  218.3 2.8 %copy-start.23 = (bf16[896,512]{1,0:T(8,128)(2,1)}, bf16[896,512]{1,0:T(8,128)(2,1)S(1)}, u32[]{:S(2)}) copy-start(bf16[896,512]{1,0:T(8,128)(2,1)S(1)} %collective-permute-done.20.refs_13_) | copy-start | bytes 2752516
  218.3 50.7 %collective-permute-start.21 = (bf16[256,2048]{1,0:T(8,128)(2,1)}, bf16[256,2048]{1,0:T(8,128)(2,1)}, u32[]{:S(2)}, u32[]{:S(2)}) collective-permute-start(bf16[256,2048]{1,0:T(8,128)(2,1)} %combine.2.refs_14_), channel_id=1, source_target_pairs={{0,16},{16,0},{1,17},{17,1},{2,18},{18,2},{3,19},{19,3},{4,20},{20... | collective-permute-start | bytes 3145736 | tf_op jit(solution)/shard_map/ppermute | solution.py:455
  219.8 28.6 %collective-permute-start.27 = (bf16[896,512]{1,0:T(8,128)(2,1)S(1)}, bf16[896,512]{1,0:T(8,128)(2,1)}, u32[]{:S(2)}, u32[]{:S(2)}) collective-permute-start(bf16[896,512]{1,0:T(8,128)(2,1)S(1)} %copy-done.15), channel_id=1, source_target_pairs={{4,0},{8,12},{5,1},{9,13},{6,2},{10,14},{7,3},{11,15},{20,16},{24,... | collective-permute-start | bytes 2752520 | tf_op jit(solution)/shard_map/ppermute | solution.py:458
  233.9 0.8 copy-start.12
  233.9 1.0 copy-start.13
  234.9 0.8 copy-start.17
  241.2 24.9 %collective-permute-start.29 = (bf16[896,512]{1,0:T(8,128)(2,1)}, bf16[896,512]{1,0:T(8,128)(2,1)}, u32[]{:S(2)}, u32[]{:S(2)}) collective-permute-start(bf16[896,512]{1,0:T(8,128)(2,1)} %for_end.7.refs_2_), channel_id=1, source_target_pairs={{4,0},{8,12},{5,1},{9,13},{6,2},{10,14},{7,3},{11,15},{20,16},{24,... | collective-permute-start | bytes 2752520 | tf_op jit(solution)/shard_map/ppermute | solution.py:458
  242.5 1.3 copy-start.5
  247.8 21.1 %collective-permute-start.28 = (bf16[256,1536]{1,0:T(8,128)(2,1)}, bf16[256,1536]{1,0:T(8,128)(2,1)S(1)}, u32[]{:S(2)}, u32[]{:S(2)}) collective-permute-start(bf16[256,1536]{1,0:T(8,128)(2,1)} %combine.3.refs_9_), channel_id=1, source_target_pairs={{0,16},{16,0},{1,17},{17,1},{2,18},{18,2},{3,19},{19,3},{4,20},{20... | collective-permute-start | bytes 2359304 | tf_op jit(solution)/shard_map/ppermute | solution.py:455

commit v2 on v1

--- a/solution.py
+++ b/solution.py
@@ -7,7 +7,7 @@
 
 BF16 = jnp.bfloat16
 F32 = jnp.float32
-VMEM_LIMIT = 56 * 1024 * 1024
+MIB = 1024 * 1024
 
 
 def dot(a, b, contract=((1,), (0,))):
@@ -39,7 +39,7 @@
     return found
 
 
-def call(body, name, scalars, ins, in_specs, outs, out_specs, grid, scratch=(), after=(), aliases=None):
+def call(body, name, scalars, ins, in_specs, outs, out_specs, grid, scratch=(), after=(), aliases=None, vmem=28):
     count, skip = len(ins), len(after)
 
     def kernel(scalar_ref, *refs):
@@ -58,7 +58,7 @@
         ),
         input_output_aliases=aliases or {},
         compiler_params=pltpu.CompilerParams(
-            dimension_semantics=("arbitrary",) * len(grid), vmem_limit_bytes=VMEM_LIMIT
+            dimension_semantics=("arbitrary",) * len(grid), vmem_limit_bytes=vmem * MIB
         ),
         cost_estimate=pl.CostEstimate(flops=1, bytes_accessed=1, transcendentals=0),
     )(jnp.stack(scalars).astype(jnp.int32), *ins, *after)
@@ -220,6 +220,7 @@
         (hidden // step,),
         scratch=[pltpu.VMEM((count, width), BF16)],
         after=after,
+        vmem=56,
     )
 
 
@@ -229,29 +230,36 @@
     return step, steps, (steps + 1) // 2
 
 
-def slot_gradients(places, gate_parts, up_parts, gate_w, up_w, after=()):
+def slot_gradients(places, gate, ups, gate_w, up_w, near=None, after=()):
     width, hidden = gate_w.shape
-    slots = up_parts[0].shape[0]
-    capacity = slots // len(places)
-    gates = len(gate_parts)
+    count = gate.shape[0]
+    skip = 0 if near is None else near.shape[0]
+    slots = skip + count
+    capacity = slots // len(places) if skip else count // 2
     step, steps, lead = halves_of(width)
 
     def body(s, ins, outs):
         j = pl.program_id(0)
-        wg, wu = ins[-2], ins[-1]
+        wg, wu = ins[0], ins[1]
         across = ((1,), (1,))
-        total = jnp.concatenate([dot(g[...], wg[...], across) for g in ins[:gates]], axis=0)
+        total = dot(ins[2][...], wg[...], across)
         at = 0
-        for g in ins[gates:-2]:
+        for g in ins[3 : 3 + len(ups)]:
             size = g.shape[1]
-            total = total + dot(g[...], wu[:, at : at + size], across)
+            total = total + dot(g[skip:], wu[:, at : at + size], across)
             at += size
         total = total.astype(BF16)
+        if near is None:
+            outs[0][...] = total
+            return
 
         def put(out):
             for r in range(len(places)):
                 at = pl.ds(pl.multiple_of(s[r] * capacity, 16), capacity)
-                out[at, :] = total[r * capacity : (r + 1) * capacity]
+                if r < 2:
+                    out[at, :] = ins[-1][r * capacity : (r + 1) * capacity]
+                else:
+                    out[at, :] = total[(r - 2) * capacity : (r - 1) * capacity]
 
         @pl.when(j < lead)
         def _():
@@ -261,21 +269,32 @@
         def _():
             put(outs[1])
 
-    return call(
-        body,
-        "slot_gradients",
-        places,
-        list(gate_parts) + list(up_parts) + [gate_w, up_w],
-        [whole(g.shape) for g in list(gate_parts) + list(up_parts)]
-        + [pl.BlockSpec((step, hidden), lambda j, s: (j, 0))] * 2,
-        [((slots, lead * step), BF16), ((slots, width - lead * step), BF16)],
-        [
+    ins = [gate_w, up_w, gate] + list(ups)
+    specs = [pl.BlockSpec((step, hidden), lambda j, s: (j, 0))] * 2 + [whole(g.shape) for g in ins[2:]]
+    if near is None:
+        outs = [((slots, width), BF16)]
+        out_specs = [pl.BlockSpec((slots, step), lambda j, s: (0, j))]
+    else:
+        ins.append(near)
+        specs.append(pl.BlockSpec((skip, step), lambda j, s: (0, j)))
+        outs = [((slots, lead * step), BF16), ((slots, width - lead * step), BF16)]
+        out_specs = [
             pl.BlockSpec((slots, step), lambda j, s: (0, jnp.minimum(j, lead - 1))),
             pl.BlockSpec((slots, step), lambda j, s: (0, jnp.maximum(j - lead, 0))),
-        ],
+        ]
+    out = call(
+        body,
+        "near_gradients" if near is None else "slot_gradients",
+        places,
+        ins,
+        specs,
+        outs,
+        out_specs,
         (steps,),
         after=after,
-    )
+        vmem=56,
+    )
+    return out[0] if near is None else out
 
 
 def combine(pair, returned, experts, after=()):
@@ -468,65 +487,58 @@
     others = {k: over_groups(cut[k], sets[k]) for k in order}
     partner = swap(own)
     near_gate, near_up = forward(expert, places, [own, partner], upstream, gate_w, up_w, [hidden])
-    epoch = [others[k] for k in order] + far_even + [near_gate]
+    near_back = slot_gradients(places, near_gate, [near_up], gate_w, up_w, after=[near_gate])
+    epoch = [others[k] for k in order] + far_even + [near_back]
 
     near_sent = {k: over_groups(tied(near_gate, *epoch), sets[k]) for k in order}
     far = []
     for value in far_even:
         far += [value, swap(tied(value, *epoch))]
-    end_columns = jnp.concatenate([others[k][:, wide:] for k in range(1, len(sets))], axis=1)
-    own_part = jnp.concatenate([others[k][:, :wide] for k in range(len(sets))], axis=1)
-    end_columns = tied(end_columns, *epoch)
+    end_columns = tied(others[order[0]], far[-1])
+    end_columns = jnp.concatenate(
+        [end_columns[:, wide:]] + [others[k][:, wide:] for k in range(1, len(sets)) if k != order[0]], axis=1
+    )
     end_far = [shift(end_columns, by) for by in chips]
     far_gate, *ups = forward(
-        expert,
-        places,
-        far,
-        upstream,
-        gate_w,
-        up_w,
-        up_parts,
-        first=near_up,
-        after=[near_gate, end_columns],
-    )
-    end_rows = [end_columns, swap(tied(end_columns, *far))]
-    epoch = [near_sent[k] for k in order] + end_far + [far_gate, end_rows[1]]
-
-    far_sent = {k: over_groups(tied(far_gate, *epoch), sets[k]) for k in order}
-    for value in end_far:
-        end_rows += [value, swap(tied(value, *epoch))]
-    own_part = tied(own_part, *epoch)
-    column_rows = [own_part]
-    column_far = [shift(own_part, by) for by in chips]
-    first_back, second_back = slot_gradients(
-        places, [near_gate, far_gate], ups, gate_w, up_w, after=[end_rows[-1]]
-    )
-    first_back = to_sources(first_back)
+        expert, places, far, upstream, gate_w, up_w, up_parts, first=near_up, after=[near_back]
+    )
     own_columns = [own, partner] + far
     own_lines = own_columns
     if wide != block:
         own_columns = [cut_padded(v, own_blocks, block, wide) for v in own_columns]
         own_blocks = [jnp.int32(0), jnp.int32(1)]
     own_picked = pick_rows(
-        expert, own_blocks, own_columns, capacity, wide, routes=own_lines, after=[second_back]
-    )
-    column_rows.append(swap(tied(own_part, *end_rows)))
+        expert, own_blocks, own_columns, capacity, wide, routes=own_lines, after=[far_gate]
+    )
+    epoch = [near_sent[k] for k in order] + [own_picked]
+
+    far_sent = {k: over_groups(tied(far_gate, *epoch), sets[k]) for k in order}
+    first_back, second_back = slot_gradients(
+        places, far_gate, ups, gate_w, up_w, near=near_back, after=[own_picked]
+    )
+    first_back = to_sources(first_back)
+    end_rows = []
+    for value in [end_columns] + end_far:
+        end_rows += [value, swap(tied(value, *epoch))]
+    own_part = tied(others[0], *end_far)
+    own_part = jnp.concatenate([own_part] + [others[k][:, :wide] for k in range(1, len(sets))], axis=1)
+    column_far = [shift(own_part, by) for by in chips]
     end_picked = pick_rows(
-        expert, [jnp.int32(k) for k in range(len(sets) - 1)], end_rows, capacity, wide, after=[own_picked]
-    )
-    epoch = [far_sent[k] for k in order] + [end_picked] + column_far + column_rows
+        expert, [jnp.int32(k) for k in range(len(sets) - 1)], end_rows, capacity, wide, after=[second_back]
+    )
+    epoch = [far_sent[k] for k in order] + [end_picked]
 
     def parts_of(c):
-        if c < 2:
+        if c == 0:
             out = [[(near_gate, c), (far_gate, c)]]
             out += [[(near_sent[k], c), (far_sent[k], c)] for k in range(len(sets))]
         else:
-            out = [[(ups[c - 2], 0)]] + [[(up_sent[c - 2][k], 0)] for k in range(len(sets))]
+            out = [[(ups[c - 1], 0)]] + [[(up_sent[c - 1][k], 0)] for k in range(len(sets))]
         return out
 
     def for_end(c, after):
         parts = parts_of(c)
-        part = hidden // 2 if c < 2 else up_parts[c - 2]
+        part = up_parts[c - 1] if c else hidden
         terms = [(own_picked, 1, parts[0])]
         terms += [(end_picked, k - 1, parts[1 + k]) for k in range(1, len(sets))]
         return products(terms, wide, part, BF16, "for_end", after=after)
@@ -544,34 +556,33 @@
         return [up_sent[c][k] for k in order]
 
     arriving = send_up(0)
-    for value in column_far:
+    column_rows = []
+    for value in [own_part] + column_far:
         column_rows += [value, swap(tied(value, *epoch))]
-    end0 = for_end(0, epoch[:1])
+    end0 = for_end(0, [end_picked])
     extra0 = to_ends(end0)
-    end1 = for_end(1, [end0])
-    extra1 = to_ends(tied(end1, *column_rows))
     picked = pick_rows(
-        expert, [jnp.int32(k) for k in range(len(sets))], column_rows, capacity, wide, after=[end1]
-    )
-    epoch = arriving + [picked, extra0]
+        expert, [jnp.int32(k) for k in range(len(sets))], column_rows, capacity, wide, after=[end0]
+    )
+    epoch = arriving + [picked, first_back]
 
     arriving = send_up(1)
-    second_back = to_sources(tied(second_back, first_back, *epoch))
-    end2 = for_end(2, epoch[:1])
+    second_back = to_sources(tied(second_back, *epoch))
+    end1 = for_end(1, [picked])
+    extra1 = to_ends(end1)
+    first_tok = combine(pair, first_back, experts, after=[end1])
+    first_passed = passed_on(first_tok)
+    gate = for_own(0, hidden, BF16, [first_tok], extras=[extra0])
+    epoch = arriving + [gate]
+
+    end2 = for_end(2, epoch)
     extra2 = to_ends(end2)
-    first_tok = combine(pair, first_back, experts, after=[end2])
-    first_passed = passed_on(tied(first_tok, extra1))
-    gate = for_own(0, hidden, BF16, [first_tok], extras=[extra0, extra1])
-    epoch = arriving + [gate]
-
-    end3 = for_end(3, epoch)
-    extra3 = to_ends(end3)
-    second_tok = combine(pair, second_back, experts, after=[end3])
+    second_tok = combine(pair, second_back, experts, after=[end2])
     second_passed = passed_on(second_tok)
-    up0 = for_own(2, up_parts[0], BF16, [second_tok], extras=[extra2], total=hidden)
-    own3 = for_own(3, up_parts[1], F32, [up0])
-    passed = jnp.concatenate([tied(first_passed, own3), second_passed], axis=1)
-    up1 = finish(own3, extra3, up0, up_parts[0] // up_parts[1], hidden)
+    up0 = for_own(1, up_parts[0], BF16, [second_tok], extras=[extra1], total=hidden)
+    own2 = for_own(2, up_parts[1], F32, [up0])
+    passed = jnp.concatenate([tied(first_passed, own2), second_passed], axis=1)
+    up1 = finish(own2, extra2, up0, up_parts[0] // up_parts[1], hidden)
     return (passed[None], gate[None, None, :block], up1[None, None, :block])
 
 

time: 273 us -> 254 us (0.930)
  waiting for transfers between devices: 50.5 us -> 34.2 us
  Pallas kernels: 129 us -> 117 us
  local copies, waits for them, and re-layouts: 9.61 us -> 16.3 us
    ppermute x15, waiting for transfers between devices: 37.9 us -> 17.3 us  [over_groups(): return lax.ppermute(value, 'dp', pairs)]
    pallas_call x17, Pallas kernels: 129 us -> 117 us  [call(): pl.pallas_call(kernel, name=name, out_shape=[jax.ShapeDtypeStruct(shape,...]
    unnamed x54 -> x66, local copies, waits for them, and re-layouts: 6.26 us -> 11.7 us
    ppermute x4 -> x3, waiting for transfers between devices: 8.25 us -> 9.76 us  [to_ends(): return lax.ppermute(value, 'dp', [(1, 0), (groups - 2, groups - 1)])]
  transfers between devices with their start and end apart: 32 -> 31, of which waited for: 6 -> 8; matrix products, arithmetic and copies ran while one was open for 3% -> 3% of each run, Pallas kernels for 45% -> 45%
where the time goes in v2:
time: 254 us; the launch traced here: 252 us
  Pallas kernels  117 us (46%)
  starting transfers between devices  75.4 us (30%)
  waiting for transfers between devices  34.2 us (13%)
  local copies, waits for them, and re-layouts  16.3 us (6%)
  other arithmetic  7.89 us (3%)
    pallas_call x17, Pallas kernels, call(): pl.pallas_call(kernel, name=name, out_shape=[jax.ShapeDtypeStruct(shape,...  117 us
    ppermute x15, starting transfers between devices, over_groups(): return lax.ppermute(value, 'dp', pairs)  52.7 us
    ppermute x15, waiting for transfers between devices, over_groups(): return lax.ppermute(value, 'dp', pairs)  17.3 us
    unnamed x66, local copies, waits for them, and re-layouts  11.7 us
    ppermute x3, waiting for transfers between devices, to_ends(): return lax.ppermute(value, 'dp', [(1, 0), (groups - 2, groups - 1)])  9.76 us
    all_to_all x2, starting transfers between devices, to_sources(): lax.all_to_all(value.reshape(experts, capacity, value.shape[1]), 'expert'...  9.25 us
    ppermute x3, starting transfers between devices, shift(): lax.ppermute(value, 'expert', [(s, (s + 2 * by) % experts) for s in range...  5.78 us
  transfers between devices with their start and end apart: 31, of which 8 were waited for; matrix products, arithmetic and copies ran while one was open for 3% of the time, Pallas kernels for 45%

profile of v2, /device:TPU:0, one launch (start us, length us, event | category | flops | bytes accessed | tf_op | source)
XLA Modules:
  0.0 252.0 jit_solution(6551552818159076287)
XLA Ops:
  0.8 1.5 copy-done.8
  2.3 0.7 copy-done.30
  2.9 3.0 %cut_columns.1 = (bf16[272,3584]{1,0:T(8,128)(2,1)S(1)}, bf16[272,896]{1,0:T(8,128)(2,1)S(1)}, bf16[272,1792]{1,0:T(8,128)(2,1)}, bf16[272,1792]{1,0:T(8,128)(2,1)S(1)}) custom-call(s32[5]{0:T(128)S(1)} %stack.82.scalar_ref, s32[2,256]{1,0:T(2,128)S(1)} %bitcast.34, bf16[256,3584]{1,0:T(8,128)(2,1)S(1)} %bitcast.27, bf16[256,3584]{1,0:T(8,128)(2,1)S(1)} %bitcast.28, ...), custom_call_target="tpu_custom_call" | custom-call | flops 1 | bytes 1 | tf_op jit(solution)/shard_map/cut_columns/pallas_call | solution.py:48
  6.4 2.5 collective-permute-start
  8.9 1.6 collective-permute-start.1
  10.6 6.2 %collective-permute-start.2 = (bf16[272,1792]{1,0:T(8,128)(2,1)S(1)}, bf16[272,1792]{1,0:T(8,128)(2,1)}, u32[]{:S(2)}, u32[]{:S(2)}) collective-permute-start(bf16[272,1792]{1,0:T(8,128)(2,1)S(1)} %get-tuple-element.29), channel_id=1, source_target_pairs={{0,8},{12,4},{1,9},{13,5},{2,10},{14,6},{3,11},{15,7},{16,24},{28,... | collective-permute-start | bytes 2924552 | tf_op jit(solution)/shard_map/ppermute | solution.py:465
  16.8 2.1 collective-permute-start.3
  20.1 13.2 %forward_first.1 = (bf16[320,1024]{1,0:T(8,128)(2,1)}, bf16[320,1024]{1,0:T(8,128)(2,1)}) custom-call(s32[3]{0:T(128)} %pad_add_fusion.2.scalar_ref, bf16[272,3584]{1,0:T(8,128)(2,1)} %copy-done.9, bf16[272,3584]{1,0:T(8,128)(2,1)} %collective-permute-done.4.refs_1_.refs_5_, bf16[640,1024]{1,0:T(8,128)(2,1)} %bitcast.45, bf16[3584,1024]{1,0:T(8,128)(2,1)} %bitcast.37, ...), custom_call_target="tpu_custom_call" | custom-call | flops 1 | bytes 1 | tf_op jit(solution)/shard_map/forward_first/pallas_call | solution.py:48
  33.2 12.0 %near_gradients.1.refs_6_.refs_5_ = bf16[320,3584]{1,0:T(8,128)(2,1)} custom-call(s32[4]{0:T(128)} %pad_add_fusion.scalar_ref, bf16[3584,1024]{1,0:T(8,128)(2,1)} %bitcast.38, bf16[3584,1024]{1,0:T(8,128)(2,1)} %bitcast.42, bf16[320,1024]{1,0:T(8,128)(2,1)} %get-tuple-element.39.refs_2_.refs_4_.refs_3_, bf16[320,1024]{1,0:T(8,128)(2,1)} %get-tuple-element.32.refs_3_.refs_5_, ...), custom_call_target="tpu_custom_call" | custom-call | flops 1 | bytes 1 | tf_op jit(solution)/shard_map/near_gradients/pallas_call | solution.py:48
  45.2 2.0 collective-permute-done.3
  47.2 5.0 %collective-permute-done.refs_0_.refs_2_.refs_6_ = bf16[272,3584]{1,0:T(8,128)(2,1)} collective-permute-done((bf16[272,3584]{1,0:T(8,128)(2,1)S(1)}, bf16[272,3584]{1,0:T(8,128)(2,1)}, u32[]{:S(2)}, u32[]{:S(2)}) %collective-permute-start) | collective-permute-done | bytes 1949728 | tf_op jit(solution)/shard_map/ppermute | solution.py:462
  52.2 2.0 fusion
  54.2 2.1 collective-permute-done.5.refs_1_.refs_3_.refs_7_
  56.4 1.4 slice.12
  57.8 1.0 pad_maximum_fusion.1.refs_0_
  58.8 1.7 collective-permute-start.10
  60.5 0.7 collective-permute-start.6
  61.2 9.4 %collective-permute-start.7 = (bf16[320,1024]{1,0:T(8,128)(2,1)S(1)}, bf16[320,1024]{1,0:T(8,128)(2,1)}, u32[]{:S(2)}, u32[]{:S(2)}) collective-permute-start(bf16[320,1024]{1,0:T(8,128)(2,1)S(1)} %copy-done.14), channel_id=1, source_target_pairs={{0,8},{12,4},{1,9},{13,5},{2,10},{14,6},{3,11},{15,7},{16,24},{28,... | collective-permute-start | bytes 1966088 | tf_op jit(solution)/shard_map/ppermute | solution.py:465
  70.6 2.1 collective-permute-start.8
  73.4 13.6 %forward_rest.1 = (bf16[320,1024]{1,0:T(8,128)(2,1)}, bf16[640,512]{1,0:T(8,128)(2,1)}, bf16[640,512]{1,0:T(8,128)(2,1)}) custom-call(s32[3]{0:T(128)} %pad_add_fusion.1.scalar_ref, bf16[272,3584]{1,0:T(8,128)(2,1)} %collective-permute-done.refs_0_.refs_2_.refs_6_, bf16[272,3584]{1,0:T(8,128)(2,1)} %copy-done.11, bf16[640,1024]{1,0:T(8,128)(2,1)} %bitcast.46, ...), custom_call_target="tpu_custom_call" | custom-call | flops 1 | bytes 1 | tf_op jit(solution)/shard_map/forward_rest/pallas_call | solution.py:48
  87.0 1.5 copy-done.12
  88.6 4.2 %pick_rows.3.refs_6_.refs_0_ = bf16[1792,640]{1,0:T(8,128)(2,1)S(1)} custom-call(s32[3]{0:T(128)S(1)} %pad_add_fusion.3.scalar_ref, bf16[272,3584]{1,0:T(8,128)(2,1)S(1)} %copy-done.10, bf16[272,3584]{1,0:T(8,128)(2,1)} %collective-permute-done.4.refs_1_.refs_5_, bf16[272,3584]{1,0:T(8,128)(2,1)} %collective-permute-done.refs_0_.refs_2_.refs_6_, ...), custom_call_target="tpu_custom_call" | custom-call | flops 1 | bytes 1 | tf_op jit(solution)/shard_map/pick_rows/pallas_call | solution.py:48
  92.8 4.7 %collective-permute-done.8.refs_6_ = bf16[320,1024]{1,0:T(8,128)(2,1)} collective-permute-done((bf16[320,1024]{1,0:T(8,128)(2,1)S(1)}, bf16[320,1024]{1,0:T(8,128)(2,1)}, u32[]{:S(2)}, u32[]{:S(2)}) %collective-permute-start.8) | collective-permute-done | bytes 655392 | tf_op jit(solution)/shard_map/ppermute | solution.py:465
  97.5 1.1 slice.17
  99.2 2.2 pad_maximum_fusion.refs_0_
  101.4 1.5 collective-permute-start.18
  102.9 1.5 collective-permute-start.12
  104.5 7.2 %collective-permute-start.13 = (bf16[320,1024]{1,0:T(8,128)(2,1)}, bf16[320,1024]{1,0:T(8,128)(2,1)}, u32[]{:S(2)}, u32[]{:S(2)}) collective-permute-start(bf16[320,1024]{1,0:T(8,128)(2,1)} %get-tuple-element.43.refs_8_.refs_2_.refs_4_.refs_5_), channel_id=1, source_target_pairs={{0,8},{12,4},{1,9},{13,5},{2,10},{14,6},{3,11},{15,7},{16,24},{28,... | collective-permute-start | bytes 1966088 | tf_op jit(solution)/shard_map/ppermute | solution.py:465
  111.7 2.1 collective-permute-start.14
  113.8 13.7 %slot_gradients.1 = (bf16[640,2048]{1,0:T(8,128)(2,1)}, bf16[640,1536]{1,0:T(8,128)(2,1)}) custom-call(s32[4]{0:T(128)} %pad_add_fusion.scalar_ref, bf16[3584,1024]{1,0:T(8,128)(2,1)} %bitcast.40, bf16[3584,1024]{1,0:T(8,128)(2,1)} %bitcast.44, bf16[320,1024]{1,0:T(8,128)(2,1)} %get-tuple-element.43.refs_8_.refs_2_.refs_4_.refs_5_, ...), custom_call_target="tpu_custom_call" | custom-call | flops 1 | bytes 1 | tf_op jit(solution)/shard_map/slot_gradients/pallas_call | solution.py:48
  127.5 4.7 %all-to-all-start = ((bf16[4,160,2048]{2,1,0:T(8,128)(2,1)}), bf16[4,160,2048]{2,1,0:T(8,128)(2,1)}, u32[]{:S(2)}, u32[]{:S(2)}) async-start(bf16[4,160,2048]{2,1,0:T(8,128)(2,1)} %bitcast.47), calls=%async_computation | async-start | bytes 5242880 | tf_op jit(solution)/shard_map/all_to_all | solution.py:468
  132.3 1.2 copy-done.29
  133.5 4.4 %pick_rows.4.refs_1_.refs_2_.refs_9_ = bf16[1792,640]{1,0:T(8,128)(2,1)S(1)} custom-call(s32[3]{0:T(128)S(1)} %pad_add_fusion.4.scalar_ref, bf16[272,1792]{1,0:T(8,128)(2,1)} %pad_maximum_fusion.1.refs_0_, bf16[272,1792]{1,0:T(8,128)(2,1)S(1)} %copy-done.29, bf16[272,1792]{1,0:T(8,128)(2,1)} %collective-permute-done.10.refs_2_, ...), custom_call_target="tpu_custom_call" | custom-call | flops 1 | bytes 1 | tf_op jit(solution)/shard_map/pick_rows/pallas_call | solution.py:48
  137.9 0.9 collective-permute-done.14.refs_7_
  139.3 1.5 collective-permute-start.15
  140.8 7.1 %collective-permute-start.16 = (bf16[640,512]{1,0:T(8,128)(2,1)}, bf16[640,512]{1,0:T(8,128)(2,1)}, u32[]{:S(2)}, u32[]{:S(2)}) collective-permute-start(bf16[640,512]{1,0:T(8,128)(2,1)} %get-tuple-element.44.refs_3_.refs_4_), channel_id=1, source_target_pairs={{0,8},{12,4},{1,9},{13,5},{2,10},{14,6},{3,11},{15,7},{16,24},{28,... | collective-permute-start | bytes 1966088 | tf_op jit(solution)/shard_map/ppermute | solution.py:465
  147.9 2.1 collective-permute-start.21
  150.1 8.7 %for_end.3.refs_4_ = bf16[896,1024]{1,0:T(8,128)(2,1)} custom-call(s32[1]{0:T(128)} %constant.31.clone.1.scalar_ref, bf16[1792,640]{1,0:T(8,128)(2,1)S(1)} %copy-done.1, bf16[1792,640]{1,0:T(8,128)(2,1)S(1)} %pick_rows.4.refs_1_.refs_2_.refs_9_, bf16[1792,640]{1,0:T(8,128)(2,1)S(1)} %pick_rows.4.refs_1_.refs_2_.refs_9_, bf16[320,1024]{1,0:T(8,128)(2,1)S(1)} %copy-done.14, ...), custom_call_target="tpu_custom_call" | custom-call | flops 1 | bytes 1 | tf_op jit(solution)/shard_map/for_end/pallas_call | solution.py:48
  158.8 1.3 collective-permute-start.26
  160.2 5.4 %pick_rows.5.refs_6_.refs_1_.refs_2_.refs_3_ = bf16[2688,640]{1,0:T(8,128)(2,1)S(1)} custom-call(s32[4]{0:T(128)S(1)} %pad_add_fusion.5.scalar_ref, bf16[272,2688]{1,0:T(8,128)(2,1)} %pad_maximum_fusion.refs_0_, bf16[272,2688]{1,0:T(8,128)(2,1)S(1)} %collective-permute-done.17.refs_1_, bf16[272,2688]{1,0:T(8,128)(2,1)} %collective-permute-done.18.refs_2_, ...), custom_call_target="tpu_custom_call" | custom-call | flops 1 | bytes 1 | tf_op jit(solution)/shard_map/pick_rows/pallas_call | solution.py:48
  165.6 9.7 %collective-permute-done.21.refs_5_ = bf16[640,512]{1,0:T(8,128)(2,1)} collective-permute-done((bf16[640,512]{1,0:T(8,128)(2,1)}, bf16[640,512]{1,0:T(8,128)(2,1)}, u32[]{:S(2)}, u32[]{:S(2)}) %collective-permute-start.21) | collective-permute-done | bytes 655392 | tf_op jit(solution)/shard_map/ppermute | solution.py:465
  175.4 4.6 %all-to-all-start.1 = ((bf16[4,160,1536]{2,1,0:T(8,128)(2,1)}), bf16[4,160,1536]{2,1,0:T(8,128)(2,1)}, u32[]{:S(2)}, u32[]{:S(2)}) async-start(bf16[4,160,1536]{2,1,0:T(8,128)(2,1)} %bitcast.32), calls=%async_computation.1 | async-start | bytes 3932160 | tf_op jit(solution)/shard_map/all_to_all | solution.py:468
  179.9 4.4 %collective-permute-start.22 = (bf16[640,512]{1,0:T(8,128)(2,1)}, bf16[640,512]{1,0:T(8,128)(2,1)S(1)}, u32[]{:S(2)}, u32[]{:S(2)}) collective-permute-start(bf16[640,512]{1,0:T(8,128)(2,1)} %get-tuple-element.48.refs_4_.refs_3_), channel_id=1, source_target_pairs={{0,4},{12,8},{1,5},{13,9},{2,6},{14,10},{3,7},{15,11},{16,20},{28,... | collective-permute-start | bytes 1966088 | tf_op jit(solution)/shard_map/ppermute | solution.py:465
  184.4 0.7 collective-permute-start.23
  185.1 4.0 %collective-permute-start.24 = (bf16[640,512]{1,0:T(8,128)(2,1)}, bf16[640,512]{1,0:T(8,128)(2,1)S(1)}, u32[]{:S(2)}, u32[]{:S(2)}) collective-permute-start(bf16[640,512]{1,0:T(8,128)(2,1)} %get-tuple-element.48.refs_4_.refs_3_), channel_id=1, source_target_pairs={{0,8},{12,4},{1,9},{13,5},{2,10},{14,6},{3,11},{15,7},{16,24},{28,... | collective-permute-start | bytes 1966088 | tf_op jit(solution)/shard_map/ppermute | solution.py:465
  189.1 1.6 copy-done.2
  190.7 1.6 copy-done.6
  192.3 4.7 %for_end.4.refs_2_ = bf16[896,512]{1,0:T(8,128)(2,1)} custom-call(s32[1]{0:T(128)} %constant.31.clone.1.scalar_ref, bf16[1792,640]{1,0:T(8,128)(2,1)S(1)} %copy-done.2, bf16[1792,640]{1,0:T(8,128)(2,1)S(1)} %copy-done.6, bf16[1792,640]{1,0:T(8,128)(2,1)S(1)} %copy-done.6, bf16[640,512]{1,0:T(8,128)(2,1)} %get-tuple-element.44.refs_3_.refs_4_, ...), custom_call_target="tpu_custom_call" | custom-call | flops 1 | bytes 1 | tf_op jit(solution)/shard_map/for_end/pallas_call | solution.py:48
  197.1 4.8 %combine.2.refs_13_ = bf16[256,2048]{1,0:T(8,128)(2,1)} custom-call(s32[1]{0:T(128)} %constant.31.clone.1.scalar_ref, s32[2,256]{1,0:T(2,128)S(1)} %bitcast.35, bf16[640,2048]{1,0:T(8,128)(2,1)} %bitcast.20.refs_1_, bf16[896,512]{1,0:T(8,128)(2,1)} %for_end.4.refs_2_), custom_call_target="tpu_custom_call" | custom-call | flops 1 | bytes 1 | tf_op jit(solution)/shard_map/combine/pallas_call | solution.py:48
  201.9 1.5 collective-permute-start.20
  203.4 1.3 collective-permute-start.25
  204.7 11.3 %for_own.3.refs_9_ = bf16[896,1024]{1,0:T(8,128)(2,1)} custom-call(s32[1]{0:T(128)} %constant.31.clone.1.scalar_ref, bf16[1792,640]{1,0:T(8,128)(2,1)S(1)} %copy-done.3, bf16[2688,640]{1,0:T(8,128)(2,1)S(1)} %pick_rows.5.refs_6_.refs_1_.refs_2_.refs_3_, bf16[2688,640]{1,0:T(8,128)(2,1)S(1)} %pick_rows.5.refs_6_.refs_1_.refs_2_.refs_3_, ...), custom_call_target="tpu_custom_call" | custom-call | flops 1 | bytes 1 | tf_op jit(solution)/shard_map/for_own/pallas_call | solution.py:48
  216.1 1.9 copy-done.17
  218.1 3.3 %for_end.5.refs_2_ = bf16[896,512]{1,0:T(8,128)(2,1)} custom-call(s32[1]{0:T(128)} %constant.31.clone.1.scalar_ref, bf16[1792,640]{1,0:T(8,128)(2,1)S(1)} %copy-done.3, bf16[1792,640]{1,0:T(8,128)(2,1)S(1)} %copy-done.7, bf16[1792,640]{1,0:T(8,128)(2,1)S(1)} %copy-done.7, bf16[640,512]{1,0:T(8,128)(2,1)S(1)} %copy-done.18, ...), custom_call_target="tpu_custom_call" | custom-call | flops 1 | bytes 1 | tf_op jit(solution)/shard_map/for_end/pallas_call | solution.py:48
  221.4 1.3 collective-permute-start.28
  222.7 3.4 %combine.3.refs_9_ = bf16[256,1536]{1,0:T(8,128)(2,1)S(1)} custom-call(s32[1]{0:T(128)} %constant.31.clone.1.scalar_ref, s32[2,256]{1,0:T(2,128)S(1)} %bitcast.36, bf16[640,1536]{1,0:T(8,128)(2,1)} %bitcast.22.refs_1_, bf16[896,512]{1,0:T(8,128)(2,1)} %for_end.5.refs_2_), custom_call_target="tpu_custom_call" | custom-call | flops 1 | bytes 1 | tf_op jit(solution)/shard_map/combine/pallas_call | solution.py:48
  226.1 0.7 collective-permute-start.27
  226.9 1.4 collective-permute-done.25.refs_8_
  228.2 5.8 %for_own.4.refs_8_.refs_2_ = bf16[896,1024]{1,0:T(8,128)(2,1)} custom-call(s32[1]{0:T(128)} %constant.31.clone.1.scalar_ref, bf16[1792,640]{1,0:T(8,128)(2,1)S(1)} %copy-done.4, bf16[2688,640]{1,0:T(8,128)(2,1)S(1)} %pick_rows.5.refs_6_.refs_1_.refs_2_.refs_3_, bf16[2688,640]{1,0:T(8,128)(2,1)S(1)} %pick_rows.5.refs_6_.refs_1_.refs_2_.refs_3_, ...), custom_call_target="tpu_custom_call" | custom-call | flops 1 | bytes 1 | tf_op jit(solution)/shard_map/for_own/pallas_call | solution.py:48
  234.1 1.5 copy-done.13
  235.6 3.2 %for_own.5.refs_0_ = f32[896,512]{1,0:T(8,128)S(1)} custom-call(s32[1]{0:T(128)} %constant.31.clone.1.scalar_ref, bf16[1792,640]{1,0:T(8,128)(2,1)S(1)} %copy-done.4, bf16[2688,640]{1,0:T(8,128)(2,1)S(1)} %pick_rows.5.refs_6_.refs_1_.refs_2_.refs_3_, bf16[2688,640]{1,0:T(8,128)(2,1)S(1)} %pick_rows.5.refs_6_.refs_1_.refs_2_.refs_3_, ...), custom_call_target="tpu_custom_call" | custom-call | flops 1 | bytes 1 | tf_op jit(solution)/shard_map/for_own/pallas_call | solution.py:48
  238.8 8.4 %collective-permute-done.28.refs_1_ = bf16[896,512]{1,0:T(8,128)(2,1)} collective-permute-done((bf16[896,512]{1,0:T(8,128)(2,1)}, bf16[896,512]{1,0:T(8,128)(2,1)}, u32[]{:S(2)}, u32[]{:S(2)}) %collective-permute-start.28) | collective-permute-done | bytes 917536 | tf_op jit(solution)/shard_map/ppermute | solution.py:477
  247.2 2.3 finish.1
  249.4 2.6 %maximum_bitcast_fusion = bf16[1,256,3584]{2,1,0:T(8,128)(2,1)} fusion(bf16[256,1536]{1,0:T(8,128)(2,1)S(1)} %collective-permute-done.27, bf16[256,2048]{1,0:T(8,128)(2,1)} %collective-permute-done.20), kind=kLoop, calls=%fused_computation | loop fusion | flops 3670016 | bytes 3670016 | tf_op jit(solution)/shard_map/broadcast_in_dim | solution.py:586
  (94 shorter events, 3.9 us)
Async XLA Ops:
  0.7 1.5 copy-start.8
  2.2 0.7 copy-start.30
  6.0 14.1 %copy-start.9 = (bf16[272,3584]{1,0:T(8,128)(2,1)}, bf16[272,3584]{1,0:T(8,128)(2,1)S(1)}, u32[]{:S(2)}) copy-start(bf16[272,3584]{1,0:T(8,128)(2,1)S(1)} %get-tuple-element.27.refs_0_.refs_4_) | copy-start | bytes 5849092
  6.0 14.1 %collective-permute-start.4 = (bf16[272,3584]{1,0:T(8,128)(2,1)S(1)}, bf16[272,3584]{1,0:T(8,128)(2,1)}, u32[]{:S(2)}, u32[]{:S(2)}) collective-permute-start(bf16[272,3584]{1,0:T(8,128)(2,1)S(1)} %get-tuple-element.27.refs_0_.refs_4_), channel_id=1, source_target_pairs={{0,1},{1,0},{2,3},{3,2},{4,5},{5,4},{6,7},{7,6},{8,9},{9,8},{10,11... | collective-permute-start | bytes 5849096 | tf_op jit(solution)/shard_map/ppermute | solution.py:459
  6.4 45.8 %collective-permute-start = (bf16[272,3584]{1,0:T(8,128)(2,1)S(1)}, bf16[272,3584]{1,0:T(8,128)(2,1)}, u32[]{:S(2)}, u32[]{:S(2)}) collective-permute-start(bf16[272,3584]{1,0:T(8,128)(2,1)S(1)} %get-tuple-element.27.refs_0_.refs_4_), channel_id=1, source_target_pairs={{0,2},{1,3},{2,0},{3,1},{4,6},{5,7},{6,4},{7,5},{8,10},{9,11},{10,... | collective-permute-start | bytes 5849096 | tf_op jit(solution)/shard_map/ppermute | solution.py:462
  8.9 38.3 %collective-permute-start.1 = (bf16[272,1792]{1,0:T(8,128)(2,1)}, bf16[272,1792]{1,0:T(8,128)(2,1)}, u32[]{:S(2)}, u32[]{:S(2)}) collective-permute-start(bf16[272,1792]{1,0:T(8,128)(2,1)} %get-tuple-element.28), channel_id=1, source_target_pairs={{4,8},{8,4},{5,9},{9,5},{6,10},{10,6},{7,11},{11,7},{20,24},{24,20... | collective-permute-start | bytes 2924552 | tf_op jit(solution)/shard_map/ppermute | solution.py:465
  10.6 36.7 %collective-permute-start.2 = (bf16[272,1792]{1,0:T(8,128)(2,1)S(1)}, bf16[272,1792]{1,0:T(8,128)(2,1)}, u32[]{:S(2)}, u32[]{:S(2)}) collective-permute-start(bf16[272,1792]{1,0:T(8,128)(2,1)S(1)} %get-tuple-element.29), channel_id=1, source_target_pairs={{0,8},{12,4},{1,9},{13,5},{2,10},{14,6},{3,11},{15,7},{16,24},{28,... | collective-permute-start | bytes 2924552 | tf_op jit(solution)/shard_map/ppermute | solution.py:465
  16.8 30.4 %collective-permute-start.3 = (bf16[272,896]{1,0:T(8,128)(2,1)S(1)}, bf16[272,896]{1,0:T(8,128)(2,1)}, u32[]{:S(2)}, u32[]{:S(2)}) collective-permute-start(bf16[272,896]{1,0:T(8,128)(2,1)S(1)} %get-tuple-element.30), channel_id=1, source_target_pairs={{0,4},{12,8},{1,5},{13,9},{2,6},{14,10},{3,7},{15,11},{16,20},{28,... | collective-permute-start | bytes 1462280 | tf_op jit(solution)/shard_map/ppermute | solution.py:465
  52.2 4.2 %collective-permute-start.5 = (bf16[272,3584]{1,0:T(8,128)(2,1)}, bf16[272,3584]{1,0:T(8,128)(2,1)S(1)}, u32[]{:S(2)}, u32[]{:S(2)}) collective-permute-start(bf16[272,3584]{1,0:T(8,128)(2,1)} %collective-permute-done.refs_0_.refs_2_.refs_6_), channel_id=1, source_target_pairs={{0,1},{1,0},{2,3},{3,2},{4,5},{5,4},{6,7},{7,6},{8,9},{9,8},{10,11... | collective-permute-start | bytes 5849096 | tf_op jit(solution)/shard_map/ppermute | solution.py:459
  54.2 6.3 %copy-start.14 = (bf16[320,1024]{1,0:T(8,128)(2,1)S(1)}, bf16[320,1024]{1,0:T(8,128)(2,1)}, u32[]{:S(2)}) copy-start(bf16[320,1024]{1,0:T(8,128)(2,1)} %get-tuple-element.39.refs_2_.refs_4_.refs_3_) | copy-start | bytes 1966084
  56.4 17.0 %copy-start.11 = (bf16[272,3584]{1,0:T(8,128)(2,1)}, bf16[272,3584]{1,0:T(8,128)(2,1)S(1)}, u32[]{:S(2)}) copy-start(bf16[272,3584]{1,0:T(8,128)(2,1)S(1)} %collective-permute-done.5.refs_1_.refs_3_.refs_7_) | copy-start | bytes 5849092
  58.8 39.8 %collective-permute-start.10 = (bf16[272,1792]{1,0:T(8,128)(2,1)}, bf16[272,1792]{1,0:T(8,128)(2,1)}, u32[]{:S(2)}, u32[]{:S(2)}) collective-permute-start(bf16[272,1792]{1,0:T(8,128)(2,1)} %pad_maximum_fusion.1.refs_0_), channel_id=1, source_target_pairs={{0,2},{1,3},{2,0},{3,1},{4,6},{5,7},{6,4},{7,5},{8,10},{9,11},{10,... | collective-permute-start | bytes 2924552 | tf_op jit(solution)/shard_map/ppermute | solution.py:462
  60.5 32.3 %collective-permute-start.6 = (bf16[320,1024]{1,0:T(8,128)(2,1)S(1)}, bf16[320,1024]{1,0:T(8,128)(2,1)S(1)}, u32[]{:S(2)}, u32[]{:S(2)}) collective-permute-start(bf16[320,1024]{1,0:T(8,128)(2,1)S(1)} %copy-done.14), channel_id=1, source_target_pairs={{4,8},{8,4},{5,9},{9,5},{6,10},{10,6},{7,11},{11,7},{20,24},{24,20... | collective-permute-start | bytes 1966088 | tf_op jit(solution)/shard_map/ppermute | solution.py:465
  61.2 31.6 %collective-permute-start.7 = (bf16[320,1024]{1,0:T(8,128)(2,1)S(1)}, bf16[320,1024]{1,0:T(8,128)(2,1)}, u32[]{:S(2)}, u32[]{:S(2)}) collective-permute-start(bf16[320,1024]{1,0:T(8,128)(2,1)S(1)} %copy-done.14), channel_id=1, source_target_pairs={{0,8},{12,4},{1,9},{13,5},{2,10},{14,6},{3,11},{15,7},{16,24},{28,... | collective-permute-start | bytes 1966088 | tf_op jit(solution)/shard_map/ppermute | solution.py:465
  70.6 26.9 %collective-permute-start.8 = (bf16[320,1024]{1,0:T(8,128)(2,1)S(1)}, bf16[320,1024]{1,0:T(8,128)(2,1)}, u32[]{:S(2)}, u32[]{:S(2)}) collective-permute-start(bf16[320,1024]{1,0:T(8,128)(2,1)S(1)} %copy-done.14), channel_id=1, source_target_pairs={{0,4},{12,8},{1,5},{13,9},{2,6},{14,10},{3,7},{15,11},{16,20},{28,... | collective-permute-start | bytes 1966088 | tf_op jit(solution)/shard_map/ppermute | solution.py:465
  73.4 13.6 %copy-start.10 = (bf16[272,3584]{1,0:T(8,128)(2,1)S(1)}, bf16[272,3584]{1,0:T(8,128)(2,1)}, u32[]{:S(2)}) copy-start(bf16[272,3584]{1,0:T(8,128)(2,1)} %copy-done.9) | copy-start | bytes 5849092
  87.0 1.5 copy-start.12
  88.6 10.6 %copy-start.32 = (bf16[272,896]{1,0:T(8,128)(2,1)S(1)}, bf16[272,896]{1,0:T(8,128)(2,1)}, u32[]{:S(2)}) copy-start(bf16[272,896]{1,0:T(8,128)(2,1)} %get-tuple-element.51) | copy-start | bytes 1462276
  92.8 8.6 %copy-start = (bf16[1792,640]{1,0:T(8,128)(2,1)}, bf16[1792,640]{1,0:T(8,128)(2,1)S(1)}, u32[]{:S(2)}) copy-start(bf16[1792,640]{1,0:T(8,128)(2,1)S(1)} %pick_rows.3.refs_6_.refs_0_) | copy-start | bytes 6881284
  92.8 57.3 %copy-start.24 = (bf16[320,1024]{1,0:T(8,128)(2,1)}, bf16[320,1024]{1,0:T(8,128)(2,1)S(1)}, u32[]{:S(2)}) copy-start(bf16[320,1024]{1,0:T(8,128)(2,1)S(1)} %collective-permute-done.6.refs_5_.refs_8_) | copy-start | bytes 1966084
  97.5 14.2 %collective-permute-start.9 = (bf16[272,1792]{1,0:T(8,128)(2,1)}, bf16[272,1792]{1,0:T(8,128)(2,1)S(1)}, u32[]{:S(2)}, u32[]{:S(2)}) collective-permute-start(bf16[272,1792]{1,0:T(8,128)(2,1)} %pad_maximum_fusion.1.refs_0_), channel_id=1, source_target_pairs={{0,1},{1,0},{2,3},{3,2},{4,5},{5,4},{6,7},{7,6},{8,9},{9,8},{10,11... | collective-permute-start | bytes 2924552 | tf_op jit(solution)/shard_map/ppermute | solution.py:459
  98.6 33.7 %collective-permute-start.11 = (bf16[272,1792]{1,0:T(8,128)(2,1)}, bf16[272,1792]{1,0:T(8,128)(2,1)}, u32[]{:S(2)}, u32[]{:S(2)}) collective-permute-start(bf16[272,1792]{1,0:T(8,128)(2,1)} %collective-permute-done.10.refs_2_), channel_id=1, source_target_pairs={{0,1},{1,0},{2,3},{3,2},{4,5},{5,4},{6,7},{7,6},{8,9},{9,8},{10,11... | collective-permute-start | bytes 2924552 | tf_op jit(solution)/shard_map/ppermute | solution.py:459
  101.4 37.4 %collective-permute-start.18 = (bf16[272,2688]{1,0:T(8,128)(2,1)}, bf16[272,2688]{1,0:T(8,128)(2,1)}, u32[]{:S(2)}, u32[]{:S(2)}) collective-permute-start(bf16[272,2688]{1,0:T(8,128)(2,1)} %pad_maximum_fusion.refs_0_), channel_id=1, source_target_pairs={{0,2},{1,3},{2,0},{3,1},{4,6},{5,7},{6,4},{7,5},{8,10},{9,11},{10,... | collective-permute-start | bytes 4386824 | tf_op jit(solution)/shard_map/ppermute | solution.py:462
  102.9 35.0 %collective-permute-start.12 = (bf16[320,1024]{1,0:T(8,128)(2,1)}, bf16[320,1024]{1,0:T(8,128)(2,1)}, u32[]{:S(2)}, u32[]{:S(2)}) collective-permute-start(bf16[320,1024]{1,0:T(8,128)(2,1)} %get-tuple-element.43.refs_8_.refs_2_.refs_4_.refs_5_), channel_id=1, source_target_pairs={{4,8},{8,4},{5,9},{9,5},{6,10},{10,6},{7,11},{11,7},{20,24},{24,20... | collective-permute-start | bytes 1966088 | tf_op jit(solution)/shard_map/ppermute | solution.py:465
  104.5 33.5 %collective-permute-start.13 = (bf16[320,1024]{1,0:T(8,128)(2,1)}, bf16[320,1024]{1,0:T(8,128)(2,1)}, u32[]{:S(2)}, u32[]{:S(2)}) collective-permute-start(bf16[320,1024]{1,0:T(8,128)(2,1)} %get-tuple-element.43.refs_8_.refs_2_.refs_4_.refs_5_), channel_id=1, source_target_pairs={{0,8},{12,4},{1,9},{13,5},{2,10},{14,6},{3,11},{15,7},{16,24},{28,... | collective-permute-start | bytes 1966088 | tf_op jit(solution)/shard_map/ppermute | solution.py:465
  111.7 15.9 %copy-start.28 = (bf16[272,1792]{1,0:T(8,128)(2,1)}, bf16[272,1792]{1,0:T(8,128)(2,1)S(1)}, u32[]{:S(2)}) copy-start(bf16[272,1792]{1,0:T(8,128)(2,1)S(1)} %collective-permute-done.9.refs_1_) | copy-start | bytes 2924548
  111.7 27.1 %collective-permute-start.14 = (bf16[320,1024]{1,0:T(8,128)(2,1)}, bf16[320,1024]{1,0:T(8,128)(2,1)}, u32[]{:S(2)}, u32[]{:S(2)}) collective-permute-start(bf16[320,1024]{1,0:T(8,128)(2,1)} %get-tuple-element.43.refs_8_.refs_2_.refs_4_.refs_5_), channel_id=1, source_target_pairs={{0,4},{12,8},{1,5},{13,9},{2,6},{14,10},{3,7},{15,11},{16,20},{28,... | collective-permute-start | bytes 1966088 | tf_op jit(solution)/shard_map/ppermute | solution.py:465
  127.5 4.8 %copy-start.16 = (bf16[640,1536]{1,0:T(8,128)(2,1)S(1)}, bf16[640,1536]{1,0:T(8,128)(2,1)}, u32[]{:S(2)}) copy-start(bf16[640,1536]{1,0:T(8,128)(2,1)} %get-tuple-element.49.refs_4_) | copy-start | bytes 5898244
  127.5 38.1 %all-to-all-start = ((bf16[4,160,2048]{2,1,0:T(8,128)(2,1)}), bf16[4,160,2048]{2,1,0:T(8,128)(2,1)}, u32[]{:S(2)}, u32[]{:S(2)}) async-start(bf16[4,160,2048]{2,1,0:T(8,128)(2,1)} %bitcast.47), calls=%async_computation | async-start | bytes 5242880 | tf_op jit(solution)/shard_map/all_to_all | solution.py:468
  132.3 1.2 copy-start.29
  133.5 16.6 %copy-start.1 = (bf16[1792,640]{1,0:T(8,128)(2,1)S(1)}, bf16[1792,640]{1,0:T(8,128)(2,1)}, u32[]{:S(2)}) copy-start(bf16[1792,640]{1,0:T(8,128)(2,1)} %copy-done) | copy-start | bytes 6881284
  137.9 20.9 %copy-start.5 = (bf16[1792,640]{1,0:T(8,128)(2,1)}, bf16[1792,640]{1,0:T(8,128)(2,1)S(1)}, u32[]{:S(2)}) copy-start(bf16[1792,640]{1,0:T(8,128)(2,1)S(1)} %pick_rows.4.refs_1_.refs_2_.refs_9_) | copy-start | bytes 6881284
  138.8 20.0 %collective-permute-start.17 = (bf16[272,2688]{1,0:T(8,128)(2,1)}, bf16[272,2688]{1,0:T(8,128)(2,1)S(1)}, u32[]{:S(2)}, u32[]{:S(2)}) collective-permute-start(bf16[272,2688]{1,0:T(8,128)(2,1)} %pad_maximum_fusion.refs_0_), channel_id=1, source_target_pairs={{0,1},{1,0},{2,3},{3,2},{4,5},{5,4},{6,7},{7,6},{8,9},{9,8},{10,11... | collective-permute-start | bytes 4386824 | tf_op jit(solution)/shard_map/ppermute | solution.py:459
  138.8 21.4 %collective-permute-start.19 = (bf16[272,2688]{1,0:T(8,128)(2,1)}, bf16[272,2688]{1,0:T(8,128)(2,1)S(1)}, u32[]{:S(2)}, u32[]{:S(2)}) collective-permute-start(bf16[272,2688]{1,0:T(8,128)(2,1)} %collective-permute-done.18.refs_2_), channel_id=1, source_target_pairs={{0,1},{1,0},{2,3},{3,2},{4,5},{5,4},{6,7},{7,6},{8,9},{9,8},{10,11... | collective-permute-start | bytes 4386824 | tf_op jit(solution)/shard_map/ppermute | solution.py:459
  139.3 26.3 %collective-permute-start.15 = (bf16[640,512]{1,0:T(8,128)(2,1)}, bf16[640,512]{1,0:T(8,128)(2,1)}, u32[]{:S(2)}, u32[]{:S(2)}) collective-permute-start(bf16[640,512]{1,0:T(8,128)(2,1)} %get-tuple-element.44.refs_3_.refs_4_), channel_id=1, source_target_pairs={{4,8},{8,4},{5,9},{9,5},{6,10},{10,6},{7,11},{11,7},{20,24},{24,20... | collective-permute-start | bytes 1966088 | tf_op jit(solution)/shard_map/ppermute | solution.py:465
  140.8 24.8 %collective-permute-start.16 = (bf16[640,512]{1,0:T(8,128)(2,1)}, bf16[640,512]{1,0:T(8,128)(2,1)}, u32[]{:S(2)}, u32[]{:S(2)}) collective-permute-start(bf16[640,512]{1,0:T(8,128)(2,1)} %get-tuple-element.44.refs_3_.refs_4_), channel_id=1, source_target_pairs={{0,8},{12,4},{1,9},{13,5},{2,10},{14,6},{3,11},{15,7},{16,24},{28,... | collective-permute-start | bytes 1966088 | tf_op jit(solution)/shard_map/ppermute | solution.py:465
  147.9 27.4 %collective-permute-start.21 = (bf16[640,512]{1,0:T(8,128)(2,1)}, bf16[640,512]{1,0:T(8,128)(2,1)}, u32[]{:S(2)}, u32[]{:S(2)}) collective-permute-start(bf16[640,512]{1,0:T(8,128)(2,1)} %get-tuple-element.44.refs_3_.refs_4_), channel_id=1, source_target_pairs={{0,4},{12,8},{1,5},{13,9},{2,6},{14,10},{3,7},{15,11},{16,20},{28,... | collective-permute-start | bytes 1966088 | tf_op jit(solution)/shard_map/ppermute | solution.py:465
  158.8 44.6 %collective-permute-start.26 = (bf16[896,1024]{1,0:T(8,128)(2,1)}, bf16[896,1024]{1,0:T(8,128)(2,1)}, u32[]{:S(2)}, u32[]{:S(2)}) collective-permute-start(bf16[896,1024]{1,0:T(8,128)(2,1)} %for_end.3.refs_4_), channel_id=1, source_target_pairs={{4,0},{8,12},{5,1},{9,13},{6,2},{10,14},{7,3},{11,15},{20,16},{24,... | collective-permute-start | bytes 5505032 | tf_op jit(solution)/shard_map/ppermute | solution.py:477
  175.4 21.7 %copy-start.31 = (s32[1,256,2]{1,2,0:T(2,128)S(1)}, s32[1,256,2]{1,2,0:T(2,128)}, u32[]{:S(2)}) copy-start(s32[1,256,2]{1,2,0:T(2,128)} %param.6) | copy-start | bytes 6148
  175.4 47.3 %all-to-all-start.1 = ((bf16[4,160,1536]{2,1,0:T(8,128)(2,1)}), bf16[4,160,1536]{2,1,0:T(8,128)(2,1)}, u32[]{:S(2)}, u32[]{:S(2)}) async-start(bf16[4,160,1536]{2,1,0:T(8,128)(2,1)} %bitcast.32), calls=%async_computation.1 | async-start | bytes 3932160 | tf_op jit(solution)/shard_map/all_to_all | solution.py:468
  179.9 36.1 %collective-permute-start.22 = (bf16[640,512]{1,0:T(8,128)(2,1)}, bf16[640,512]{1,0:T(8,128)(2,1)S(1)}, u32[]{:S(2)}, u32[]{:S(2)}) collective-permute-start(bf16[640,512]{1,0:T(8,128)(2,1)} %get-tuple-element.48.refs_4_.refs_3_), channel_id=1, source_target_pairs={{0,4},{12,8},{1,5},{13,9},{2,6},{14,10},{3,7},{15,11},{16,20},{28,... | collective-permute-start | bytes 1966088 | tf_op jit(solution)/shard_map/ppermute | solution.py:465
  184.4 31.7 %collective-permute-start.23 = (bf16[640,512]{1,0:T(8,128)(2,1)}, bf16[640,512]{1,0:T(8,128)(2,1)S(1)}, u32[]{:S(2)}, u32[]{:S(2)}) collective-permute-start(bf16[640,512]{1,0:T(8,128)(2,1)} %get-tuple-element.48.refs_4_.refs_3_), channel_id=1, source_target_pairs={{4,8},{8,4},{5,9},{9,5},{6,10},{10,6},{7,11},{11,7},{20,24},{24,20... | collective-permute-start | bytes 1966088 | tf_op jit(solution)/shard_map/ppermute | solution.py:465
  185.1 31.0 %collective-permute-start.24 = (bf16[640,512]{1,0:T(8,128)(2,1)}, bf16[640,512]{1,0:T(8,128)(2,1)S(1)}, u32[]{:S(2)}, u32[]{:S(2)}) collective-permute-start(bf16[640,512]{1,0:T(8,128)(2,1)} %get-tuple-element.48.refs_4_.refs_3_), channel_id=1, source_target_pairs={{0,8},{12,4},{1,9},{13,5},{2,10},{14,6},{3,11},{15,7},{16,24},{28,... | collective-permute-start | bytes 1966088 | tf_op jit(solution)/shard_map/ppermute | solution.py:465
  189.0 1.6 copy-start.2
  190.7 1.6 copy-start.6
  197.1 7.6 %copy-start.3 = (bf16[1792,640]{1,0:T(8,128)(2,1)S(1)}, bf16[1792,640]{1,0:T(8,128)(2,1)}, u32[]{:S(2)}) copy-start(bf16[1792,640]{1,0:T(8,128)(2,1)} %copy-done) | copy-start | bytes 6881284
  197.1 7.6 %copy-start.15 = (bf16[320,1024]{1,0:T(8,128)(2,1)S(1)}, bf16[320,1024]{1,0:T(8,128)(2,1)}, u32[]{:S(2)}) copy-start(bf16[320,1024]{1,0:T(8,128)(2,1)} %get-tuple-element.39.refs_2_.refs_4_.refs_3_) | copy-start | bytes 1966084
  197.1 7.6 %copy-start.25 = (bf16[320,1024]{1,0:T(8,128)(2,1)S(1)}, bf16[320,1024]{1,0:T(8,128)(2,1)}, u32[]{:S(2)}) copy-start(bf16[320,1024]{1,0:T(8,128)(2,1)} %copy-done.24) | copy-start | bytes 1966084
  201.9 14.2 %copy-start.7 = (bf16[1792,640]{1,0:T(8,128)(2,1)S(1)}, bf16[1792,640]{1,0:T(8,128)(2,1)}, u32[]{:S(2)}) copy-start(bf16[1792,640]{1,0:T(8,128)(2,1)} %copy-done.5) | copy-start | bytes 6881284
  201.9 14.2 %copy-start.18 = (bf16[640,512]{1,0:T(8,128)(2,1)S(1)}, bf16[640,512]{1,0:T(8,128)(2,1)}, u32[]{:S(2)}) copy-start(bf16[640,512]{1,0:T(8,128)(2,1)} %get-tuple-element.48.refs_4_.refs_3_) | copy-start | bytes 1966084
  201.9 36.8 %collective-permute-start.20 = (bf16[256,2048]{1,0:T(8,128)(2,1)}, bf16[256,2048]{1,0:T(8,128)(2,1)}, u32[]{:S(2)}, u32[]{:S(2)}) collective-permute-start(bf16[256,2048]{1,0:T(8,128)(2,1)} %combine.2.refs_13_), channel_id=1, source_target_pairs={{0,16},{16,0},{1,17},{17,1},{2,18},{18,2},{3,19},{19,3},{4,20},{20... | collective-permute-start | bytes 3145736 | tf_op jit(solution)/shard_map/ppermute | solution.py:474
  203.4 24.8 %collective-permute-start.25 = (bf16[896,512]{1,0:T(8,128)(2,1)}, bf16[896,512]{1,0:T(8,128)(2,1)}, u32[]{:S(2)}, u32[]{:S(2)}) collective-permute-start(bf16[896,512]{1,0:T(8,128)(2,1)} %for_end.4.refs_2_), channel_id=1, source_target_pairs={{4,0},{8,12},{5,1},{9,13},{6,2},{10,14},{7,3},{11,15},{20,16},{24,... | collective-permute-start | bytes 2752520 | tf_op jit(solution)/shard_map/ppermute | solution.py:477
  216.1 5.3 %copy-start.26 = (bf16[640,512]{1,0:T(8,128)(2,1)}, bf16[640,512]{1,0:T(8,128)(2,1)S(1)}, u32[]{:S(2)}) copy-start(bf16[640,512]{1,0:T(8,128)(2,1)S(1)} %collective-permute-done.22.refs_8_.refs_5_) | copy-start | bytes 1966084
  216.1 5.3 %copy-start.20 = (bf16[640,512]{1,0:T(8,128)(2,1)}, bf16[640,512]{1,0:T(8,128)(2,1)S(1)}, u32[]{:S(2)}) copy-start(bf16[640,512]{1,0:T(8,128)(2,1)S(1)} %collective-permute-done.23.refs_4_.refs_6_) | copy-start | bytes 1966084
  216.1 1.9 copy-start.17
  218.1 3.3 %copy-start.22 = (bf16[640,512]{1,0:T(8,128)(2,1)}, bf16[640,512]{1,0:T(8,128)(2,1)S(1)}, u32[]{:S(2)}) copy-start(bf16[640,512]{1,0:T(8,128)(2,1)S(1)} %collective-permute-done.24.refs_5_.refs_7_) | copy-start | bytes 1966084
  221.4 25.8 %collective-permute-start.28 = (bf16[896,512]{1,0:T(8,128)(2,1)}, bf16[896,512]{1,0:T(8,128)(2,1)}, u32[]{:S(2)}, u32[]{:S(2)}) collective-permute-start(bf16[896,512]{1,0:T(8,128)(2,1)} %for_end.5.refs_2_), channel_id=1, source_target_pairs={{4,0},{8,12},{5,1},{9,13},{6,2},{10,14},{7,3},{11,15},{20,16},{24,... | collective-permute-start | bytes 2752520 | tf_op jit(solution)/shard_map/ppermute | solution.py:477
  222.7 5.6 %copy-start.4 = (bf16[1792,640]{1,0:T(8,128)(2,1)S(1)}, bf16[1792,640]{1,0:T(8,128)(2,1)}, u32[]{:S(2)}) copy-start(bf16[1792,640]{1,0:T(8,128)(2,1)} %copy-done) | copy-start | bytes 6881284
  226.1 7.9 %copy-start.19 = (bf16[640,512]{1,0:T(8,128)(2,1)S(1)}, bf16[640,512]{1,0:T(8,128)(2,1)}, u32[]{:S(2)}) copy-start(bf16[640,512]{1,0:T(8,128)(2,1)} %get-tuple-element.48.refs_4_.refs_3_) | copy-start | bytes 1966084
  226.1 7.9 %copy-start.21 = (bf16[640,512]{1,0:T(8,128)(2,1)S(1)}, bf16[640,512]{1,0:T(8,128)(2,1)}, u32[]{:S(2)}) copy-start(bf16[640,512]{1,0:T(8,128)(2,1)} %copy-done.20) | copy-start | bytes 1966084
  226.1 7.9 %copy-start.23 = (bf16[640,512]{1,0:T(8,128)(2,1)S(1)}, bf16[640,512]{1,0:T(8,128)(2,1)}, u32[]{:S(2)}) copy-start(bf16[640,512]{1,0:T(8,128)(2,1)} %copy-done.22) | copy-start | bytes 1966084
  226.1 7.9 %copy-start.27 = (bf16[640,512]{1,0:T(8,128)(2,1)S(1)}, bf16[640,512]{1,0:T(8,128)(2,1)}, u32[]{:S(2)}) copy-start(bf16[640,512]{1,0:T(8,128)(2,1)} %copy-done.26) | copy-start | bytes 1966084
  226.1 23.3 %collective-permute-start.27 = (bf16[256,1536]{1,0:T(8,128)(2,1)S(1)}, bf16[256,1536]{1,0:T(8,128)(2,1)S(1)}, u32[]{:S(2)}, u32[]{:S(2)}) collective-permute-start(bf16[256,1536]{1,0:T(8,128)(2,1)S(1)} %combine.3.refs_9_), channel_id=1, source_target_pairs={{0,16},{16,0},{1,17},{17,1},{2,18},{18,2},{3,19},{19,3},{4,20},{20... | collective-permute-start | bytes 2359304 | tf_op jit(solution)/shard_map/ppermute | solution.py:474
  234.1 1.5 copy-start.13

commit v3 on v2

--- a/solution.py
+++ b/solution.py
@@ -147,6 +147,29 @@
     return jnp.concatenate([jnp.pad(p, ((0, 0), (0, wide - block))) for p in pieces], axis=1)
 
 
+def join_columns(pieces, after=()):
+    lines = pieces[0][0].shape[0]
+    total = sum(size for _, _, size in pieces)
+
+    def body(s, ins, outs):
+        at = 0
+        for ref, (_, first, size) in zip(ins, pieces):
+            outs[0][:, at : at + size] = ref[...]
+            at += size
+
+    return call(
+        body,
+        "join_columns",
+        [jnp.int32(0)],
+        [array for array, _, _ in pieces],
+        [pl.BlockSpec((lines, size), lambda j, s, c=first // size: (0, c)) for _, first, size in pieces],
+        [((lines, total), BF16)],
+        [whole((lines, total))],
+        (1,),
+        after=after,
+    )[0]
+
+
 def forward(expert, places, rows, upstream, gate_w, up_w, up_parts, first=None, after=()):
     sources = len(rows)
     lines, width = rows[0].shape
@@ -220,7 +243,7 @@
         (hidden // step,),
         scratch=[pltpu.VMEM((count, width), BF16)],
         after=after,
-        vmem=56,
+        vmem=60,
     )
 
 
@@ -292,7 +315,7 @@
         out_specs,
         (steps,),
         after=after,
-        vmem=56,
+        vmem=60,
     )
     return out[0] if near is None else out
 
@@ -365,7 +388,7 @@
     )[0]
 
 
-def products(terms, block, part, dtype, name, extras=(), total=None, after=()):
+def products(terms, block, part, dtype, name, extras=(), total=None, after=(), vmem=28):
     slots = terms[0][0].shape[1]
     split = 2 if block % 32 == 0 else 1
     lines = block // split
@@ -403,6 +426,7 @@
         [pl.BlockSpec((lines, part), lambda j, s: (j, 0))],
         (split,),
         after=after,
+        vmem=vmem,
     )[0]
 
 
@@ -494,13 +518,10 @@
     far = []
     for value in far_even:
         far += [value, swap(tied(value, *epoch))]
-    end_columns = tied(others[order[0]], far[-1])
-    end_columns = jnp.concatenate(
-        [end_columns[:, wide:]] + [others[k][:, wide:] for k in range(1, len(sets)) if k != order[0]], axis=1
-    )
+    end_columns = join_columns([(others[k], wide, wide) for k in range(1, len(sets))], after=epoch)
     end_far = [shift(end_columns, by) for by in chips]
     far_gate, *ups = forward(
-        expert, places, far, upstream, gate_w, up_w, up_parts, first=near_up, after=[near_back]
+        expert, places, far, upstream, gate_w, up_w, up_parts, first=near_up, after=[end_columns]
     )
     own_columns = [own, partner] + far
     own_lines = own_columns
@@ -510,19 +531,18 @@
     own_picked = pick_rows(
         expert, own_blocks, own_columns, capacity, wide, routes=own_lines, after=[far_gate]
     )
-    epoch = [near_sent[k] for k in order] + [own_picked]
+    own_part = join_columns([(others[k], 0, wide) for k in range(len(sets))], after=[own_picked])
+    epoch = [near_sent[k] for k in order] + [own_part]
 
     far_sent = {k: over_groups(tied(far_gate, *epoch), sets[k]) for k in order}
     first_back, second_back = slot_gradients(
-        places, far_gate, ups, gate_w, up_w, near=near_back, after=[own_picked]
+        places, far_gate, ups, gate_w, up_w, near=near_back, after=epoch
     )
     first_back = to_sources(first_back)
     end_rows = []
     for value in [end_columns] + end_far:
         end_rows += [value, swap(tied(value, *epoch))]
-    own_part = tied(others[0], *end_far)
-    own_part = jnp.concatenate([own_part] + [others[k][:, :wide] for k in range(1, len(sets))], axis=1)
-    column_far = [shift(own_part, by) for by in chips]
+    column_far = [shift(tied(own_part, *epoch), by) for by in chips]
     end_picked = pick_rows(
         expert, [jnp.int32(k) for k in range(len(sets) - 1)], end_rows, capacity, wide, after=[second_back]
     )
@@ -541,13 +561,13 @@
         part = up_parts[c - 1] if c else hidden
         terms = [(own_picked, 1, parts[0])]
         terms += [(end_picked, k - 1, parts[1 + k]) for k in range(1, len(sets))]
-        return products(terms, wide, part, BF16, "for_end", after=after)
+        return products(terms, wide, part, BF16, "for_end", after=after, vmem=60 if c else 28)
 
     def for_own(c, part, dtype, after, extras=(), total=None):
         parts = parts_of(c)
         terms = [(own_picked, 0, parts[0])]
         terms += [(picked, k, parts[1 + k]) for k in range(len(sets))]
-        return products(terms, wide, part, dtype, "for_own", extras=extras, total=total, after=after)
+        return products(terms, wide, part, dtype, "for_own", extras=extras, total=total, after=after, vmem=60 if c == 0 else 28)
 
     up_sent = []
 
@@ -559,7 +579,7 @@
     column_rows = []
     for value in [own_part] + column_far:
         column_rows += [value, swap(tied(value, *epoch))]
-    end0 = for_end(0, [end_picked])
+    end0 = for_end(0, epoch)
     extra0 = to_ends(end0)
     picked = pick_rows(
         expert, [jnp.int32(k) for k in range(len(sets))], column_rows, capacity, wide, after=[end0]
@@ -568,7 +588,7 @@
 
     arriving = send_up(1)
     second_back = to_sources(tied(second_back, *epoch))
-    end1 = for_end(1, [picked])
+    end1 = for_end(1, epoch)
     extra1 = to_ends(end1)
     first_tok = combine(pair, first_back, experts, after=[end1])
     first_passed = passed_on(first_tok)

time: 254 us -> 249 us (0.980)
  waiting for transfers between devices: 34.2 us -> 18.8 us
  Pallas kernels: 117 us -> 128 us
  local copies, waits for them, and re-layouts: 16.3 us -> 21.3 us
  other arithmetic: 7.89 us -> 4.61 us
    pallas_call x17 -> x19, Pallas kernels: 117 us -> 128 us  [call(): pl.pallas_call(kernel, name=name, out_shape=[jax.ShapeDtypeStruct(shape,...]
    unnamed x66 -> x64, local copies, waits for them, and re-layouts: 11.7 us -> 21.2 us
    ppermute x3, waiting for transfers between devices: 9.76 us -> 3.02 us  [to_ends(): return lax.ppermute(value, 'dp', [(1, 0), (groups - 2, groups - 1)])]
    ppermute x15, waiting for transfers between devices: 17.3 us -> 11 us  [over_groups(): return lax.ppermute(value, 'dp', pairs)]
    slice x3 -> x0, local copies, waits for them, and re-layouts: 4.5 us -> none  [the longest x2 3.1 us: shards(): others[k][:, :wide]]
    concatenate x2 -> x0, other arithmetic: 3.26 us -> none  [the longest x1 2.24 us: shards(): jnp.concatenate([own_part] + [others[k][:, :wide] for k in range(1, len(s...]
  transfers between devices with their start and end apart: 31 -> 31, of which waited for: 8 -> 7; matrix products, arithmetic and copies ran while one was open for 3% -> 1% of each run, Pallas kernels for 45% -> 50%
where the time goes in v3:
time: 249 us; the launch traced here: 247 us
  Pallas kernels  128 us (51%)
  starting transfers between devices  74.1 us (30%)
  local copies, waits for them, and re-layouts  21.3 us (9%)
  waiting for transfers between devices  18.8 us (8%)
  other arithmetic  4.61 us (2%)
    pallas_call x19, Pallas kernels, call(): pl.pallas_call(kernel, name=name, out_shape=[jax.ShapeDtypeStruct(shape,...  128 us
    ppermute x15, starting transfers between devices, over_groups(): return lax.ppermute(value, 'dp', pairs)  50.4 us
    unnamed x64, local copies, waits for them, and re-layouts  21.2 us
    ppermute x15, waiting for transfers between devices, over_groups(): return lax.ppermute(value, 'dp', pairs)  11 us
    all_to_all x2, starting transfers between devices, to_sources(): lax.all_to_all(value.reshape(experts, capacity, value.shape[1]), 'expert'...  9.1 us
    ppermute x3, starting transfers between devices, shift(): lax.ppermute(value, 'expert', [(s, (s + 2 * by) % experts) for s in range...  5.78 us
  transfers between devices with their start and end apart: 31, of which 7 were waited for; matrix products, arithmetic and copies ran while one was open for 1% of the time, Pallas kernels for 50%

profile of v3, /device:TPU:0, one launch (start us, length us, event | category | flops | bytes accessed | tf_op | source)
XLA Modules:
  0.0 247.3 jit_solution(13401629841166432750)
XLA Ops:
  0.8 1.5 copy-done.8
  2.9 3.6 %cut_columns.1 = (bf16[272,3584]{1,0:T(8,128)(2,1)}, bf16[272,896]{1,0:T(8,128)(2,1)}, bf16[272,1792]{1,0:T(8,128)(2,1)}, bf16[272,1792]{1,0:T(8,128)(2,1)}) custom-call(s32[5]{0:T(128)S(1)} %stack.82.scalar_ref, s32[2,256]{1,0:T(2,128)S(1)} %bitcast.32, bf16[256,3584]{1,0:T(8,128)(2,1)S(1)} %bitcast.27, bf16[256,3584]{1,0:T(8,128)(2,1)S(1)} %bitcast.28, ...), custom_call_target="tpu_custom_call" | custom-call | flops 1 | bytes 1 | tf_op jit(solution)/shard_map/cut_columns/pallas_call | solution.py:48
  7.0 2.5 %collective-permute-start = (bf16[272,3584]{1,0:T(8,128)(2,1)}, bf16[272,3584]{1,0:T(8,128)(2,1)S(1)}, u32[]{:S(2)}, u32[]{:S(2)}) collective-permute-start(bf16[272,3584]{1,0:T(8,128)(2,1)} %get-tuple-element.26.refs_0_.refs_4_), channel_id=1, source_target_pairs={{0,2},{1,3},{2,0},{3,1},{4,6},{5,7},{6,4},{7,5},{8,10},{9,11},{10,... | collective-permute-start | bytes 5849096 | tf_op jit(solution)/shard_map/ppermute | solution.py:486
  9.5 1.6 collective-permute-start.1
  11.2 6.2 %collective-permute-start.2 = (bf16[272,1792]{1,0:T(8,128)(2,1)}, bf16[272,1792]{1,0:T(8,128)(2,1)}, u32[]{:S(2)}, u32[]{:S(2)}) collective-permute-start(bf16[272,1792]{1,0:T(8,128)(2,1)} %get-tuple-element.28), channel_id=1, source_target_pairs={{0,8},{12,4},{1,9},{13,5},{2,10},{14,6},{3,11},{15,7},{16,24},{28,... | collective-permute-start | bytes 2924552 | tf_op jit(solution)/shard_map/ppermute | solution.py:489
  17.4 1.3 collective-permute-start.3
  20.0 13.2 %forward_first.1 = (bf16[320,1024]{1,0:T(8,128)(2,1)}, bf16[320,1024]{1,0:T(8,128)(2,1)}) custom-call(s32[3]{0:T(128)} %pad_add_fusion.2.scalar_ref, bf16[272,3584]{1,0:T(8,128)(2,1)} %get-tuple-element.26.refs_0_.refs_4_, bf16[272,3584]{1,0:T(8,128)(2,1)} %collective-permute-done.4.refs_1_.refs_5_, bf16[640,1024]{1,0:T(8,128)(2,1)} %bitcast.44, ...), custom_call_target="tpu_custom_call" | custom-call | flops 1 | bytes 1 | tf_op jit(solution)/shard_map/forward_first/pallas_call | solution.py:48
  33.1 12.5 %near_gradients.1.refs_6_.refs_5_ = bf16[320,3584]{1,0:T(8,128)(2,1)} custom-call(s32[4]{0:T(128)} %pad_add_fusion.scalar_ref, bf16[3584,1024]{1,0:T(8,128)(2,1)} %bitcast.36, bf16[3584,1024]{1,0:T(8,128)(2,1)} %bitcast.40, bf16[320,1024]{1,0:T(8,128)(2,1)} %get-tuple-element.36.refs_2_.refs_4_.refs_3_, bf16[320,1024]{1,0:T(8,128)(2,1)} %get-tuple-element.31.refs_3_.refs_5_, ...), custom_call_target="tpu_custom_call" | custom-call | flops 1 | bytes 1 | tf_op jit(solution)/shard_map/near_gradients/pallas_call | solution.py:48
  45.6 2.5 %collective-permute-done.3.refs_4_.refs_0_ = bf16[272,896]{1,0:T(8,128)(2,1)S(1)} collective-permute-done((bf16[272,896]{1,0:T(8,128)(2,1)}, bf16[272,896]{1,0:T(8,128)(2,1)S(1)}, u32[]{:S(2)}, u32[]{:S(2)}) %collective-permute-start.3) | collective-permute-done | bytes 487456 | tf_op jit(solution)/shard_map/ppermute | solution.py:489
  48.1 4.7 %collective-permute-done.refs_5_.refs_0_.refs_2_.refs_6_ = bf16[272,3584]{1,0:T(8,128)(2,1)S(1)} collective-permute-done((bf16[272,3584]{1,0:T(8,128)(2,1)}, bf16[272,3584]{1,0:T(8,128)(2,1)S(1)}, u32[]{:S(2)}, u32[]{:S(2)}) %collective-permute-start) | collective-permute-done | bytes 1949728 | tf_op jit(solution)/shard_map/ppermute | solution.py:486
  52.9 2.4 copy-done.9
  55.2 2.2 join_columns.2.refs_6_.refs_0_
  57.4 1.7 collective-permute-start.10
  59.2 1.5 collective-permute-start.6
  60.7 8.4 %collective-permute-start.7 = (bf16[320,1024]{1,0:T(8,128)(2,1)S(1)}, bf16[320,1024]{1,0:T(8,128)(2,1)}, u32[]{:S(2)}, u32[]{:S(2)}) collective-permute-start(bf16[320,1024]{1,0:T(8,128)(2,1)S(1)} %copy-done.11), channel_id=1, source_target_pairs={{0,8},{12,4},{1,9},{13,5},{2,10},{14,6},{3,11},{15,7},{16,24},{28,... | collective-permute-start | bytes 1966088 | tf_op jit(solution)/shard_map/ppermute | solution.py:489
  69.1 2.1 collective-permute-start.8
  71.9 13.5 %forward_rest.1 = (bf16[320,1024]{1,0:T(8,128)(2,1)}, bf16[640,512]{1,0:T(8,128)(2,1)}, bf16[640,512]{1,0:T(8,128)(2,1)}) custom-call(s32[3]{0:T(128)} %pad_add_fusion.1.scalar_ref, bf16[272,3584]{1,0:T(8,128)(2,1)} %copy-done.6, bf16[272,3584]{1,0:T(8,128)(2,1)} %collective-permute-done.5.refs_1_.refs_3_.refs_7_, bf16[640,1024]{1,0:T(8,128)(2,1)} %bitcast.45, ...), custom_call_target="tpu_custom_call" | custom-call | flops 1 | bytes 1 | tf_op jit(solution)/shard_map/forward_rest/pallas_call | solution.py:48
  85.4 1.5 copy-done.7
  87.0 4.3 %pick_rows.3.refs_3_.refs_0_ = bf16[1792,640]{1,0:T(8,128)(2,1)S(1)} custom-call(s32[3]{0:T(128)S(1)} %pad_add_fusion.3.scalar_ref, bf16[272,3584]{1,0:T(8,128)(2,1)} %get-tuple-element.26.refs_0_.refs_4_, bf16[272,3584]{1,0:T(8,128)(2,1)} %collective-permute-done.4.refs_1_.refs_5_, bf16[272,3584]{1,0:T(8,128)(2,1)S(1)} %copy-done.7, ...), custom_call_target="tpu_custom_call" | custom-call | flops 1 | bytes 1 | tf_op jit(solution)/shard_map/pick_rows/pallas_call | solution.py:48
  91.3 3.1 %join_columns.3.refs_9_.refs_0_ = bf16[272,2688]{1,0:T(8,128)(2,1)} custom-call(s32[1]{0:T(128)} %constant.31.clone.1.scalar_ref, bf16[272,896]{1,0:T(8,128)(2,1)S(1)} %collective-permute-done.3.refs_4_.refs_0_, bf16[272,1792]{1,0:T(8,128)(2,1)} %collective-permute-done.1.refs_0_.refs_2_.refs_1_, ...), custom_call_target="tpu_custom_call" | custom-call | flops 1 | bytes 1 | tf_op jit(solution)/shard_map/join_columns/pallas_call | solution.py:48
  94.4 1.4 collective-permute-done.8.refs_8_.refs_6_
  96.3 1.5 collective-permute-start.19
  97.8 1.6 collective-permute-start.12
  99.4 7.1 %collective-permute-start.13 = (bf16[320,1024]{1,0:T(8,128)(2,1)}, bf16[320,1024]{1,0:T(8,128)(2,1)}, u32[]{:S(2)}, u32[]{:S(2)}) collective-permute-start(bf16[320,1024]{1,0:T(8,128)(2,1)} %get-tuple-element.41.refs_8_.refs_2_.refs_4_.refs_5_), channel_id=1, source_target_pairs={{0,8},{12,4},{1,9},{13,5},{2,10},{14,6},{3,11},{15,7},{16,24},{28,... | collective-permute-start | bytes 1966088 | tf_op jit(solution)/shard_map/ppermute | solution.py:489
  106.5 0.9 copy-done.28
  107.5 1.3 collective-permute-start.14
  108.8 13.8 %slot_gradients.1 = (bf16[640,2048]{1,0:T(8,128)(2,1)}, bf16[640,1536]{1,0:T(8,128)(2,1)}) custom-call(s32[4]{0:T(128)} %pad_add_fusion.scalar_ref, bf16[3584,1024]{1,0:T(8,128)(2,1)} %bitcast.38, bf16[3584,1024]{1,0:T(8,128)(2,1)} %bitcast.42, bf16[320,1024]{1,0:T(8,128)(2,1)} %get-tuple-element.41.refs_8_.refs_2_.refs_4_.refs_5_, ...), custom_call_target="tpu_custom_call" | custom-call | flops 1 | bytes 1 | tf_op jit(solution)/shard_map/slot_gradients/pallas_call | solution.py:48
  122.6 4.5 %all-to-all-start = ((bf16[4,160,2048]{2,1,0:T(8,128)(2,1)}), bf16[4,160,2048]{2,1,0:T(8,128)(2,1)}, u32[]{:S(2)}, u32[]{:S(2)}) async-start(bf16[4,160,2048]{2,1,0:T(8,128)(2,1)} %bitcast.46), calls=%async_computation | async-start | bytes 5242880 | tf_op jit(solution)/shard_map/all_to_all | solution.py:492
  127.2 1.2 copy-done.29
  128.4 4.6 %pick_rows.4.refs_1_.refs_2_.refs_12_ = bf16[1792,640]{1,0:T(8,128)(2,1)S(1)} custom-call(s32[3]{0:T(128)S(1)} %pad_add_fusion.4.scalar_ref, bf16[272,1792]{1,0:T(8,128)(2,1)} %join_columns.2.refs_6_.refs_0_, bf16[272,1792]{1,0:T(8,128)(2,1)} %collective-permute-done.9.refs_1_, bf16[272,1792]{1,0:T(8,128)(2,1)} %collective-permute-done.10.refs_2_, ...), custom_call_target="tpu_custom_call" | custom-call | flops 1 | bytes 1 | tf_op jit(solution)/shard_map/pick_rows/pallas_call | solution.py:48
  134.9 7.0 %collective-permute-start.16 = (bf16[640,512]{1,0:T(8,128)(2,1)S(1)}, bf16[640,512]{1,0:T(8,128)(2,1)S(1)}, u32[]{:S(2)}, u32[]{:S(2)}) collective-permute-start(bf16[640,512]{1,0:T(8,128)(2,1)S(1)} %copy-done.12), channel_id=1, source_target_pairs={{0,8},{12,4},{1,9},{13,5},{2,10},{14,6},{3,11},{15,7},{16,24},{28,... | collective-permute-start | bytes 1966088 | tf_op jit(solution)/shard_map/ppermute | solution.py:489
  141.9 2.2 collective-permute-start.17
  144.1 8.9 %for_end.3.refs_4_ = bf16[896,1024]{1,0:T(8,128)(2,1)} custom-call(s32[1]{0:T(128)} %constant.31.clone.1.scalar_ref, bf16[1792,640]{1,0:T(8,128)(2,1)S(1)} %copy-done.4, bf16[1792,640]{1,0:T(8,128)(2,1)S(1)} %pick_rows.4.refs_1_.refs_2_.refs_12_, bf16[1792,640]{1,0:T(8,128)(2,1)S(1)} %pick_rows.4.refs_1_.refs_2_.refs_12_, bf16[320,1024]{1,0:T(8,128)(2,1)S(1)} %copy-done.11, ...), custom_call_target="tpu_custom_call" | custom-call | flops 1 | bytes 1 | tf_op jit(solution)/shard_map/for_end/pallas_call | solution.py:48
  153.0 1.5 collective-permute-start.26
  154.6 5.3 %pick_rows.5.refs_9_.refs_1_.refs_2_.refs_3_ = bf16[2688,640]{1,0:T(8,128)(2,1)S(1)} custom-call(s32[4]{0:T(128)S(1)} %pad_add_fusion.5.scalar_ref, bf16[272,2688]{1,0:T(8,128)(2,1)} %join_columns.3.refs_9_.refs_0_, bf16[272,2688]{1,0:T(8,128)(2,1)S(1)} %collective-permute-done.18.refs_1_, bf16[272,2688]{1,0:T(8,128)(2,1)S(1)} %collective-permute-done.19.refs_2_, ...), custom_call_target="tpu_custom_call" | custom-call | flops 1 | bytes 1 | tf_op jit(solution)/shard_map/pick_rows/pallas_call | solution.py:48
  159.9 1.7 copy-done
  161.6 0.8 copy-done.14
  162.5 0.9 copy-done.16
  163.4 6.5 %collective-permute-done.17.refs_8_.refs_5_ = bf16[640,512]{1,0:T(8,128)(2,1)} collective-permute-done((bf16[640,512]{1,0:T(8,128)(2,1)S(1)}, bf16[640,512]{1,0:T(8,128)(2,1)}, u32[]{:S(2)}, u32[]{:S(2)}) %collective-permute-start.17) | collective-permute-done | bytes 655392 | tf_op jit(solution)/shard_map/ppermute | solution.py:489
  169.9 4.6 %all-to-all-start.1 = ((bf16[4,160,1536]{2,1,0:T(8,128)(2,1)}), bf16[4,160,1536]{2,1,0:T(8,128)(2,1)}, u32[]{:S(2)}, u32[]{:S(2)}) async-start(bf16[4,160,1536]{2,1,0:T(8,128)(2,1)} %bitcast.21), calls=%async_computation.1 | async-start | bytes 3932160 | tf_op jit(solution)/shard_map/all_to_all | solution.py:492
  174.5 4.5 %collective-permute-start.22 = (bf16[640,512]{1,0:T(8,128)(2,1)S(1)}, bf16[640,512]{1,0:T(8,128)(2,1)S(1)}, u32[]{:S(2)}, u32[]{:S(2)}) collective-permute-start(bf16[640,512]{1,0:T(8,128)(2,1)S(1)} %copy-done.18), channel_id=1, source_target_pairs={{0,4},{12,8},{1,5},{13,9},{2,6},{14,10},{3,7},{15,11},{16,20},{28,... | collective-permute-start | bytes 1966088 | tf_op jit(solution)/shard_map/ppermute | solution.py:489
  179.7 4.0 %collective-permute-start.24 = (bf16[640,512]{1,0:T(8,128)(2,1)S(1)}, bf16[640,512]{1,0:T(8,128)(2,1)S(1)}, u32[]{:S(2)}, u32[]{:S(2)}) collective-permute-start(bf16[640,512]{1,0:T(8,128)(2,1)S(1)} %copy-done.18), channel_id=1, source_target_pairs={{0,8},{12,4},{1,9},{13,5},{2,10},{14,6},{3,11},{15,7},{16,24},{28,... | collective-permute-start | bytes 1966088 | tf_op jit(solution)/shard_map/ppermute | solution.py:489
  183.7 5.5 %for_end.4.refs_2_ = bf16[896,512]{1,0:T(8,128)(2,1)} custom-call(s32[1]{0:T(128)} %constant.31.clone.1.scalar_ref, bf16[1792,640]{1,0:T(8,128)(2,1)} %copy-done.3, bf16[1792,640]{1,0:T(8,128)(2,1)} %copy-done.2, bf16[1792,640]{1,0:T(8,128)(2,1)} %copy-done.2, bf16[640,512]{1,0:T(8,128)(2,1)} %get-tuple-element.42.refs_3_.refs_4_, ...), custom_call_target="tpu_custom_call" | custom-call | flops 1 | bytes 1 | tf_op jit(solution)/shard_map/for_end/pallas_call | solution.py:48
  189.2 4.7 %combine.2.refs_13_ = bf16[256,2048]{1,0:T(8,128)(2,1)} custom-call(s32[1]{0:T(128)} %constant.31.clone.1.scalar_ref, s32[2,256]{1,0:T(2,128)S(1)} %bitcast.33, bf16[640,2048]{1,0:T(8,128)(2,1)} %bitcast.20.refs_10_.refs_1_, bf16[896,512]{1,0:T(8,128)(2,1)} %for_end.4.refs_2_), custom_call_target="tpu_custom_call" | custom-call | flops 1 | bytes 1 | tf_op jit(solution)/shard_map/combine/pallas_call | solution.py:48
  193.8 1.5 collective-permute-start.21
  195.3 1.4 collective-permute-done.26.refs_12_
  196.7 1.3 collective-permute-start.25
  198.0 12.9 %for_own.3.refs_9_ = bf16[896,1024]{1,0:T(8,128)(2,1)} custom-call(s32[1]{0:T(128)} %constant.31.clone.1.scalar_ref, bf16[1792,640]{1,0:T(8,128)(2,1)} %copy-done.3, bf16[2688,640]{1,0:T(8,128)(2,1)} %copy-done, bf16[2688,640]{1,0:T(8,128)(2,1)} %copy-done, bf16[2688,640]{1,0:T(8,128)(2,1)} %copy-done, ...), custom_call_target="tpu_custom_call" | custom-call | flops 1 | bytes 1 | tf_op jit(solution)/shard_map/for_own/pallas_call | solution.py:48
  211.9 0.8 copy-done.22
  212.8 5.5 %for_end.5.refs_2_ = bf16[896,512]{1,0:T(8,128)(2,1)} custom-call(s32[1]{0:T(128)} %constant.31.clone.1.scalar_ref, bf16[1792,640]{1,0:T(8,128)(2,1)} %copy-done.3, bf16[1792,640]{1,0:T(8,128)(2,1)} %copy-done.2, bf16[1792,640]{1,0:T(8,128)(2,1)} %copy-done.2, bf16[640,512]{1,0:T(8,128)(2,1)} %get-tuple-element.46.refs_4_.refs_3_, ...), custom_call_target="tpu_custom_call" | custom-call | flops 1 | bytes 1 | tf_op jit(solution)/shard_map/for_end/pallas_call | solution.py:48
  218.3 1.5 collective-permute-start.28
  219.8 1.2 copy-done.24
  221.0 3.2 %combine.3.refs_9_ = bf16[256,1536]{1,0:T(8,128)(2,1)S(1)} custom-call(s32[1]{0:T(128)} %constant.31.clone.1.scalar_ref, s32[2,256]{1,0:T(2,128)S(1)} %bitcast.34, bf16[640,1536]{1,0:T(8,128)(2,1)} %bitcast.22.refs_1_, bf16[896,512]{1,0:T(8,128)(2,1)S(1)} %copy-done.24), custom_call_target="tpu_custom_call" | custom-call | flops 1 | bytes 1 | tf_op jit(solution)/shard_map/combine/pallas_call | solution.py:48
  224.3 1.5 collective-permute-start.27
  225.8 1.6 copy-done.5
  227.5 1.1 copy-done.13
  228.6 1.1 copy-done.15
  229.7 1.1 copy-done.17
  230.8 5.4 %for_own.4.refs_8_.refs_2_ = bf16[896,1024]{1,0:T(8,128)(2,1)} custom-call(s32[1]{0:T(128)} %constant.31.clone.1.scalar_ref, bf16[1792,640]{1,0:T(8,128)(2,1)S(1)} %copy-done.5, bf16[2688,640]{1,0:T(8,128)(2,1)S(1)} %copy-done.1, bf16[2688,640]{1,0:T(8,128)(2,1)S(1)} %copy-done.1, bf16[2688,640]{1,0:T(8,128)(2,1)S(1)} %copy-done.1, ...), custom_call_target="tpu_custom_call" | custom-call | flops 1 | bytes 1 | tf_op jit(solution)/shard_map/for_own/pallas_call | solution.py:48
  236.1 1.5 copy-done.10
  237.6 3.2 %for_own.5.refs_0_ = f32[896,512]{1,0:T(8,128)S(1)} custom-call(s32[1]{0:T(128)} %constant.31.clone.1.scalar_ref, bf16[1792,640]{1,0:T(8,128)(2,1)S(1)} %copy-done.5, bf16[2688,640]{1,0:T(8,128)(2,1)S(1)} %copy-done.1, bf16[2688,640]{1,0:T(8,128)(2,1)S(1)} %copy-done.1, bf16[2688,640]{1,0:T(8,128)(2,1)S(1)} %copy-done.1, bf16[640,512]{1,0:T(8,128)(2,1)S(1)} %copy-done.19, ...), custom_call_target="tpu_custom_call" | custom-call | flops 1 | bytes 1 | tf_op jit(solution)/shard_map/for_own/pallas_call | solution.py:48
  240.8 1.7 collective-permute-done.28.refs_1_
  242.5 2.3 finish.1
  244.8 2.6 %maximum_bitcast_fusion = bf16[1,256,3584]{2,1,0:T(8,128)(2,1)} fusion(bf16[256,1536]{1,0:T(8,128)(2,1)S(1)} %collective-permute-done.27, bf16[256,2048]{1,0:T(8,128)(2,1)} %collective-permute-done.21), kind=kLoop, calls=%fused_computation | loop fusion | flops 3670016 | bytes 3670016 | tf_op jit(solution)/shard_map/broadcast_in_dim | solution.py:606
  (89 shorter events, 7.5 us)
Async XLA Ops:
  0.7 1.5 copy-start.8
  2.2 0.7 copy-start.30
  6.5 13.4 %collective-permute-start.4 = (bf16[272,3584]{1,0:T(8,128)(2,1)}, bf16[272,3584]{1,0:T(8,128)(2,1)}, u32[]{:S(2)}, u32[]{:S(2)}) collective-permute-start(bf16[272,3584]{1,0:T(8,128)(2,1)} %get-tuple-element.26.refs_0_.refs_4_), channel_id=1, source_target_pairs={{0,1},{1,0},{2,3},{3,2},{4,5},{5,4},{6,7},{7,6},{8,9},{9,8},{10,11... | collective-permute-start | bytes 5849096 | tf_op jit(solution)/shard_map/ppermute | solution.py:483
  7.0 45.9 %collective-permute-start = (bf16[272,3584]{1,0:T(8,128)(2,1)}, bf16[272,3584]{1,0:T(8,128)(2,1)S(1)}, u32[]{:S(2)}, u32[]{:S(2)}) collective-permute-start(bf16[272,3584]{1,0:T(8,128)(2,1)} %get-tuple-element.26.refs_0_.refs_4_), channel_id=1, source_target_pairs={{0,2},{1,3},{2,0},{3,1},{4,6},{5,7},{6,4},{7,5},{8,10},{9,11},{10,... | collective-permute-start | bytes 5849096 | tf_op jit(solution)/shard_map/ppermute | solution.py:486
  9.5 38.6 %collective-permute-start.1 = (bf16[272,1792]{1,0:T(8,128)(2,1)}, bf16[272,1792]{1,0:T(8,128)(2,1)}, u32[]{:S(2)}, u32[]{:S(2)}) collective-permute-start(bf16[272,1792]{1,0:T(8,128)(2,1)} %get-tuple-element.27), channel_id=1, source_target_pairs={{4,8},{8,4},{5,9},{9,5},{6,10},{10,6},{7,11},{11,7},{20,24},{24,20... | collective-permute-start | bytes 2924552 | tf_op jit(solution)/shard_map/ppermute | solution.py:489
  11.2 37.0 %collective-permute-start.2 = (bf16[272,1792]{1,0:T(8,128)(2,1)}, bf16[272,1792]{1,0:T(8,128)(2,1)}, u32[]{:S(2)}, u32[]{:S(2)}) collective-permute-start(bf16[272,1792]{1,0:T(8,128)(2,1)} %get-tuple-element.28), channel_id=1, source_target_pairs={{0,8},{12,4},{1,9},{13,5},{2,10},{14,6},{3,11},{15,7},{16,24},{28,... | collective-permute-start | bytes 2924552 | tf_op jit(solution)/shard_map/ppermute | solution.py:489
  17.4 30.7 %collective-permute-start.3 = (bf16[272,896]{1,0:T(8,128)(2,1)}, bf16[272,896]{1,0:T(8,128)(2,1)S(1)}, u32[]{:S(2)}, u32[]{:S(2)}) collective-permute-start(bf16[272,896]{1,0:T(8,128)(2,1)} %get-tuple-element.29), channel_id=1, source_target_pairs={{0,4},{12,8},{1,5},{13,9},{2,6},{14,10},{3,7},{15,11},{16,20},{28,... | collective-permute-start | bytes 1462280 | tf_op jit(solution)/shard_map/ppermute | solution.py:489
  33.1 26.0 %copy-start.11 = (bf16[320,1024]{1,0:T(8,128)(2,1)S(1)}, bf16[320,1024]{1,0:T(8,128)(2,1)}, u32[]{:S(2)}) copy-start(bf16[320,1024]{1,0:T(8,128)(2,1)} %get-tuple-element.36.refs_2_.refs_4_.refs_3_) | copy-start | bytes 1966084
  52.9 19.1 %copy-start.6 = (bf16[272,3584]{1,0:T(8,128)(2,1)}, bf16[272,3584]{1,0:T(8,128)(2,1)S(1)}, u32[]{:S(2)}) copy-start(bf16[272,3584]{1,0:T(8,128)(2,1)S(1)} %collective-permute-done.refs_5_.refs_0_.refs_2_.refs_6_) | copy-start | bytes 5849092
  52.9 19.1 %collective-permute-start.5 = (bf16[272,3584]{1,0:T(8,128)(2,1)S(1)}, bf16[272,3584]{1,0:T(8,128)(2,1)}, u32[]{:S(2)}, u32[]{:S(2)}) collective-permute-start(bf16[272,3584]{1,0:T(8,128)(2,1)S(1)} %collective-permute-done.refs_5_.refs_0_.refs_2_.refs_6_), channel_id=1, source_target_pairs={{0,1},{1,0},{2,3},{3,2},{4,5},{5,4},{6,7},{7,6},{8,9},{9,8},{10,11... | collective-permute-start | bytes 5849096 | tf_op jit(solution)/shard_map/ppermute | solution.py:483
  52.9 2.4 copy-start.9
  57.4 38.4 %collective-permute-start.10 = (bf16[272,1792]{1,0:T(8,128)(2,1)}, bf16[272,1792]{1,0:T(8,128)(2,1)}, u32[]{:S(2)}, u32[]{:S(2)}) collective-permute-start(bf16[272,1792]{1,0:T(8,128)(2,1)} %join_columns.2.refs_6_.refs_0_), channel_id=1, source_target_pairs={{0,2},{1,3},{2,0},{3,1},{4,6},{5,7},{6,4},{7,5},{8,10},{9,11},{10,... | collective-permute-start | bytes 2924552 | tf_op jit(solution)/shard_map/ppermute | solution.py:486
  59.2 35.3 %collective-permute-start.6 = (bf16[320,1024]{1,0:T(8,128)(2,1)S(1)}, bf16[320,1024]{1,0:T(8,128)(2,1)}, u32[]{:S(2)}, u32[]{:S(2)}) collective-permute-start(bf16[320,1024]{1,0:T(8,128)(2,1)S(1)} %copy-done.11), channel_id=1, source_target_pairs={{4,8},{8,4},{5,9},{9,5},{6,10},{10,6},{7,11},{11,7},{20,24},{24,20... | collective-permute-start | bytes 1966088 | tf_op jit(solution)/shard_map/ppermute | solution.py:489
  60.7 33.7 %collective-permute-start.7 = (bf16[320,1024]{1,0:T(8,128)(2,1)S(1)}, bf16[320,1024]{1,0:T(8,128)(2,1)}, u32[]{:S(2)}, u32[]{:S(2)}) collective-permute-start(bf16[320,1024]{1,0:T(8,128)(2,1)S(1)} %copy-done.11), channel_id=1, source_target_pairs={{0,8},{12,4},{1,9},{13,5},{2,10},{14,6},{3,11},{15,7},{16,24},{28,... | collective-permute-start | bytes 1966088 | tf_op jit(solution)/shard_map/ppermute | solution.py:489
  69.1 26.7 %collective-permute-start.8 = (bf16[320,1024]{1,0:T(8,128)(2,1)S(1)}, bf16[320,1024]{1,0:T(8,128)(2,1)}, u32[]{:S(2)}, u32[]{:S(2)}) collective-permute-start(bf16[320,1024]{1,0:T(8,128)(2,1)S(1)} %copy-done.11), channel_id=1, source_target_pairs={{0,4},{12,8},{1,5},{13,9},{2,6},{14,10},{3,7},{15,11},{16,20},{28,... | collective-permute-start | bytes 1966088 | tf_op jit(solution)/shard_map/ppermute | solution.py:489
  85.4 1.5 copy-start.7
  91.3 3.1 %copy-start.3 = (bf16[1792,640]{1,0:T(8,128)(2,1)}, bf16[1792,640]{1,0:T(8,128)(2,1)S(1)}, u32[]{:S(2)}) copy-start(bf16[1792,640]{1,0:T(8,128)(2,1)S(1)} %pick_rows.3.refs_3_.refs_0_) | copy-start | bytes 6881284
  95.8 10.7 %collective-permute-start.11 = (bf16[272,1792]{1,0:T(8,128)(2,1)}, bf16[272,1792]{1,0:T(8,128)(2,1)S(1)}, u32[]{:S(2)}, u32[]{:S(2)}) collective-permute-start(bf16[272,1792]{1,0:T(8,128)(2,1)} %collective-permute-done.10.refs_2_), channel_id=1, source_target_pairs={{0,1},{1,0},{2,3},{3,2},{4,5},{5,4},{6,7},{7,6},{8,9},{9,8},{10,11... | collective-permute-start | bytes 2924552 | tf_op jit(solution)/shard_map/ppermute | solution.py:483
  95.8 31.4 %collective-permute-start.9 = (bf16[272,1792]{1,0:T(8,128)(2,1)}, bf16[272,1792]{1,0:T(8,128)(2,1)}, u32[]{:S(2)}, u32[]{:S(2)}) collective-permute-start(bf16[272,1792]{1,0:T(8,128)(2,1)} %join_columns.2.refs_6_.refs_0_), channel_id=1, source_target_pairs={{0,1},{1,0},{2,3},{3,2},{4,5},{5,4},{6,7},{7,6},{8,9},{9,8},{10,11... | collective-permute-start | bytes 2924552 | tf_op jit(solution)/shard_map/ppermute | solution.py:483
  96.3 37.4 %collective-permute-start.19 = (bf16[272,2688]{1,0:T(8,128)(2,1)}, bf16[272,2688]{1,0:T(8,128)(2,1)S(1)}, u32[]{:S(2)}, u32[]{:S(2)}) collective-permute-start(bf16[272,2688]{1,0:T(8,128)(2,1)} %join_columns.3.refs_9_.refs_0_), channel_id=1, source_target_pairs={{0,2},{1,3},{2,0},{3,1},{4,6},{5,7},{6,4},{7,5},{8,10},{9,11},{10,... | collective-permute-start | bytes 4386824 | tf_op jit(solution)/shard_map/ppermute | solution.py:486
  97.8 35.2 %collective-permute-start.12 = (bf16[320,1024]{1,0:T(8,128)(2,1)}, bf16[320,1024]{1,0:T(8,128)(2,1)}, u32[]{:S(2)}, u32[]{:S(2)}) collective-permute-start(bf16[320,1024]{1,0:T(8,128)(2,1)} %get-tuple-element.41.refs_8_.refs_2_.refs_4_.refs_5_), channel_id=1, source_target_pairs={{4,8},{8,4},{5,9},{9,5},{6,10},{10,6},{7,11},{11,7},{20,24},{24,20... | collective-permute-start | bytes 1966088 | tf_op jit(solution)/shard_map/ppermute | solution.py:489
  99.4 33.6 %collective-permute-start.13 = (bf16[320,1024]{1,0:T(8,128)(2,1)}, bf16[320,1024]{1,0:T(8,128)(2,1)}, u32[]{:S(2)}, u32[]{:S(2)}) collective-permute-start(bf16[320,1024]{1,0:T(8,128)(2,1)} %get-tuple-element.41.refs_8_.refs_2_.refs_4_.refs_5_), channel_id=1, source_target_pairs={{0,8},{12,4},{1,9},{13,5},{2,10},{14,6},{3,11},{15,7},{16,24},{28,... | collective-permute-start | bytes 1966088 | tf_op jit(solution)/shard_map/ppermute | solution.py:489
  106.5 0.9 copy-start.28
  107.5 26.2 %collective-permute-start.14 = (bf16[320,1024]{1,0:T(8,128)(2,1)}, bf16[320,1024]{1,0:T(8,128)(2,1)S(1)}, u32[]{:S(2)}, u32[]{:S(2)}) collective-permute-start(bf16[320,1024]{1,0:T(8,128)(2,1)} %get-tuple-element.41.refs_8_.refs_2_.refs_4_.refs_5_), channel_id=1, source_target_pairs={{0,4},{12,8},{1,5},{13,9},{2,6},{14,10},{3,7},{15,11},{16,20},{28,... | collective-permute-start | bytes 1966088 | tf_op jit(solution)/shard_map/ppermute | solution.py:489
  122.6 47.3 %all-to-all-start = ((bf16[4,160,2048]{2,1,0:T(8,128)(2,1)}), bf16[4,160,2048]{2,1,0:T(8,128)(2,1)}, u32[]{:S(2)}, u32[]{:S(2)}) async-start(bf16[4,160,2048]{2,1,0:T(8,128)(2,1)} %bitcast.46), calls=%async_computation | async-start | bytes 5242880 | tf_op jit(solution)/shard_map/all_to_all | solution.py:492
  127.2 1.2 copy-start.29
  128.4 5.8 %copy-start.12 = (bf16[640,512]{1,0:T(8,128)(2,1)S(1)}, bf16[640,512]{1,0:T(8,128)(2,1)}, u32[]{:S(2)}) copy-start(bf16[640,512]{1,0:T(8,128)(2,1)} %get-tuple-element.42.refs_3_.refs_4_) | copy-start | bytes 1966084
  128.4 15.7 %copy-start.4 = (bf16[1792,640]{1,0:T(8,128)(2,1)S(1)}, bf16[1792,640]{1,0:T(8,128)(2,1)}, u32[]{:S(2)}) copy-start(bf16[1792,640]{1,0:T(8,128)(2,1)} %copy-done.3) | copy-start | bytes 6881284
  133.0 20.1 %copy-start.2 = (bf16[1792,640]{1,0:T(8,128)(2,1)}, bf16[1792,640]{1,0:T(8,128)(2,1)S(1)}, u32[]{:S(2)}) copy-start(bf16[1792,640]{1,0:T(8,128)(2,1)S(1)} %pick_rows.4.refs_1_.refs_2_.refs_12_) | copy-start | bytes 6881284
  133.7 19.4 %copy-start.25 = (bf16[320,1024]{1,0:T(8,128)(2,1)}, bf16[320,1024]{1,0:T(8,128)(2,1)S(1)}, u32[]{:S(2)}) copy-start(bf16[320,1024]{1,0:T(8,128)(2,1)S(1)} %collective-permute-done.14.refs_11_.refs_7_) | copy-start | bytes 1966084
  133.7 19.4 %collective-permute-start.18 = (bf16[272,2688]{1,0:T(8,128)(2,1)}, bf16[272,2688]{1,0:T(8,128)(2,1)S(1)}, u32[]{:S(2)}, u32[]{:S(2)}) collective-permute-start(bf16[272,2688]{1,0:T(8,128)(2,1)} %join_columns.3.refs_9_.refs_0_), channel_id=1, source_target_pairs={{0,1},{1,0},{2,3},{3,2},{4,5},{5,4},{6,7},{7,6},{8,9},{9,8},{10,11... | collective-permute-start | bytes 4386824 | tf_op jit(solution)/shard_map/ppermute | solution.py:483
  133.7 20.9 %collective-permute-start.20 = (bf16[272,2688]{1,0:T(8,128)(2,1)S(1)}, bf16[272,2688]{1,0:T(8,128)(2,1)S(1)}, u32[]{:S(2)}, u32[]{:S(2)}) collective-permute-start(bf16[272,2688]{1,0:T(8,128)(2,1)S(1)} %collective-permute-done.19.refs_2_), channel_id=1, source_target_pairs={{0,1},{1,0},{2,3},{3,2},{4,5},{5,4},{6,7},{7,6},{8,9},{9,8},{10,11... | collective-permute-start | bytes 4386824 | tf_op jit(solution)/shard_map/ppermute | solution.py:483
  134.2 27.4 %collective-permute-start.15 = (bf16[640,512]{1,0:T(8,128)(2,1)S(1)}, bf16[640,512]{1,0:T(8,128)(2,1)S(1)}, u32[]{:S(2)}, u32[]{:S(2)}) collective-permute-start(bf16[640,512]{1,0:T(8,128)(2,1)S(1)} %copy-done.12), channel_id=1, source_target_pairs={{4,8},{8,4},{5,9},{9,5},{6,10},{10,6},{7,11},{11,7},{20,24},{24,20... | collective-permute-start | bytes 1966088 | tf_op jit(solution)/shard_map/ppermute | solution.py:489
  134.9 26.7 %collective-permute-start.16 = (bf16[640,512]{1,0:T(8,128)(2,1)S(1)}, bf16[640,512]{1,0:T(8,128)(2,1)S(1)}, u32[]{:S(2)}, u32[]{:S(2)}) collective-permute-start(bf16[640,512]{1,0:T(8,128)(2,1)S(1)} %copy-done.12), channel_id=1, source_target_pairs={{0,8},{12,4},{1,9},{13,5},{2,10},{14,6},{3,11},{15,7},{16,24},{28,... | collective-permute-start | bytes 1966088 | tf_op jit(solution)/shard_map/ppermute | solution.py:489
  141.9 28.0 %collective-permute-start.17 = (bf16[640,512]{1,0:T(8,128)(2,1)S(1)}, bf16[640,512]{1,0:T(8,128)(2,1)}, u32[]{:S(2)}, u32[]{:S(2)}) collective-permute-start(bf16[640,512]{1,0:T(8,128)(2,1)S(1)} %copy-done.12), channel_id=1, source_target_pairs={{0,4},{12,8},{1,5},{13,9},{2,6},{14,10},{3,7},{15,11},{16,20},{28,... | collective-permute-start | bytes 1966088 | tf_op jit(solution)/shard_map/ppermute | solution.py:489
  153.0 43.6 %collective-permute-start.26 = (bf16[896,1024]{1,0:T(8,128)(2,1)}, bf16[896,1024]{1,0:T(8,128)(2,1)}, u32[]{:S(2)}, u32[]{:S(2)}) collective-permute-start(bf16[896,1024]{1,0:T(8,128)(2,1)} %for_end.3.refs_4_), channel_id=1, source_target_pairs={{4,0},{8,12},{5,1},{9,13},{6,2},{10,14},{7,3},{11,15},{20,16},{24,... | collective-permute-start | bytes 5505032 | tf_op jit(solution)/shard_map/ppermute | solution.py:501
  159.9 1.7 copy-start
  161.6 0.8 copy-start.14
  162.5 0.9 copy-start.16
  169.9 4.6 %copy-start.18 = (bf16[640,512]{1,0:T(8,128)(2,1)S(1)}, bf16[640,512]{1,0:T(8,128)(2,1)}, u32[]{:S(2)}) copy-start(bf16[640,512]{1,0:T(8,128)(2,1)} %get-tuple-element.46.refs_4_.refs_3_) | copy-start | bytes 1966084
  169.9 50.0 %all-to-all-start.1 = ((bf16[4,160,1536]{2,1,0:T(8,128)(2,1)}), bf16[4,160,1536]{2,1,0:T(8,128)(2,1)}, u32[]{:S(2)}, u32[]{:S(2)}) async-start(bf16[4,160,1536]{2,1,0:T(8,128)(2,1)} %bitcast.21), calls=%async_computation.1 | async-start | bytes 3932160 | tf_op jit(solution)/shard_map/all_to_all | solution.py:492
  174.5 14.7 %copy-start.31 = (s32[1,256,2]{1,2,0:T(2,128)S(1)}, s32[1,256,2]{1,2,0:T(2,128)}, u32[]{:S(2)}) copy-start(s32[1,256,2]{1,2,0:T(2,128)} %param.6) | copy-start | bytes 6148
  174.5 36.4 %collective-permute-start.22 = (bf16[640,512]{1,0:T(8,128)(2,1)S(1)}, bf16[640,512]{1,0:T(8,128)(2,1)S(1)}, u32[]{:S(2)}, u32[]{:S(2)}) collective-permute-start(bf16[640,512]{1,0:T(8,128)(2,1)S(1)} %copy-done.18), channel_id=1, source_target_pairs={{0,4},{12,8},{1,5},{13,9},{2,6},{14,10},{3,7},{15,11},{16,20},{28,... | collective-permute-start | bytes 1966088 | tf_op jit(solution)/shard_map/ppermute | solution.py:489
  179.0 31.9 %collective-permute-start.23 = (bf16[640,512]{1,0:T(8,128)(2,1)S(1)}, bf16[640,512]{1,0:T(8,128)(2,1)S(1)}, u32[]{:S(2)}, u32[]{:S(2)}) collective-permute-start(bf16[640,512]{1,0:T(8,128)(2,1)S(1)} %copy-done.18), channel_id=1, source_target_pairs={{4,8},{8,4},{5,9},{9,5},{6,10},{10,6},{7,11},{11,7},{20,24},{24,20... | collective-permute-start | bytes 1966088 | tf_op jit(solution)/shard_map/ppermute | solution.py:489
  179.7 31.2 %collective-permute-start.24 = (bf16[640,512]{1,0:T(8,128)(2,1)S(1)}, bf16[640,512]{1,0:T(8,128)(2,1)S(1)}, u32[]{:S(2)}, u32[]{:S(2)}) collective-permute-start(bf16[640,512]{1,0:T(8,128)(2,1)S(1)} %copy-done.18), channel_id=1, source_target_pairs={{0,8},{12,4},{1,9},{13,5},{2,10},{14,6},{3,11},{15,7},{16,24},{28,... | collective-permute-start | bytes 1966088 | tf_op jit(solution)/shard_map/ppermute | solution.py:489
  193.8 47.0 %collective-permute-start.21 = (bf16[256,2048]{1,0:T(8,128)(2,1)}, bf16[256,2048]{1,0:T(8,128)(2,1)}, u32[]{:S(2)}, u32[]{:S(2)}) collective-permute-start(bf16[256,2048]{1,0:T(8,128)(2,1)} %combine.2.refs_13_), channel_id=1, source_target_pairs={{0,16},{16,0},{1,17},{17,1},{2,18},{18,2},{3,19},{19,3},{4,20},{20... | collective-permute-start | bytes 3145736 | tf_op jit(solution)/shard_map/ppermute | solution.py:498
  196.7 29.1 %collective-permute-start.25 = (bf16[896,512]{1,0:T(8,128)(2,1)}, bf16[896,512]{1,0:T(8,128)(2,1)}, u32[]{:S(2)}, u32[]{:S(2)}) collective-permute-start(bf16[896,512]{1,0:T(8,128)(2,1)} %for_end.4.refs_2_), channel_id=1, source_target_pairs={{4,0},{8,12},{5,1},{9,13},{6,2},{10,14},{7,3},{11,15},{20,16},{24,... | collective-permute-start | bytes 2752520 | tf_op jit(solution)/shard_map/ppermute | solution.py:501
  210.9 0.8 copy-start.26
  210.9 1.0 copy-start.20
  211.9 0.8 copy-start.22
  218.3 7.6 %copy-start.1 = (bf16[2688,640]{1,0:T(8,128)(2,1)S(1)}, bf16[2688,640]{1,0:T(8,128)(2,1)}, u32[]{:S(2)}) copy-start(bf16[2688,640]{1,0:T(8,128)(2,1)} %copy-done) | copy-start | bytes 10321924
  218.3 24.2 %collective-permute-start.28 = (bf16[896,512]{1,0:T(8,128)(2,1)}, bf16[896,512]{1,0:T(8,128)(2,1)}, u32[]{:S(2)}, u32[]{:S(2)}) collective-permute-start(bf16[896,512]{1,0:T(8,128)(2,1)} %for_end.5.refs_2_), channel_id=1, source_target_pairs={{4,0},{8,12},{5,1},{9,13},{6,2},{10,14},{7,3},{11,15},{20,16},{24,... | collective-permute-start | bytes 2752520 | tf_op jit(solution)/shard_map/ppermute | solution.py:501
  219.8 1.2 copy-start.24
  224.3 20.5 %collective-permute-start.27 = (bf16[256,1536]{1,0:T(8,128)(2,1)S(1)}, bf16[256,1536]{1,0:T(8,128)(2,1)S(1)}, u32[]{:S(2)}, u32[]{:S(2)}) collective-permute-start(bf16[256,1536]{1,0:T(8,128)(2,1)S(1)} %combine.3.refs_9_), channel_id=1, source_target_pairs={{0,16},{16,0},{1,17},{17,1},{2,18},{18,2},{3,19},{19,3},{4,20},{20... | collective-permute-start | bytes 2359304 | tf_op jit(solution)/shard_map/ppermute | solution.py:498
  225.8 1.6 copy-start.5
  227.5 1.1 copy-start.13
  228.6 1.1 copy-start.15
  229.7 1.1 copy-start.17
  230.7 5.4 %copy-start.19 = (bf16[640,512]{1,0:T(8,128)(2,1)S(1)}, bf16[640,512]{1,0:T(8,128)(2,1)}, u32[]{:S(2)}) copy-start(bf16[640,512]{1,0:T(8,128)(2,1)} %get-tuple-element.46.refs_4_.refs_3_) | copy-start | bytes 1966084
  230.7 5.4 %copy-start.21 = (bf16[640,512]{1,0:T(8,128)(2,1)S(1)}, bf16[640,512]{1,0:T(8,128)(2,1)}, u32[]{:S(2)}) copy-start(bf16[640,512]{1,0:T(8,128)(2,1)} %copy-done.20) | copy-start | bytes 1966084
  230.7 5.4 %copy-start.23 = (bf16[640,512]{1,0:T(8,128)(2,1)S(1)}, bf16[640,512]{1,0:T(8,128)(2,1)}, u32[]{:S(2)}) copy-start(bf16[640,512]{1,0:T(8,128)(2,1)} %copy-done.22) | copy-start | bytes 1966084
  230.7 5.4 %copy-start.27 = (bf16[640,512]{1,0:T(8,128)(2,1)S(1)}, bf16[640,512]{1,0:T(8,128)(2,1)}, u32[]{:S(2)}) copy-start(bf16[640,512]{1,0:T(8,128)(2,1)} %copy-done.26) | copy-start | bytes 1966084
  236.1 1.5 copy-start.10

commit v4 on v3

--- a/solution.py
+++ b/solution.py
@@ -393,18 +393,15 @@
     split = 2 if block % 32 == 0 else 1
     lines = block // split
 
+    count = len(terms)
+    pieces = sum(len(parts) for _, _, parts in terms)
+
     def body(s, ins, outs):
-        at, result = len(terms), None
-        for k, (_, _, parts) in enumerate(terms):
-            row = 0
-            for _ in parts:
-                g = ins[at]
-                new = dot(ins[k][:, row : row + g.shape[0]] if len(parts) > 1 else ins[k][...], g[...])
-                result = new if result is None else result + new
-                row += g.shape[0]
-                at += 1
+        left = jnp.concatenate([p[...] for p in ins[:count]], axis=1)
+        right = jnp.concatenate([g[...] for g in ins[count : count + pieces]], axis=0)
+        result = dot(left, right)
         if extras:
-            result = result + jnp.concatenate([e[...].astype(F32) for e in ins[at:]], axis=1)
+            result = result + jnp.concatenate([e[...].astype(F32) for e in ins[count + pieces :]], axis=1)
         outs[0][...] = result.astype(dtype)
 
     ins = [p for p, _, _ in terms]
@@ -503,7 +500,7 @@
     chips = range(1, experts // 2)
     places = [jnp.bitwise_xor((expert - 2 * (r // 2)) % experts, r % 2) for r in range(experts)]
     targets = [target_in(pairs, group) for pairs in sets]
-    order = list(range(1, len(sets))) + [0]
+    order = list(range(2, len(sets))) + [1, 0]
 
     pair = routes[0].T
     own, *cut = cut_columns(rows, pair, group, targets, groups, block)
@@ -560,14 +557,14 @@
         parts = parts_of(c)
         part = up_parts[c - 1] if c else hidden
         terms = [(own_picked, 1, parts[0])]
-        terms += [(end_picked, k - 1, parts[1 + k]) for k in range(1, len(sets))]
-        return products(terms, wide, part, BF16, "for_end", after=after, vmem=60 if c else 28)
+        terms += [(end_picked, k - 1, parts[1 + k]) for k in reversed(range(1, len(sets)))]
+        return products(terms, wide, part, BF16, "for_end", after=after, vmem=60)
 
     def for_own(c, part, dtype, after, extras=(), total=None):
         parts = parts_of(c)
         terms = [(own_picked, 0, parts[0])]
-        terms += [(picked, k, parts[1 + k]) for k in range(len(sets))]
-        return products(terms, wide, part, dtype, "for_own", extras=extras, total=total, after=after, vmem=60 if c == 0 else 28)
+        terms += [(picked, k, parts[1 + k]) for k in reversed(range(len(sets)))]
+        return products(terms, wide, part, dtype, "for_own", extras=extras, total=total, after=after, vmem=60)
 
     up_sent = []
 

time: 249 us -> 243 us (0.976)
  Pallas kernels: 128 us -> 122 us
  waiting for transfers between devices: 18.8 us -> 23.4 us
  starting transfers between devices: 74.1 us -> 69.8 us
    pallas_call x19, Pallas kernels: 128 us -> 122 us  [call(): pl.pallas_call(kernel, name=name, out_shape=[jax.ShapeDtypeStruct(shape,...]
    ppermute x3, waiting for transfers between devices: 3.02 us -> 7.21 us  [to_ends(): return lax.ppermute(value, 'dp', [(1, 0), (groups - 2, groups - 1)])]
    ppermute x15, starting transfers between devices: 50.4 us -> 47.2 us  [over_groups(): return lax.ppermute(value, 'dp', pairs)]
    unnamed x64 -> x42, local copies, waits for them, and re-layouts: 21.2 us -> 19.5 us
  transfers between devices with their start and end apart: 31 -> 31, of which waited for: 7 -> 7; matrix products, arithmetic and copies ran while one was open for 1% -> 1% of each run, Pallas kernels for 50% -> 49%
where the time goes in v4:
time: 243 us; the launch traced here: 241 us
  Pallas kernels  122 us (50%)
  starting transfers between devices  69.8 us (29%)
  waiting for transfers between devices  23.4 us (10%)
  local copies, waits for them, and re-layouts  19.6 us (8%)
  other arithmetic  4.86 us (2%)
    pallas_call x19, Pallas kernels, call(): pl.pallas_call(kernel, name=name, out_shape=[jax.ShapeDtypeStruct(shape,...  122 us
    ppermute x15, starting transfers between devices, over_groups(): return lax.ppermute(value, 'dp', pairs)  47.2 us
    unnamed x42, local copies, waits for them, and re-layouts  19.5 us
    ppermute x15, waiting for transfers between devices, over_groups(): return lax.ppermute(value, 'dp', pairs)  9.34 us
    all_to_all x2, starting transfers between devices, to_sources(): lax.all_to_all(value.reshape(experts, capacity, value.shape[1]), 'expert'...  8.07 us
    ppermute x3, waiting for transfers between devices, to_ends(): return lax.ppermute(value, 'dp', [(1, 0), (groups - 2, groups - 1)])  7.21 us
    ppermute x3, waiting for transfers between devices, shift(): lax.ppermute(value, 'expert', [(s, (s + 2 * by) % experts) for s in range...  6.84 us
    ppermute x3, starting transfers between devices, shift(): lax.ppermute(value, 'expert', [(s, (s + 2 * by) % experts) for s in range...  5.78 us
  transfers between devices with their start and end apart: 31, of which 7 were waited for; matrix products, arithmetic and copies ran while one was open for 1% of the time, Pallas kernels for 49%

profile of v4, /device:TPU:0, one launch (start us, length us, event | category | flops | bytes accessed | tf_op | source)
XLA Modules:
  0.0 241.0 jit_solution(12422135139329939337)
XLA Ops:
  0.8 1.5 copy-done.5
  2.9 3.6 %cut_columns.1 = (bf16[272,3584]{1,0:T(8,128)(2,1)}, bf16[272,896]{1,0:T(8,128)(2,1)}, bf16[272,1792]{1,0:T(8,128)(2,1)}, bf16[272,1792]{1,0:T(8,128)(2,1)}) custom-call(s32[5]{0:T(128)S(1)} %stack.82.scalar_ref, s32[2,256]{1,0:T(2,128)S(1)} %bitcast.34, bf16[256,3584]{1,0:T(8,128)(2,1)S(1)} %bitcast.27, bf16[256,3584]{1,0:T(8,128)(2,1)S(1)} %bitcast.28, ...), custom_call_target="tpu_custom_call" | custom-call | flops 1 | bytes 1 | tf_op jit(solution)/shard_map/cut_columns/pallas_call | solution.py:48
  7.0 2.5 %collective-permute-start = (bf16[272,3584]{1,0:T(8,128)(2,1)}, bf16[272,3584]{1,0:T(8,128)(2,1)S(1)}, u32[]{:S(2)}, u32[]{:S(2)}) collective-permute-start(bf16[272,3584]{1,0:T(8,128)(2,1)} %get-tuple-element.26.refs_0_.refs_4_), channel_id=1, source_target_pairs={{0,2},{1,3},{2,0},{3,1},{4,6},{5,7},{6,4},{7,5},{8,10},{9,11},{10,... | collective-permute-start | bytes 5849096 | tf_op jit(solution)/shard_map/ppermute | solution.py:483
  9.5 4.5 %collective-permute-start.1 = (bf16[272,1792]{1,0:T(8,128)(2,1)}, bf16[272,1792]{1,0:T(8,128)(2,1)S(1)}, u32[]{:S(2)}, u32[]{:S(2)}) collective-permute-start(bf16[272,1792]{1,0:T(8,128)(2,1)} %get-tuple-element.27), channel_id=1, source_target_pairs={{0,8},{12,4},{1,9},{13,5},{2,10},{14,6},{3,11},{15,7},{16,24},{28,... | collective-permute-start | bytes 2924552 | tf_op jit(solution)/shard_map/ppermute | solution.py:486
  14.1 1.6 collective-permute-start.2
  15.7 2.1 collective-permute-start.3
  19.1 13.2 %forward_first.1 = (bf16[320,1024]{1,0:T(8,128)(2,1)}, bf16[320,1024]{1,0:T(8,128)(2,1)}) custom-call(s32[3]{0:T(128)} %pad_add_fusion.2.scalar_ref, bf16[272,3584]{1,0:T(8,128)(2,1)} %get-tuple-element.26.refs_0_.refs_4_, bf16[272,3584]{1,0:T(8,128)(2,1)} %collective-permute-done.4.refs_1_.refs_5_, bf16[640,1024]{1,0:T(8,128)(2,1)} %bitcast.47, ...), custom_call_target="tpu_custom_call" | custom-call | flops 1 | bytes 1 | tf_op jit(solution)/shard_map/forward_first/pallas_call | solution.py:48
  32.2 12.0 %near_gradients.1.refs_6_.refs_5_ = bf16[320,3584]{1,0:T(8,128)(2,1)} custom-call(s32[4]{0:T(128)} %pad_add_fusion.scalar_ref, bf16[3584,1024]{1,0:T(8,128)(2,1)} %bitcast.38, bf16[3584,1024]{1,0:T(8,128)(2,1)} %bitcast.42, bf16[320,1024]{1,0:T(8,128)(2,1)} %get-tuple-element.36.refs_2_.refs_4_.refs_3_, bf16[320,1024]{1,0:T(8,128)(2,1)} %get-tuple-element.31.refs_3_.refs_5_, ...), custom_call_target="tpu_custom_call" | custom-call | flops 1 | bytes 1 | tf_op jit(solution)/shard_map/near_gradients/pallas_call | solution.py:48
  44.2 1.8 collective-permute-done.3.refs_4_.refs_0_
  46.0 6.8 %collective-permute-done.refs_5_.refs_0_.refs_2_.refs_6_ = bf16[272,3584]{1,0:T(8,128)(2,1)S(1)} collective-permute-done((bf16[272,3584]{1,0:T(8,128)(2,1)}, bf16[272,3584]{1,0:T(8,128)(2,1)S(1)}, u32[]{:S(2)}, u32[]{:S(2)}) %collective-permute-start) | collective-permute-done | bytes 1949728 | tf_op jit(solution)/shard_map/ppermute | solution.py:483
  52.9 2.4 copy-done.8
  55.2 2.0 join_columns.2.refs_6_.refs_0_
  57.3 1.7 collective-permute-start.10
  59.0 8.5 %collective-permute-start.6 = (bf16[320,1024]{1,0:T(8,128)(2,1)}, bf16[320,1024]{1,0:T(8,128)(2,1)}, u32[]{:S(2)}, u32[]{:S(2)}) collective-permute-start(bf16[320,1024]{1,0:T(8,128)(2,1)} %get-tuple-element.36.refs_2_.refs_4_.refs_3_), channel_id=1, source_target_pairs={{0,8},{12,4},{1,9},{13,5},{2,10},{14,6},{3,11},{15,7},{16,24},{28,... | collective-permute-start | bytes 1966088 | tf_op jit(solution)/shard_map/ppermute | solution.py:486
  67.5 1.5 collective-permute-start.7
  69.0 2.3 collective-permute-start.8
  71.9 13.5 %forward_rest.1 = (bf16[320,1024]{1,0:T(8,128)(2,1)}, bf16[640,512]{1,0:T(8,128)(2,1)}, bf16[640,512]{1,0:T(8,128)(2,1)}) custom-call(s32[3]{0:T(128)} %pad_add_fusion.1.scalar_ref, bf16[272,3584]{1,0:T(8,128)(2,1)} %copy-done.3, bf16[272,3584]{1,0:T(8,128)(2,1)} %collective-permute-done.5.refs_1_.refs_3_.refs_7_, bf16[640,1024]{1,0:T(8,128)(2,1)} %bitcast.48, ...), custom_call_target="tpu_custom_call" | custom-call | flops 1 | bytes 1 | tf_op jit(solution)/shard_map/forward_rest/pallas_call | solution.py:48
  85.4 1.5 copy-done.4
  87.0 4.3 %pick_rows.3.refs_3_.refs_0_ = bf16[1792,640]{1,0:T(8,128)(2,1)S(1)} custom-call(s32[3]{0:T(128)S(1)} %pad_add_fusion.3.scalar_ref, bf16[272,3584]{1,0:T(8,128)(2,1)} %get-tuple-element.26.refs_0_.refs_4_, bf16[272,3584]{1,0:T(8,128)(2,1)} %collective-permute-done.4.refs_1_.refs_5_, bf16[272,3584]{1,0:T(8,128)(2,1)S(1)} %copy-done.4, ...), custom_call_target="tpu_custom_call" | custom-call | flops 1 | bytes 1 | tf_op jit(solution)/shard_map/pick_rows/pallas_call | solution.py:48
  91.3 2.6 %join_columns.3.refs_9_.refs_0_ = bf16[272,2688]{1,0:T(8,128)(2,1)} custom-call(s32[1]{0:T(128)} %constant.31.clone.1.scalar_ref, bf16[272,896]{1,0:T(8,128)(2,1)S(1)} %collective-permute-done.3.refs_4_.refs_0_, bf16[272,1792]{1,0:T(8,128)(2,1)} %collective-permute-done.2.refs_0_.refs_3_.refs_1_, ...), custom_call_target="tpu_custom_call" | custom-call | flops 1 | bytes 1 | tf_op jit(solution)/shard_map/join_columns/pallas_call | solution.py:48
  93.9 1.0 collective-permute-done.8.refs_8_.refs_10_
  95.4 1.5 collective-permute-start.19
  96.9 6.1 %collective-permute-start.12 = (bf16[320,1024]{1,0:T(8,128)(2,1)}, bf16[320,1024]{1,0:T(8,128)(2,1)}, u32[]{:S(2)}, u32[]{:S(2)}) collective-permute-start(bf16[320,1024]{1,0:T(8,128)(2,1)} %get-tuple-element.41.refs_8_.refs_2_.refs_4_.refs_5_), channel_id=1, source_target_pairs={{0,8},{12,4},{1,9},{13,5},{2,10},{14,6},{3,11},{15,7},{16,24},{28,... | collective-permute-start | bytes 1966088 | tf_op jit(solution)/shard_map/ppermute | solution.py:486
  103.0 1.5 collective-permute-start.13
  104.6 0.9 copy-done.15
  105.5 2.2 collective-permute-start.14
  107.7 13.8 %slot_gradients.1 = (bf16[640,2048]{1,0:T(8,128)(2,1)}, bf16[640,1536]{1,0:T(8,128)(2,1)}) custom-call(s32[4]{0:T(128)} %pad_add_fusion.scalar_ref, bf16[3584,1024]{1,0:T(8,128)(2,1)} %bitcast.40, bf16[3584,1024]{1,0:T(8,128)(2,1)} %bitcast.44, bf16[320,1024]{1,0:T(8,128)(2,1)} %get-tuple-element.41.refs_8_.refs_2_.refs_4_.refs_5_, ...), custom_call_target="tpu_custom_call" | custom-call | flops 1 | bytes 1 | tf_op jit(solution)/shard_map/slot_gradients/pallas_call | solution.py:48
  121.5 3.7 %all-to-all-start = ((bf16[4,160,2048]{2,1,0:T(8,128)(2,1)}), bf16[4,160,2048]{2,1,0:T(8,128)(2,1)S(1)}, u32[]{:S(2)}, u32[]{:S(2)}) async-start(bf16[4,160,2048]{2,1,0:T(8,128)(2,1)} %bitcast.49), calls=%async_computation | async-start | bytes 5242880 | tf_op jit(solution)/shard_map/all_to_all | solution.py:489
  125.3 1.5 copy-done.9
  126.8 1.2 copy-done.16
  128.0 4.3 %pick_rows.4.refs_1_.refs_2_.refs_12_ = bf16[1792,640]{1,0:T(8,128)(2,1)S(1)} custom-call(s32[3]{0:T(128)S(1)} %pad_add_fusion.4.scalar_ref, bf16[272,1792]{1,0:T(8,128)(2,1)} %join_columns.2.refs_6_.refs_0_, bf16[272,1792]{1,0:T(8,128)(2,1)} %collective-permute-done.9.refs_1_, bf16[272,1792]{1,0:T(8,128)(2,1)} %collective-permute-done.10.refs_2_, ...), custom_call_target="tpu_custom_call" | custom-call | flops 1 | bytes 1 | tf_op jit(solution)/shard_map/pick_rows/pallas_call | solution.py:48
  132.3 1.4 copy-done.1
  134.3 2.8 %collective-permute-start.15 = (bf16[640,512]{1,0:T(8,128)(2,1)S(1)}, bf16[640,512]{1,0:T(8,128)(2,1)}, u32[]{:S(2)}, u32[]{:S(2)}) collective-permute-start(bf16[640,512]{1,0:T(8,128)(2,1)S(1)} %copy-done.19), channel_id=1, source_target_pairs={{0,8},{12,4},{1,9},{13,5},{2,10},{14,6},{3,11},{15,7},{16,24},{28,... | collective-permute-start | bytes 1966088 | tf_op jit(solution)/shard_map/ppermute | solution.py:486
  137.2 1.6 collective-permute-start.16
  138.7 2.1 collective-permute-start.17
  140.9 7.9 %for_end.3.refs_4_ = bf16[896,1024]{1,0:T(8,128)(2,1)} custom-call(s32[1]{0:T(128)} %constant.31.clone.1.scalar_ref, bf16[1792,640]{1,0:T(8,128)(2,1)} %copy-done.2, bf16[1792,640]{1,0:T(8,128)(2,1)} %copy-done.1, bf16[1792,640]{1,0:T(8,128)(2,1)} %copy-done.1, bf16[320,1024]{1,0:T(8,128)(2,1)} %get-tuple-element.36.refs_2_.refs_4_.refs_3_, ...), custom_call_target="tpu_custom_call" | custom-call | flops 1 | bytes 1 | tf_op jit(solution)/shard_map/for_end/pallas_call | solution.py:48
  148.7 1.5 collective-permute-start.26
  150.3 1.5 copy-done.10
  151.8 5.9 %pick_rows.5.refs_9_.refs_1_.refs_2_.refs_3_ = bf16[2688,640]{1,0:T(8,128)(2,1)S(1)} custom-call(s32[4]{0:T(128)S(1)} %pad_add_fusion.5.scalar_ref, bf16[272,2688]{1,0:T(8,128)(2,1)} %join_columns.3.refs_9_.refs_0_, bf16[272,2688]{1,0:T(8,128)(2,1)} %collective-permute-done.18.refs_1_, bf16[272,2688]{1,0:T(8,128)(2,1)} %collective-permute-done.19.refs_2_, ...), custom_call_target="tpu_custom_call" | custom-call | flops 1 | bytes 1 | tf_op jit(solution)/shard_map/pick_rows/pallas_call | solution.py:48
  157.7 1.7 copy-done
  159.4 5.2 %collective-permute-done.17.refs_8_.refs_7_ = bf16[640,512]{1,0:T(8,128)(2,1)} collective-permute-done((bf16[640,512]{1,0:T(8,128)(2,1)S(1)}, bf16[640,512]{1,0:T(8,128)(2,1)}, u32[]{:S(2)}, u32[]{:S(2)}) %collective-permute-start.17) | collective-permute-done | bytes 655392 | tf_op jit(solution)/shard_map/ppermute | solution.py:486
  164.6 1.5 copy-done.6
  166.1 4.4 %all-to-all-start.1 = ((bf16[4,160,1536]{2,1,0:T(8,128)(2,1)}), bf16[4,160,1536]{2,1,0:T(8,128)(2,1)}, u32[]{:S(2)}, u32[]{:S(2)}) async-start(bf16[4,160,1536]{2,1,0:T(8,128)(2,1)} %bitcast.33), calls=%async_computation.1 | async-start | bytes 3932160 | tf_op jit(solution)/shard_map/all_to_all | solution.py:489
  170.6 6.5 %collective-permute-start.22 = (bf16[640,512]{1,0:T(8,128)(2,1)}, bf16[640,512]{1,0:T(8,128)(2,1)}, u32[]{:S(2)}, u32[]{:S(2)}) collective-permute-start(bf16[640,512]{1,0:T(8,128)(2,1)} %get-tuple-element.46.refs_4_.refs_3_), channel_id=1, source_target_pairs={{0,8},{12,4},{1,9},{13,5},{2,10},{14,6},{3,11},{15,7},{16,24},{28,... | collective-permute-start | bytes 1966088 | tf_op jit(solution)/shard_map/ppermute | solution.py:486
  177.0 1.5 collective-permute-start.23
  178.5 2.3 collective-permute-start.24
  180.8 5.2 %for_end.4.refs_2_ = bf16[896,512]{1,0:T(8,128)(2,1)} custom-call(s32[1]{0:T(128)} %constant.31.clone.1.scalar_ref, bf16[1792,640]{1,0:T(8,128)(2,1)} %copy-done.2, bf16[1792,640]{1,0:T(8,128)(2,1)} %copy-done.1, bf16[1792,640]{1,0:T(8,128)(2,1)} %copy-done.1, bf16[640,512]{1,0:T(8,128)(2,1)} %get-tuple-element.42.refs_3_.refs_4_, ...), custom_call_target="tpu_custom_call" | custom-call | flops 1 | bytes 1 | tf_op jit(solution)/shard_map/for_end/pallas_call | solution.py:48
  186.1 2.1 combine.2.refs_13_
  188.2 1.6 collective-permute-start.21
  189.8 2.9 %collective-permute-done.26.refs_12_ = bf16[896,1024]{1,0:T(8,128)(2,1)} collective-permute-done((bf16[896,1024]{1,0:T(8,128)(2,1)}, bf16[896,1024]{1,0:T(8,128)(2,1)}, u32[]{:S(2)}, u32[]{:S(2)}) %collective-permute-start.26) | collective-permute-done | bytes 1835040 | tf_op jit(solution)/shard_map/ppermute | solution.py:498
  192.7 1.3 collective-permute-start.25
  194.0 9.8 %for_own.3.refs_9_ = bf16[896,1024]{1,0:T(8,128)(2,1)} custom-call(s32[1]{0:T(128)} %constant.31.clone.1.scalar_ref, bf16[1792,640]{1,0:T(8,128)(2,1)} %copy-done.2, bf16[2688,640]{1,0:T(8,128)(2,1)} %copy-done, bf16[2688,640]{1,0:T(8,128)(2,1)} %copy-done, bf16[2688,640]{1,0:T(8,128)(2,1)} %copy-done, ...), custom_call_target="tpu_custom_call" | custom-call | flops 1 | bytes 1 | tf_op jit(solution)/shard_map/for_own/pallas_call | solution.py:48
  203.8 1.4 collective-permute-done.24.refs_8_.refs_7_
  205.2 5.2 %for_end.5.refs_2_ = bf16[896,512]{1,0:T(8,128)(2,1)} custom-call(s32[1]{0:T(128)} %constant.31.clone.1.scalar_ref, bf16[1792,640]{1,0:T(8,128)(2,1)} %copy-done.2, bf16[1792,640]{1,0:T(8,128)(2,1)} %copy-done.1, bf16[1792,640]{1,0:T(8,128)(2,1)} %copy-done.1, bf16[640,512]{1,0:T(8,128)(2,1)} %get-tuple-element.46.refs_4_.refs_3_, ...), custom_call_target="tpu_custom_call" | custom-call | flops 1 | bytes 1 | tf_op jit(solution)/shard_map/for_end/pallas_call | solution.py:48
  210.4 1.3 collective-permute-start.28
  211.7 1.2 copy-done.13
  212.9 3.2 %combine.3.refs_9_ = bf16[256,1536]{1,0:T(8,128)(2,1)S(1)} custom-call(s32[1]{0:T(128)} %constant.31.clone.1.scalar_ref, s32[2,256]{1,0:T(2,128)S(1)} %bitcast.36, bf16[640,1536]{1,0:T(8,128)(2,1)} %bitcast.22.refs_1_, bf16[896,512]{1,0:T(8,128)(2,1)S(1)} %copy-done.13), custom_call_target="tpu_custom_call" | custom-call | flops 1 | bytes 1 | tf_op jit(solution)/shard_map/combine/pallas_call | solution.py:48
  216.2 1.6 collective-permute-start.27
  218.6 6.4 %for_own.4.refs_8_.refs_2_ = bf16[896,1024]{1,0:T(8,128)(2,1)} custom-call(s32[1]{0:T(128)} %constant.31.clone.1.scalar_ref, bf16[1792,640]{1,0:T(8,128)(2,1)} %copy-done.2, bf16[2688,640]{1,0:T(8,128)(2,1)} %copy-done, bf16[2688,640]{1,0:T(8,128)(2,1)} %copy-done, bf16[2688,640]{1,0:T(8,128)(2,1)} %copy-done, ...), custom_call_target="tpu_custom_call" | custom-call | flops 1 | bytes 1 | tf_op jit(solution)/shard_map/for_own/pallas_call | solution.py:48
  225.0 6.2 %for_own.5.refs_0_ = f32[896,512]{1,0:T(8,128)} custom-call(s32[1]{0:T(128)} %constant.31.clone.1.scalar_ref, bf16[1792,640]{1,0:T(8,128)(2,1)} %copy-done.2, bf16[2688,640]{1,0:T(8,128)(2,1)} %copy-done, bf16[2688,640]{1,0:T(8,128)(2,1)} %copy-done, bf16[2688,640]{1,0:T(8,128)(2,1)} %copy-done, bf16[640,512]{1,0:T(8,128)(2,1)} %get-tuple-element.46.refs_4_.refs_3_, ...), custom_call_target="tpu_custom_call" | custom-call | flops 1 | bytes 1 | tf_op jit(solution)/shard_map/for_own/pallas_call | solution.py:48
  231.3 4.3 %collective-permute-done.28.refs_1_ = bf16[896,512]{1,0:T(8,128)(2,1)S(1)} collective-permute-done((bf16[896,512]{1,0:T(8,128)(2,1)}, bf16[896,512]{1,0:T(8,128)(2,1)S(1)}, u32[]{:S(2)}, u32[]{:S(2)}) %collective-permute-start.28) | collective-permute-done | bytes 917536 | tf_op jit(solution)/shard_map/ppermute | solution.py:498
  235.6 1.5 copy-done.11
  237.1 1.1 finish.1
  238.2 2.8 %maximum_bitcast_fusion = bf16[1,256,3584]{2,1,0:T(8,128)(2,1)} fusion(bf16[256,1536]{1,0:T(8,128)(2,1)} %collective-permute-done.27, bf16[256,2048]{1,0:T(8,128)(2,1)} %collective-permute-done.21), kind=kLoop, calls=%fused_computation | loop fusion | flops 3670016 | bytes 3670016 | tf_op jit(solution)/shard_map/broadcast_in_dim | solution.py:603
  (67 shorter events, 5.4 us)
Async XLA Ops:
  0.7 1.5 copy-start.5
  2.2 0.7 copy-start.17
  6.5 12.5 %collective-permute-start.4 = (bf16[272,3584]{1,0:T(8,128)(2,1)}, bf16[272,3584]{1,0:T(8,128)(2,1)}, u32[]{:S(2)}, u32[]{:S(2)}) collective-permute-start(bf16[272,3584]{1,0:T(8,128)(2,1)} %get-tuple-element.26.refs_0_.refs_4_), channel_id=1, source_target_pairs={{0,1},{1,0},{2,3},{3,2},{4,5},{5,4},{6,7},{7,6},{8,9},{9,8},{10,11... | collective-permute-start | bytes 5849096 | tf_op jit(solution)/shard_map/ppermute | solution.py:480
  7.0 45.9 %collective-permute-start = (bf16[272,3584]{1,0:T(8,128)(2,1)}, bf16[272,3584]{1,0:T(8,128)(2,1)S(1)}, u32[]{:S(2)}, u32[]{:S(2)}) collective-permute-start(bf16[272,3584]{1,0:T(8,128)(2,1)} %get-tuple-element.26.refs_0_.refs_4_), channel_id=1, source_target_pairs={{0,2},{1,3},{2,0},{3,1},{4,6},{5,7},{6,4},{7,5},{8,10},{9,11},{10,... | collective-permute-start | bytes 5849096 | tf_op jit(solution)/shard_map/ppermute | solution.py:483
  9.5 36.5 %collective-permute-start.1 = (bf16[272,1792]{1,0:T(8,128)(2,1)}, bf16[272,1792]{1,0:T(8,128)(2,1)S(1)}, u32[]{:S(2)}, u32[]{:S(2)}) collective-permute-start(bf16[272,1792]{1,0:T(8,128)(2,1)} %get-tuple-element.27), channel_id=1, source_target_pairs={{0,8},{12,4},{1,9},{13,5},{2,10},{14,6},{3,11},{15,7},{16,24},{28,... | collective-permute-start | bytes 2924552 | tf_op jit(solution)/shard_map/ppermute | solution.py:486
  14.1 32.0 %collective-permute-start.2 = (bf16[272,1792]{1,0:T(8,128)(2,1)}, bf16[272,1792]{1,0:T(8,128)(2,1)}, u32[]{:S(2)}, u32[]{:S(2)}) collective-permute-start(bf16[272,1792]{1,0:T(8,128)(2,1)} %get-tuple-element.28), channel_id=1, source_target_pairs={{4,8},{8,4},{5,9},{9,5},{6,10},{10,6},{7,11},{11,7},{20,24},{24,20... | collective-permute-start | bytes 2924552 | tf_op jit(solution)/shard_map/ppermute | solution.py:486
  15.7 30.3 %collective-permute-start.3 = (bf16[272,896]{1,0:T(8,128)(2,1)}, bf16[272,896]{1,0:T(8,128)(2,1)S(1)}, u32[]{:S(2)}, u32[]{:S(2)}) collective-permute-start(bf16[272,896]{1,0:T(8,128)(2,1)} %get-tuple-element.29), channel_id=1, source_target_pairs={{0,4},{12,8},{1,5},{13,9},{2,6},{14,10},{3,7},{15,11},{16,20},{28,... | collective-permute-start | bytes 1462280 | tf_op jit(solution)/shard_map/ppermute | solution.py:486
  52.9 4.4 %copy-start.3 = (bf16[272,3584]{1,0:T(8,128)(2,1)}, bf16[272,3584]{1,0:T(8,128)(2,1)S(1)}, u32[]{:S(2)}) copy-start(bf16[272,3584]{1,0:T(8,128)(2,1)S(1)} %collective-permute-done.refs_5_.refs_0_.refs_2_.refs_6_) | copy-start | bytes 5849092
  52.9 19.1 %collective-permute-start.5 = (bf16[272,3584]{1,0:T(8,128)(2,1)S(1)}, bf16[272,3584]{1,0:T(8,128)(2,1)}, u32[]{:S(2)}, u32[]{:S(2)}) collective-permute-start(bf16[272,3584]{1,0:T(8,128)(2,1)S(1)} %collective-permute-done.refs_5_.refs_0_.refs_2_.refs_6_), channel_id=1, source_target_pairs={{0,1},{1,0},{2,3},{3,2},{4,5},{5,4},{6,7},{7,6},{8,9},{9,8},{10,11... | collective-permute-start | bytes 5849096 | tf_op jit(solution)/shard_map/ppermute | solution.py:480
  52.9 2.4 copy-start.8
  57.3 37.6 %collective-permute-start.10 = (bf16[272,1792]{1,0:T(8,128)(2,1)}, bf16[272,1792]{1,0:T(8,128)(2,1)}, u32[]{:S(2)}, u32[]{:S(2)}) collective-permute-start(bf16[272,1792]{1,0:T(8,128)(2,1)} %join_columns.2.refs_6_.refs_0_), channel_id=1, source_target_pairs={{0,2},{1,3},{2,0},{3,1},{4,6},{5,7},{6,4},{7,5},{8,10},{9,11},{10,... | collective-permute-start | bytes 2924552 | tf_op jit(solution)/shard_map/ppermute | solution.py:483
  59.0 34.9 %collective-permute-start.6 = (bf16[320,1024]{1,0:T(8,128)(2,1)}, bf16[320,1024]{1,0:T(8,128)(2,1)}, u32[]{:S(2)}, u32[]{:S(2)}) collective-permute-start(bf16[320,1024]{1,0:T(8,128)(2,1)} %get-tuple-element.36.refs_2_.refs_4_.refs_3_), channel_id=1, source_target_pairs={{0,8},{12,4},{1,9},{13,5},{2,10},{14,6},{3,11},{15,7},{16,24},{28,... | collective-permute-start | bytes 1966088 | tf_op jit(solution)/shard_map/ppermute | solution.py:486
  67.5 26.4 %collective-permute-start.7 = (bf16[320,1024]{1,0:T(8,128)(2,1)}, bf16[320,1024]{1,0:T(8,128)(2,1)}, u32[]{:S(2)}, u32[]{:S(2)}) collective-permute-start(bf16[320,1024]{1,0:T(8,128)(2,1)} %get-tuple-element.36.refs_2_.refs_4_.refs_3_), channel_id=1, source_target_pairs={{4,8},{8,4},{5,9},{9,5},{6,10},{10,6},{7,11},{11,7},{20,24},{24,20... | collective-permute-start | bytes 1966088 | tf_op jit(solution)/shard_map/ppermute | solution.py:486
  69.0 25.9 %collective-permute-start.8 = (bf16[320,1024]{1,0:T(8,128)(2,1)}, bf16[320,1024]{1,0:T(8,128)(2,1)}, u32[]{:S(2)}, u32[]{:S(2)}) collective-permute-start(bf16[320,1024]{1,0:T(8,128)(2,1)} %get-tuple-element.36.refs_2_.refs_4_.refs_3_), channel_id=1, source_target_pairs={{0,4},{12,8},{1,5},{13,9},{2,6},{14,10},{3,7},{15,11},{16,20},{28,... | collective-permute-start | bytes 1966088 | tf_op jit(solution)/shard_map/ppermute | solution.py:486
  85.4 1.5 copy-start.4
  91.3 2.6 %copy-start.2 = (bf16[1792,640]{1,0:T(8,128)(2,1)}, bf16[1792,640]{1,0:T(8,128)(2,1)S(1)}, u32[]{:S(2)}) copy-start(bf16[1792,640]{1,0:T(8,128)(2,1)S(1)} %pick_rows.3.refs_3_.refs_0_) | copy-start | bytes 6881284
  94.9 9.6 %collective-permute-start.11 = (bf16[272,1792]{1,0:T(8,128)(2,1)}, bf16[272,1792]{1,0:T(8,128)(2,1)S(1)}, u32[]{:S(2)}, u32[]{:S(2)}) collective-permute-start(bf16[272,1792]{1,0:T(8,128)(2,1)} %collective-permute-done.10.refs_2_), channel_id=1, source_target_pairs={{0,1},{1,0},{2,3},{3,2},{4,5},{5,4},{6,7},{7,6},{8,9},{9,8},{10,11... | collective-permute-start | bytes 2924552 | tf_op jit(solution)/shard_map/ppermute | solution.py:480
  94.9 30.3 %collective-permute-start.9 = (bf16[272,1792]{1,0:T(8,128)(2,1)}, bf16[272,1792]{1,0:T(8,128)(2,1)}, u32[]{:S(2)}, u32[]{:S(2)}) collective-permute-start(bf16[272,1792]{1,0:T(8,128)(2,1)} %join_columns.2.refs_6_.refs_0_), channel_id=1, source_target_pairs={{0,1},{1,0},{2,3},{3,2},{4,5},{5,4},{6,7},{7,6},{8,9},{9,8},{10,11... | collective-permute-start | bytes 2924552 | tf_op jit(solution)/shard_map/ppermute | solution.py:480
  95.4 38.8 %collective-permute-start.19 = (bf16[272,2688]{1,0:T(8,128)(2,1)}, bf16[272,2688]{1,0:T(8,128)(2,1)}, u32[]{:S(2)}, u32[]{:S(2)}) collective-permute-start(bf16[272,2688]{1,0:T(8,128)(2,1)} %join_columns.3.refs_9_.refs_0_), channel_id=1, source_target_pairs={{0,2},{1,3},{2,0},{3,1},{4,6},{5,7},{6,4},{7,5},{8,10},{9,11},{10,... | collective-permute-start | bytes 4386824 | tf_op jit(solution)/shard_map/ppermute | solution.py:483
  96.9 36.8 %collective-permute-start.12 = (bf16[320,1024]{1,0:T(8,128)(2,1)}, bf16[320,1024]{1,0:T(8,128)(2,1)}, u32[]{:S(2)}, u32[]{:S(2)}) collective-permute-start(bf16[320,1024]{1,0:T(8,128)(2,1)} %get-tuple-element.41.refs_8_.refs_2_.refs_4_.refs_5_), channel_id=1, source_target_pairs={{0,8},{12,4},{1,9},{13,5},{2,10},{14,6},{3,11},{15,7},{16,24},{28,... | collective-permute-start | bytes 1966088 | tf_op jit(solution)/shard_map/ppermute | solution.py:486
  103.0 30.7 %collective-permute-start.13 = (bf16[320,1024]{1,0:T(8,128)(2,1)}, bf16[320,1024]{1,0:T(8,128)(2,1)}, u32[]{:S(2)}, u32[]{:S(2)}) collective-permute-start(bf16[320,1024]{1,0:T(8,128)(2,1)} %get-tuple-element.41.refs_8_.refs_2_.refs_4_.refs_5_), channel_id=1, source_target_pairs={{4,8},{8,4},{5,9},{9,5},{6,10},{10,6},{7,11},{11,7},{20,24},{24,20... | collective-permute-start | bytes 1966088 | tf_op jit(solution)/shard_map/ppermute | solution.py:486
  104.5 0.9 copy-start.15
  105.5 28.2 %collective-permute-start.14 = (bf16[320,1024]{1,0:T(8,128)(2,1)}, bf16[320,1024]{1,0:T(8,128)(2,1)}, u32[]{:S(2)}, u32[]{:S(2)}) collective-permute-start(bf16[320,1024]{1,0:T(8,128)(2,1)} %get-tuple-element.41.refs_8_.refs_2_.refs_4_.refs_5_), channel_id=1, source_target_pairs={{0,4},{12,8},{1,5},{13,9},{2,6},{14,10},{3,7},{15,11},{16,20},{28,... | collective-permute-start | bytes 1966088 | tf_op jit(solution)/shard_map/ppermute | solution.py:486
  121.5 43.1 %all-to-all-start = ((bf16[4,160,2048]{2,1,0:T(8,128)(2,1)}), bf16[4,160,2048]{2,1,0:T(8,128)(2,1)S(1)}, u32[]{:S(2)}, u32[]{:S(2)}) async-start(bf16[4,160,2048]{2,1,0:T(8,128)(2,1)} %bitcast.49), calls=%async_computation | async-start | bytes 5242880 | tf_op jit(solution)/shard_map/all_to_all | solution.py:489
  125.3 1.5 copy-start.9
  126.8 1.2 copy-start.16
  128.0 6.3 %copy-start.19 = (bf16[640,512]{1,0:T(8,128)(2,1)S(1)}, bf16[640,512]{1,0:T(8,128)(2,1)}, u32[]{:S(2)}) copy-start(bf16[640,512]{1,0:T(8,128)(2,1)} %get-tuple-element.42.refs_3_.refs_4_) | copy-start | bytes 1966084
  132.3 1.4 copy-start.1
  133.7 15.0 %collective-permute-start.18 = (bf16[272,2688]{1,0:T(8,128)(2,1)}, bf16[272,2688]{1,0:T(8,128)(2,1)}, u32[]{:S(2)}, u32[]{:S(2)}) collective-permute-start(bf16[272,2688]{1,0:T(8,128)(2,1)} %join_columns.3.refs_9_.refs_0_), channel_id=1, source_target_pairs={{0,1},{1,0},{2,3},{3,2},{4,5},{5,4},{6,7},{7,6},{8,9},{9,8},{10,11... | collective-permute-start | bytes 4386824 | tf_op jit(solution)/shard_map/ppermute | solution.py:480
  134.2 16.1 %collective-permute-start.20 = (bf16[272,2688]{1,0:T(8,128)(2,1)}, bf16[272,2688]{1,0:T(8,128)(2,1)}, u32[]{:S(2)}, u32[]{:S(2)}) collective-permute-start(bf16[272,2688]{1,0:T(8,128)(2,1)} %collective-permute-done.19.refs_2_), channel_id=1, source_target_pairs={{0,1},{1,0},{2,3},{3,2},{4,5},{5,4},{6,7},{7,6},{8,9},{9,8},{10,11... | collective-permute-start | bytes 4386824 | tf_op jit(solution)/shard_map/ppermute | solution.py:480
  134.3 25.1 %collective-permute-start.15 = (bf16[640,512]{1,0:T(8,128)(2,1)S(1)}, bf16[640,512]{1,0:T(8,128)(2,1)}, u32[]{:S(2)}, u32[]{:S(2)}) collective-permute-start(bf16[640,512]{1,0:T(8,128)(2,1)S(1)} %copy-done.19), channel_id=1, source_target_pairs={{0,8},{12,4},{1,9},{13,5},{2,10},{14,6},{3,11},{15,7},{16,24},{28,... | collective-permute-start | bytes 1966088 | tf_op jit(solution)/shard_map/ppermute | solution.py:486
  137.2 22.3 %collective-permute-start.16 = (bf16[640,512]{1,0:T(8,128)(2,1)S(1)}, bf16[640,512]{1,0:T(8,128)(2,1)}, u32[]{:S(2)}, u32[]{:S(2)}) collective-permute-start(bf16[640,512]{1,0:T(8,128)(2,1)S(1)} %copy-done.19), channel_id=1, source_target_pairs={{4,8},{8,4},{5,9},{9,5},{6,10},{10,6},{7,11},{11,7},{20,24},{24,20... | collective-permute-start | bytes 1966088 | tf_op jit(solution)/shard_map/ppermute | solution.py:486
  138.7 25.8 %collective-permute-start.17 = (bf16[640,512]{1,0:T(8,128)(2,1)S(1)}, bf16[640,512]{1,0:T(8,128)(2,1)}, u32[]{:S(2)}, u32[]{:S(2)}) collective-permute-start(bf16[640,512]{1,0:T(8,128)(2,1)S(1)} %copy-done.19), channel_id=1, source_target_pairs={{0,4},{12,8},{1,5},{13,9},{2,6},{14,10},{3,7},{15,11},{16,20},{28,... | collective-permute-start | bytes 1966088 | tf_op jit(solution)/shard_map/ppermute | solution.py:486
  148.7 43.9 %collective-permute-start.26 = (bf16[896,1024]{1,0:T(8,128)(2,1)}, bf16[896,1024]{1,0:T(8,128)(2,1)}, u32[]{:S(2)}, u32[]{:S(2)}) collective-permute-start(bf16[896,1024]{1,0:T(8,128)(2,1)} %for_end.3.refs_4_), channel_id=1, source_target_pairs={{4,0},{8,12},{5,1},{9,13},{6,2},{10,14},{7,3},{11,15},{20,16},{24,... | collective-permute-start | bytes 5505032 | tf_op jit(solution)/shard_map/ppermute | solution.py:498
  150.3 1.5 copy-start.10
  157.7 1.7 copy-start
  164.6 1.5 copy-start.6
  166.1 45.6 %all-to-all-start.1 = ((bf16[4,160,1536]{2,1,0:T(8,128)(2,1)}), bf16[4,160,1536]{2,1,0:T(8,128)(2,1)}, u32[]{:S(2)}, u32[]{:S(2)}) async-start(bf16[4,160,1536]{2,1,0:T(8,128)(2,1)} %bitcast.33), calls=%async_computation.1 | async-start | bytes 3932160 | tf_op jit(solution)/shard_map/all_to_all | solution.py:489
  170.6 15.5 %copy-start.7 = (bf16[4,160,2048]{2,1,0:T(8,128)(2,1)S(1)}, bf16[4,160,2048]{2,1,0:T(8,128)(2,1)}, u32[]{:S(2)}) copy-start(bf16[4,160,2048]{2,1,0:T(8,128)(2,1)} %copy-done.6) | copy-start | bytes 7864324
  170.6 15.5 %copy-start.18 = (s32[1,256,2]{1,2,0:T(2,128)S(1)}, s32[1,256,2]{1,2,0:T(2,128)}, u32[]{:S(2)}) copy-start(s32[1,256,2]{1,2,0:T(2,128)} %param.6) | copy-start | bytes 6148
  170.6 33.2 %collective-permute-start.22 = (bf16[640,512]{1,0:T(8,128)(2,1)}, bf16[640,512]{1,0:T(8,128)(2,1)}, u32[]{:S(2)}, u32[]{:S(2)}) collective-permute-start(bf16[640,512]{1,0:T(8,128)(2,1)} %get-tuple-element.46.refs_4_.refs_3_), channel_id=1, source_target_pairs={{0,8},{12,4},{1,9},{13,5},{2,10},{14,6},{3,11},{15,7},{16,24},{28,... | collective-permute-start | bytes 1966088 | tf_op jit(solution)/shard_map/ppermute | solution.py:486
  177.0 26.8 %collective-permute-start.23 = (bf16[640,512]{1,0:T(8,128)(2,1)}, bf16[640,512]{1,0:T(8,128)(2,1)}, u32[]{:S(2)}, u32[]{:S(2)}) collective-permute-start(bf16[640,512]{1,0:T(8,128)(2,1)} %get-tuple-element.46.refs_4_.refs_3_), channel_id=1, source_target_pairs={{4,8},{8,4},{5,9},{9,5},{6,10},{10,6},{7,11},{11,7},{20,24},{24,20... | collective-permute-start | bytes 1966088 | tf_op jit(solution)/shard_map/ppermute | solution.py:486
  178.5 26.7 %collective-permute-start.24 = (bf16[640,512]{1,0:T(8,128)(2,1)}, bf16[640,512]{1,0:T(8,128)(2,1)}, u32[]{:S(2)}, u32[]{:S(2)}) collective-permute-start(bf16[640,512]{1,0:T(8,128)(2,1)} %get-tuple-element.46.refs_4_.refs_3_), channel_id=1, source_target_pairs={{0,4},{12,8},{1,5},{13,9},{2,6},{14,10},{3,7},{15,11},{16,20},{28,... | collective-permute-start | bytes 1966088 | tf_op jit(solution)/shard_map/ppermute | solution.py:486
  188.2 5.8 %copy-start.12 = (bf16[256,2048]{1,0:T(8,128)(2,1)}, bf16[256,2048]{1,0:T(8,128)(2,1)S(1)}, u32[]{:S(2)}) copy-start(bf16[256,2048]{1,0:T(8,128)(2,1)S(1)} %combine.2.refs_13_) | copy-start | bytes 3145732
  188.2 43.1 %collective-permute-start.21 = (bf16[256,2048]{1,0:T(8,128)(2,1)S(1)}, bf16[256,2048]{1,0:T(8,128)(2,1)}, u32[]{:S(2)}, u32[]{:S(2)}) collective-permute-start(bf16[256,2048]{1,0:T(8,128)(2,1)S(1)} %combine.2.refs_13_), channel_id=1, source_target_pairs={{0,16},{16,0},{1,17},{17,1},{2,18},{18,2},{3,19},{19,3},{4,20},{20... | collective-permute-start | bytes 3145736 | tf_op jit(solution)/shard_map/ppermute | solution.py:495
  192.7 25.1 %collective-permute-start.25 = (bf16[896,512]{1,0:T(8,128)(2,1)}, bf16[896,512]{1,0:T(8,128)(2,1)S(1)}, u32[]{:S(2)}, u32[]{:S(2)}) collective-permute-start(bf16[896,512]{1,0:T(8,128)(2,1)} %for_end.4.refs_2_), channel_id=1, source_target_pairs={{4,0},{8,12},{5,1},{9,13},{6,2},{10,14},{7,3},{11,15},{20,16},{24,... | collective-permute-start | bytes 2752520 | tf_op jit(solution)/shard_map/ppermute | solution.py:498
  210.4 25.2 %collective-permute-start.28 = (bf16[896,512]{1,0:T(8,128)(2,1)}, bf16[896,512]{1,0:T(8,128)(2,1)S(1)}, u32[]{:S(2)}, u32[]{:S(2)}) collective-permute-start(bf16[896,512]{1,0:T(8,128)(2,1)} %for_end.5.refs_2_), channel_id=1, source_target_pairs={{4,0},{8,12},{5,1},{9,13},{6,2},{10,14},{7,3},{11,15},{20,16},{24,... | collective-permute-start | bytes 2752520 | tf_op jit(solution)/shard_map/ppermute | solution.py:498
  211.7 1.2 copy-start.13
  216.2 1.6 copy-start.14
  216.2 22.0 %collective-permute-start.27 = (bf16[256,1536]{1,0:T(8,128)(2,1)S(1)}, bf16[256,1536]{1,0:T(8,128)(2,1)}, u32[]{:S(2)}, u32[]{:S(2)}) collective-permute-start(bf16[256,1536]{1,0:T(8,128)(2,1)S(1)} %combine.3.refs_9_), channel_id=1, source_target_pairs={{0,16},{16,0},{1,17},{17,1},{2,18},{18,2},{3,19},{19,3},{4,20},{20... | collective-permute-start | bytes 2359304 | tf_op jit(solution)/shard_map/ppermute | solution.py:495
  217.7 0.9 copy-start.20
  235.6 1.5 copy-start.11

commit v5 on v4

--- a/solution.py
+++ b/solution.py
@@ -449,6 +449,7 @@
         (1,),
         after=after,
         aliases={3: 0} if target is not None else None,
+        vmem=60,
     )[0]
 
 
@@ -515,7 +516,7 @@
     far = []
     for value in far_even:
         far += [value, swap(tied(value, *epoch))]
-    end_columns = join_columns([(others[k], wide, wide) for k in range(1, len(sets))], after=epoch)
+    end_columns = join_columns([(others[k], wide, wide) for k in range(1, len(sets))], after=epoch[:-1])
     end_far = [shift(end_columns, by) for by in chips]
     far_gate, *ups = forward(
         expert, places, far, upstream, gate_w, up_w, up_parts, first=near_up, after=[end_columns]

time: 243 us -> 240 us (0.988)
  local copies, waits for them, and re-layouts: 19.6 us -> 14.8 us
  Pallas kernels: 122 us -> 125 us
    unnamed x42 -> x36, local copies, waits for them, and re-layouts: 19.5 us -> 14.8 us
  transfers between devices with their start and end apart: 31 -> 31, of which waited for: 7 -> 7; matrix products, arithmetic and copies ran while one was open for 1% -> 1% of each run, Pallas kernels for 49% -> 51%
where the time goes in v5:
time: 240 us; the launch traced here: 238 us
  Pallas kernels  125 us (52%)
  starting transfers between devices  69.8 us (29%)
  waiting for transfers between devices  24.6 us (10%)
  local copies, waits for them, and re-layouts  14.8 us (6%)
  other arithmetic  3.5 us (1%)
    pallas_call x19, Pallas kernels, call(): pl.pallas_call(kernel, name=name, out_shape=[jax.ShapeDtypeStruct(shape,...  125 us
    ppermute x15, starting transfers between devices, over_groups(): return lax.ppermute(value, 'dp', pairs)  47.2 us
    unnamed x36, local copies, waits for them, and re-layouts  14.8 us
    ppermute x15, waiting for transfers between devices, over_groups(): return lax.ppermute(value, 'dp', pairs)  9.52 us
    ppermute x3, waiting for transfers between devices, to_ends(): return lax.ppermute(value, 'dp', [(1, 0), (groups - 2, groups - 1)])  8.25 us
    all_to_all x2, starting transfers between devices, to_sources(): lax.all_to_all(value.reshape(experts, capacity, value.shape[1]), 'expert'...  8.07 us
    ppermute x3, waiting for transfers between devices, shift(): lax.ppermute(value, 'expert', [(s, (s + 2 * by) % experts) for s in range...  6.84 us
    ppermute x3, starting transfers between devices, shift(): lax.ppermute(value, 'expert', [(s, (s + 2 * by) % experts) for s in range...  5.78 us
  transfers between devices with their start and end apart: 31, of which 7 were waited for; matrix products, arithmetic and copies ran while one was open for 1% of the time, Pallas kernels for 51%

profile of v5, /device:TPU:0, one launch (start us, length us, event | category | flops | bytes accessed | tf_op | source)
XLA Modules:
  0.0 238.2 jit_solution(407257119423524207)
XLA Ops:
  0.8 1.5 copy-done.5
  2.3 0.7 copy-done.15
  2.9 3.6 %cut_columns.1 = (bf16[272,3584]{1,0:T(8,128)(2,1)}, bf16[272,896]{1,0:T(8,128)(2,1)}, bf16[272,1792]{1,0:T(8,128)(2,1)}, bf16[272,1792]{1,0:T(8,128)(2,1)}) custom-call(s32[5]{0:T(128)S(1)} %stack.82.scalar_ref, s32[2,256]{1,0:T(2,128)S(1)} %bitcast.34, bf16[256,3584]{1,0:T(8,128)(2,1)S(1)} %bitcast.27, bf16[256,3584]{1,0:T(8,128)(2,1)S(1)} %bitcast.28, ...), custom_call_target="tpu_custom_call" | custom-call | flops 1 | bytes 1 | tf_op jit(solution)/shard_map/cut_columns/pallas_call | solution.py:48
  7.0 2.5 %collective-permute-start = (bf16[272,3584]{1,0:T(8,128)(2,1)}, bf16[272,3584]{1,0:T(8,128)(2,1)S(1)}, u32[]{:S(2)}, u32[]{:S(2)}) collective-permute-start(bf16[272,3584]{1,0:T(8,128)(2,1)} %get-tuple-element.26.refs_0_.refs_4_), channel_id=1, source_target_pairs={{0,2},{1,3},{2,0},{3,1},{4,6},{5,7},{6,4},{7,5},{8,10},{9,11},{10,... | collective-permute-start | bytes 5849096 | tf_op jit(solution)/shard_map/ppermute | solution.py:484
  9.5 4.5 %collective-permute-start.1 = (bf16[272,1792]{1,0:T(8,128)(2,1)}, bf16[272,1792]{1,0:T(8,128)(2,1)S(1)}, u32[]{:S(2)}, u32[]{:S(2)}) collective-permute-start(bf16[272,1792]{1,0:T(8,128)(2,1)} %get-tuple-element.27), channel_id=1, source_target_pairs={{0,8},{12,4},{1,9},{13,5},{2,10},{14,6},{3,11},{15,7},{16,24},{28,... | collective-permute-start | bytes 2924552 | tf_op jit(solution)/shard_map/ppermute | solution.py:487
  14.1 1.6 collective-permute-start.2
  15.7 2.1 collective-permute-start.3
  18.5 0.7 pad_add_fusion.scalar_ref
  19.2 13.2 %forward_first.1 = (bf16[320,1024]{1,0:T(8,128)(2,1)}, bf16[320,1024]{1,0:T(8,128)(2,1)}) custom-call(s32[3]{0:T(128)} %pad_add_fusion.2.scalar_ref, bf16[272,3584]{1,0:T(8,128)(2,1)} %get-tuple-element.26.refs_0_.refs_4_, bf16[272,3584]{1,0:T(8,128)(2,1)} %collective-permute-done.4.refs_1_.refs_5_, bf16[640,1024]{1,0:T(8,128)(2,1)} %bitcast.47, ...), custom_call_target="tpu_custom_call" | custom-call | flops 1 | bytes 1 | tf_op jit(solution)/shard_map/forward_first/pallas_call | solution.py:48
  32.3 12.0 %near_gradients.1.refs_5_ = bf16[320,3584]{1,0:T(8,128)(2,1)} custom-call(s32[4]{0:T(128)} %pad_add_fusion.scalar_ref, bf16[3584,1024]{1,0:T(8,128)(2,1)} %bitcast.38, bf16[3584,1024]{1,0:T(8,128)(2,1)} %bitcast.42, bf16[320,1024]{1,0:T(8,128)(2,1)} %get-tuple-element.36.refs_2_.refs_4_.refs_3_, bf16[320,1024]{1,0:T(8,128)(2,1)} %get-tuple-element.31.refs_3_.refs_5_, ...), custom_call_target="tpu_custom_call" | custom-call | flops 1 | bytes 1 | tf_op jit(solution)/shard_map/near_gradients/pallas_call | solution.py:48
  44.3 1.7 collective-permute-done.3.refs_4_.refs_0_
  46.0 6.8 %collective-permute-done.refs_5_.refs_0_.refs_2_.refs_6_ = bf16[272,3584]{1,0:T(8,128)(2,1)S(1)} collective-permute-done((bf16[272,3584]{1,0:T(8,128)(2,1)}, bf16[272,3584]{1,0:T(8,128)(2,1)S(1)}, u32[]{:S(2)}, u32[]{:S(2)}) %collective-permute-start) | collective-permute-done | bytes 1949728 | tf_op jit(solution)/shard_map/ppermute | solution.py:484
  52.9 2.4 %join_columns.2.refs_6_.refs_0_ = bf16[272,1792]{1,0:T(8,128)(2,1)} custom-call(s32[1]{0:T(128)} %constant.31.clone.1.scalar_ref, bf16[272,1792]{1,0:T(8,128)(2,1)} %collective-permute-done.2.refs_0_.refs_3_.refs_1_, bf16[272,1792]{1,0:T(8,128)(2,1)S(1)} %collective-permute-done.1.refs_1_.refs_2_, ...), custom_call_target="tpu_custom_call" | custom-call | flops 1 | bytes 1 | tf_op jit(solution)/shard_map/join_columns/pallas_call | solution.py:48
  55.3 1.7 collective-permute-start.10
  57.0 8.5 %collective-permute-start.6 = (bf16[320,1024]{1,0:T(8,128)(2,1)}, bf16[320,1024]{1,0:T(8,128)(2,1)}, u32[]{:S(2)}, u32[]{:S(2)}) collective-permute-start(bf16[320,1024]{1,0:T(8,128)(2,1)} %get-tuple-element.36.refs_2_.refs_4_.refs_3_), channel_id=1, source_target_pairs={{0,8},{12,4},{1,9},{13,5},{2,10},{14,6},{3,11},{15,7},{16,24},{28,... | collective-permute-start | bytes 1966088 | tf_op jit(solution)/shard_map/ppermute | solution.py:487
  65.5 1.5 collective-permute-start.7
  67.0 2.3 collective-permute-start.8
  70.0 13.5 %forward_rest.1 = (bf16[320,1024]{1,0:T(8,128)(2,1)}, bf16[640,512]{1,0:T(8,128)(2,1)}, bf16[640,512]{1,0:T(8,128)(2,1)}) custom-call(s32[3]{0:T(128)} %pad_add_fusion.1.scalar_ref, bf16[272,3584]{1,0:T(8,128)(2,1)} %copy-done.3, bf16[272,3584]{1,0:T(8,128)(2,1)} %collective-permute-done.5.refs_1_.refs_3_.refs_7_, bf16[640,1024]{1,0:T(8,128)(2,1)} %bitcast.48, ...), custom_call_target="tpu_custom_call" | custom-call | flops 1 | bytes 1 | tf_op jit(solution)/shard_map/forward_rest/pallas_call | solution.py:48
  83.5 1.5 copy-done.4
  85.0 4.3 %pick_rows.3.refs_3_.refs_0_ = bf16[1792,640]{1,0:T(8,128)(2,1)S(1)} custom-call(s32[3]{0:T(128)S(1)} %pad_add_fusion.3.scalar_ref, bf16[272,3584]{1,0:T(8,128)(2,1)} %get-tuple-element.26.refs_0_.refs_4_, bf16[272,3584]{1,0:T(8,128)(2,1)} %collective-permute-done.4.refs_1_.refs_5_, bf16[272,3584]{1,0:T(8,128)(2,1)S(1)} %copy-done.4, ...), custom_call_target="tpu_custom_call" | custom-call | flops 1 | bytes 1 | tf_op jit(solution)/shard_map/pick_rows/pallas_call | solution.py:48
  89.3 2.6 %join_columns.3.refs_9_.refs_0_ = bf16[272,2688]{1,0:T(8,128)(2,1)} custom-call(s32[1]{0:T(128)} %constant.31.clone.1.scalar_ref, bf16[272,896]{1,0:T(8,128)(2,1)S(1)} %collective-permute-done.3.refs_4_.refs_0_, bf16[272,1792]{1,0:T(8,128)(2,1)} %collective-permute-done.2.refs_0_.refs_3_.refs_1_, ...), custom_call_target="tpu_custom_call" | custom-call | flops 1 | bytes 1 | tf_op jit(solution)/shard_map/join_columns/pallas_call | solution.py:48
  92.0 1.3 collective-permute-done.8.refs_8_.refs_10_
  93.8 1.5 collective-permute-start.19
  95.3 6.1 %collective-permute-start.12 = (bf16[320,1024]{1,0:T(8,128)(2,1)}, bf16[320,1024]{1,0:T(8,128)(2,1)}, u32[]{:S(2)}, u32[]{:S(2)}) collective-permute-start(bf16[320,1024]{1,0:T(8,128)(2,1)} %get-tuple-element.41.refs_8_.refs_2_.refs_4_.refs_5_), channel_id=1, source_target_pairs={{0,8},{12,4},{1,9},{13,5},{2,10},{14,6},{3,11},{15,7},{16,24},{28,... | collective-permute-start | bytes 1966088 | tf_op jit(solution)/shard_map/ppermute | solution.py:487
  101.4 1.5 collective-permute-start.13
  102.9 0.9 copy-done.13
  103.8 2.2 collective-permute-start.14
  106.1 13.7 %slot_gradients.1 = (bf16[640,2048]{1,0:T(8,128)(2,1)}, bf16[640,1536]{1,0:T(8,128)(2,1)}) custom-call(s32[4]{0:T(128)} %pad_add_fusion.scalar_ref, bf16[3584,1024]{1,0:T(8,128)(2,1)} %bitcast.40, bf16[3584,1024]{1,0:T(8,128)(2,1)} %bitcast.44, bf16[320,1024]{1,0:T(8,128)(2,1)} %get-tuple-element.41.refs_8_.refs_2_.refs_4_.refs_5_, ...), custom_call_target="tpu_custom_call" | custom-call | flops 1 | bytes 1 | tf_op jit(solution)/shard_map/slot_gradients/pallas_call | solution.py:48
  119.8 3.7 %all-to-all-start = ((bf16[4,160,2048]{2,1,0:T(8,128)(2,1)}), bf16[4,160,2048]{2,1,0:T(8,128)(2,1)S(1)}, u32[]{:S(2)}, u32[]{:S(2)}) async-start(bf16[4,160,2048]{2,1,0:T(8,128)(2,1)} %bitcast.49), calls=%async_computation | async-start | bytes 5242880 | tf_op jit(solution)/shard_map/all_to_all | solution.py:490
  123.6 1.5 copy-done.8
  125.1 1.2 copy-done.14
  126.3 4.3 %pick_rows.4.refs_1_.refs_2_.refs_12_ = bf16[1792,640]{1,0:T(8,128)(2,1)S(1)} custom-call(s32[3]{0:T(128)S(1)} %pad_add_fusion.4.scalar_ref, bf16[272,1792]{1,0:T(8,128)(2,1)} %join_columns.2.refs_6_.refs_0_, bf16[272,1792]{1,0:T(8,128)(2,1)} %collective-permute-done.9.refs_1_, bf16[272,1792]{1,0:T(8,128)(2,1)} %collective-permute-done.10.refs_2_, ...), custom_call_target="tpu_custom_call" | custom-call | flops 1 | bytes 1 | tf_op jit(solution)/shard_map/pick_rows/pallas_call | solution.py:48
  130.6 1.4 copy-done.1
  132.7 2.9 %collective-permute-start.15 = (bf16[640,512]{1,0:T(8,128)(2,1)S(1)}, bf16[640,512]{1,0:T(8,128)(2,1)}, u32[]{:S(2)}, u32[]{:S(2)}) collective-permute-start(bf16[640,512]{1,0:T(8,128)(2,1)S(1)} %copy-done.17), channel_id=1, source_target_pairs={{0,8},{12,4},{1,9},{13,5},{2,10},{14,6},{3,11},{15,7},{16,24},{28,... | collective-permute-start | bytes 1966088 | tf_op jit(solution)/shard_map/ppermute | solution.py:487
  135.5 1.6 collective-permute-start.16
  137.1 2.1 collective-permute-start.17
  139.2 7.9 %for_end.3.refs_4_ = bf16[896,1024]{1,0:T(8,128)(2,1)} custom-call(s32[1]{0:T(128)} %constant.31.clone.1.scalar_ref, bf16[1792,640]{1,0:T(8,128)(2,1)} %copy-done.2, bf16[1792,640]{1,0:T(8,128)(2,1)} %copy-done.1, bf16[1792,640]{1,0:T(8,128)(2,1)} %copy-done.1, bf16[320,1024]{1,0:T(8,128)(2,1)} %get-tuple-element.36.refs_2_.refs_4_.refs_3_, ...), custom_call_target="tpu_custom_call" | custom-call | flops 1 | bytes 1 | tf_op jit(solution)/shard_map/for_end/pallas_call | solution.py:48
  147.1 1.5 collective-permute-start.26
  148.7 1.5 copy-done.9
  150.2 5.9 %pick_rows.5.refs_9_.refs_1_.refs_2_.refs_3_ = bf16[2688,640]{1,0:T(8,128)(2,1)S(1)} custom-call(s32[4]{0:T(128)S(1)} %pad_add_fusion.5.scalar_ref, bf16[272,2688]{1,0:T(8,128)(2,1)} %join_columns.3.refs_9_.refs_0_, bf16[272,2688]{1,0:T(8,128)(2,1)} %collective-permute-done.18.refs_1_, bf16[272,2688]{1,0:T(8,128)(2,1)} %collective-permute-done.19.refs_2_, ...), custom_call_target="tpu_custom_call" | custom-call | flops 1 | bytes 1 | tf_op jit(solution)/shard_map/pick_rows/pallas_call | solution.py:48
  156.1 1.7 copy-done
  157.8 5.2 %collective-permute-done.17.refs_8_.refs_7_ = bf16[640,512]{1,0:T(8,128)(2,1)} collective-permute-done((bf16[640,512]{1,0:T(8,128)(2,1)S(1)}, bf16[640,512]{1,0:T(8,128)(2,1)}, u32[]{:S(2)}, u32[]{:S(2)}) %collective-permute-start.17) | collective-permute-done | bytes 655392 | tf_op jit(solution)/shard_map/ppermute | solution.py:487
  162.9 1.5 copy-done.6
  164.5 4.4 %all-to-all-start.1 = ((bf16[4,160,1536]{2,1,0:T(8,128)(2,1)}), bf16[4,160,1536]{2,1,0:T(8,128)(2,1)}, u32[]{:S(2)}, u32[]{:S(2)}) async-start(bf16[4,160,1536]{2,1,0:T(8,128)(2,1)} %bitcast.33), calls=%async_computation.1 | async-start | bytes 3932160 | tf_op jit(solution)/shard_map/all_to_all | solution.py:490
  168.9 6.5 %collective-permute-start.22 = (bf16[640,512]{1,0:T(8,128)(2,1)}, bf16[640,512]{1,0:T(8,128)(2,1)}, u32[]{:S(2)}, u32[]{:S(2)}) collective-permute-start(bf16[640,512]{1,0:T(8,128)(2,1)} %get-tuple-element.46.refs_4_.refs_3_), channel_id=1, source_target_pairs={{0,8},{12,4},{1,9},{13,5},{2,10},{14,6},{3,11},{15,7},{16,24},{28,... | collective-permute-start | bytes 1966088 | tf_op jit(solution)/shard_map/ppermute | solution.py:487
  175.4 1.5 collective-permute-start.23
  176.9 2.3 collective-permute-start.24
  179.2 5.3 %for_end.4.refs_2_ = bf16[896,512]{1,0:T(8,128)(2,1)} custom-call(s32[1]{0:T(128)} %constant.31.clone.1.scalar_ref, bf16[1792,640]{1,0:T(8,128)(2,1)} %copy-done.2, bf16[1792,640]{1,0:T(8,128)(2,1)} %copy-done.1, bf16[1792,640]{1,0:T(8,128)(2,1)} %copy-done.1, bf16[640,512]{1,0:T(8,128)(2,1)} %get-tuple-element.42.refs_3_.refs_4_, ...), custom_call_target="tpu_custom_call" | custom-call | flops 1 | bytes 1 | tf_op jit(solution)/shard_map/for_end/pallas_call | solution.py:48
  184.4 2.1 combine.2.refs_13_
  186.6 1.6 collective-permute-start.21
  188.1 2.9 %collective-permute-done.26.refs_12_ = bf16[896,1024]{1,0:T(8,128)(2,1)} collective-permute-done((bf16[896,1024]{1,0:T(8,128)(2,1)}, bf16[896,1024]{1,0:T(8,128)(2,1)}, u32[]{:S(2)}, u32[]{:S(2)}) %collective-permute-start.26) | collective-permute-done | bytes 1835040 | tf_op jit(solution)/shard_map/ppermute | solution.py:499
  191.0 1.3 collective-permute-start.25
  192.3 9.8 %for_own.3.refs_9_ = bf16[896,1024]{1,0:T(8,128)(2,1)} custom-call(s32[1]{0:T(128)} %constant.31.clone.1.scalar_ref, bf16[1792,640]{1,0:T(8,128)(2,1)} %copy-done.2, bf16[2688,640]{1,0:T(8,128)(2,1)} %copy-done, bf16[2688,640]{1,0:T(8,128)(2,1)} %copy-done, bf16[2688,640]{1,0:T(8,128)(2,1)} %copy-done, ...), custom_call_target="tpu_custom_call" | custom-call | flops 1 | bytes 1 | tf_op jit(solution)/shard_map/for_own/pallas_call | solution.py:48
  202.2 1.3 collective-permute-done.24.refs_8_.refs_7_
  203.5 5.2 %for_end.5.refs_2_ = bf16[896,512]{1,0:T(8,128)(2,1)} custom-call(s32[1]{0:T(128)} %constant.31.clone.1.scalar_ref, bf16[1792,640]{1,0:T(8,128)(2,1)} %copy-done.2, bf16[1792,640]{1,0:T(8,128)(2,1)} %copy-done.1, bf16[1792,640]{1,0:T(8,128)(2,1)} %copy-done.1, bf16[640,512]{1,0:T(8,128)(2,1)} %get-tuple-element.46.refs_4_.refs_3_, ...), custom_call_target="tpu_custom_call" | custom-call | flops 1 | bytes 1 | tf_op jit(solution)/shard_map/for_end/pallas_call | solution.py:48
  208.8 1.3 collective-permute-start.28
  210.1 1.2 copy-done.11
  211.3 3.2 %combine.3.refs_9_ = bf16[256,1536]{1,0:T(8,128)(2,1)S(1)} custom-call(s32[1]{0:T(128)} %constant.31.clone.1.scalar_ref, s32[2,256]{1,0:T(2,128)S(1)} %bitcast.36, bf16[640,1536]{1,0:T(8,128)(2,1)} %bitcast.22.refs_1_, bf16[896,512]{1,0:T(8,128)(2,1)S(1)} %copy-done.11), custom_call_target="tpu_custom_call" | custom-call | flops 1 | bytes 1 | tf_op jit(solution)/shard_map/combine/pallas_call | solution.py:48
  214.5 1.6 collective-permute-start.27
  216.1 6.4 %for_own.4.refs_8_.refs_2_ = bf16[896,1024]{1,0:T(8,128)(2,1)} custom-call(s32[1]{0:T(128)} %constant.31.clone.1.scalar_ref, bf16[1792,640]{1,0:T(8,128)(2,1)} %copy-done.2, bf16[2688,640]{1,0:T(8,128)(2,1)} %copy-done, bf16[2688,640]{1,0:T(8,128)(2,1)} %copy-done, bf16[2688,640]{1,0:T(8,128)(2,1)} %copy-done, ...), custom_call_target="tpu_custom_call" | custom-call | flops 1 | bytes 1 | tf_op jit(solution)/shard_map/for_own/pallas_call | solution.py:48
  222.5 6.2 %for_own.5.refs_0_ = f32[896,512]{1,0:T(8,128)} custom-call(s32[1]{0:T(128)} %constant.31.clone.1.scalar_ref, bf16[1792,640]{1,0:T(8,128)(2,1)} %copy-done.2, bf16[2688,640]{1,0:T(8,128)(2,1)} %copy-done, bf16[2688,640]{1,0:T(8,128)(2,1)} %copy-done, bf16[2688,640]{1,0:T(8,128)(2,1)} %copy-done, bf16[640,512]{1,0:T(8,128)(2,1)} %get-tuple-element.46.refs_4_.refs_3_, ...), custom_call_target="tpu_custom_call" | custom-call | flops 1 | bytes 1 | tf_op jit(solution)/shard_map/for_own/pallas_call | solution.py:48
  228.7 5.3 %collective-permute-done.28.refs_1_ = bf16[896,512]{1,0:T(8,128)(2,1)} collective-permute-done((bf16[896,512]{1,0:T(8,128)(2,1)}, bf16[896,512]{1,0:T(8,128)(2,1)}, u32[]{:S(2)}, u32[]{:S(2)}) %collective-permute-start.28) | collective-permute-done | bytes 917536 | tf_op jit(solution)/shard_map/ppermute | solution.py:499
  234.1 2.8 %finish.1 = bf16[896,1024]{1,0:T(8,128)(2,1)} custom-call(s32[1]{0:T(128)} %constant.31.clone.1.scalar_ref, f32[896,512]{1,0:T(8,128)} %for_own.5.refs_0_, bf16[896,512]{1,0:T(8,128)(2,1)} %collective-permute-done.28.refs_1_, bf16[896,1024]{1,0:T(8,128)(2,1)} %for_own.4.refs_8_.refs_2_), custom_call_target="tpu_custom_call", output_to_operand_aliasing={{}: (3, {})} | custom-call | flops 1 | bytes 1 | tf_op jit(solution)/shard_map/finish/pallas_call | solution.py:48
  236.9 1.4 maximum_bitcast_fusion
  (61 shorter events, 3.3 us)
Async XLA Ops:
  0.7 1.5 copy-start.5
  2.2 0.7 copy-start.15
  6.5 12.6 %collective-permute-start.4 = (bf16[272,3584]{1,0:T(8,128)(2,1)}, bf16[272,3584]{1,0:T(8,128)(2,1)}, u32[]{:S(2)}, u32[]{:S(2)}) collective-permute-start(bf16[272,3584]{1,0:T(8,128)(2,1)} %get-tuple-element.26.refs_0_.refs_4_), channel_id=1, source_target_pairs={{0,1},{1,0},{2,3},{3,2},{4,5},{5,4},{6,7},{7,6},{8,9},{9,8},{10,11... | collective-permute-start | bytes 5849096 | tf_op jit(solution)/shard_map/ppermute | solution.py:481
  7.0 45.9 %collective-permute-start = (bf16[272,3584]{1,0:T(8,128)(2,1)}, bf16[272,3584]{1,0:T(8,128)(2,1)S(1)}, u32[]{:S(2)}, u32[]{:S(2)}) collective-permute-start(bf16[272,3584]{1,0:T(8,128)(2,1)} %get-tuple-element.26.refs_0_.refs_4_), channel_id=1, source_target_pairs={{0,2},{1,3},{2,0},{3,1},{4,6},{5,7},{6,4},{7,5},{8,10},{9,11},{10,... | collective-permute-start | bytes 5849096 | tf_op jit(solution)/shard_map/ppermute | solution.py:484
  9.5 36.5 %collective-permute-start.1 = (bf16[272,1792]{1,0:T(8,128)(2,1)}, bf16[272,1792]{1,0:T(8,128)(2,1)S(1)}, u32[]{:S(2)}, u32[]{:S(2)}) collective-permute-start(bf16[272,1792]{1,0:T(8,128)(2,1)} %get-tuple-element.27), channel_id=1, source_target_pairs={{0,8},{12,4},{1,9},{13,5},{2,10},{14,6},{3,11},{15,7},{16,24},{28,... | collective-permute-start | bytes 2924552 | tf_op jit(solution)/shard_map/ppermute | solution.py:487
  14.1 32.0 %collective-permute-start.2 = (bf16[272,1792]{1,0:T(8,128)(2,1)}, bf16[272,1792]{1,0:T(8,128)(2,1)}, u32[]{:S(2)}, u32[]{:S(2)}) collective-permute-start(bf16[272,1792]{1,0:T(8,128)(2,1)} %get-tuple-element.28), channel_id=1, source_target_pairs={{4,8},{8,4},{5,9},{9,5},{6,10},{10,6},{7,11},{11,7},{20,24},{24,20... | collective-permute-start | bytes 2924552 | tf_op jit(solution)/shard_map/ppermute | solution.py:487
  15.7 30.3 %collective-permute-start.3 = (bf16[272,896]{1,0:T(8,128)(2,1)}, bf16[272,896]{1,0:T(8,128)(2,1)S(1)}, u32[]{:S(2)}, u32[]{:S(2)}) collective-permute-start(bf16[272,896]{1,0:T(8,128)(2,1)} %get-tuple-element.29), channel_id=1, source_target_pairs={{0,4},{12,8},{1,5},{13,9},{2,6},{14,10},{3,7},{15,11},{16,20},{28,... | collective-permute-start | bytes 1462280 | tf_op jit(solution)/shard_map/ppermute | solution.py:487
  52.9 2.4 %copy-start.3 = (bf16[272,3584]{1,0:T(8,128)(2,1)}, bf16[272,3584]{1,0:T(8,128)(2,1)S(1)}, u32[]{:S(2)}) copy-start(bf16[272,3584]{1,0:T(8,128)(2,1)S(1)} %collective-permute-done.refs_5_.refs_0_.refs_2_.refs_6_) | copy-start | bytes 5849092
  52.9 17.1 %collective-permute-start.5 = (bf16[272,3584]{1,0:T(8,128)(2,1)S(1)}, bf16[272,3584]{1,0:T(8,128)(2,1)}, u32[]{:S(2)}, u32[]{:S(2)}) collective-permute-start(bf16[272,3584]{1,0:T(8,128)(2,1)S(1)} %collective-permute-done.refs_5_.refs_0_.refs_2_.refs_6_), channel_id=1, source_target_pairs={{0,1},{1,0},{2,3},{3,2},{4,5},{5,4},{6,7},{7,6},{8,9},{9,8},{10,11... | collective-permute-start | bytes 5849096 | tf_op jit(solution)/shard_map/ppermute | solution.py:481
  55.3 38.0 %collective-permute-start.10 = (bf16[272,1792]{1,0:T(8,128)(2,1)}, bf16[272,1792]{1,0:T(8,128)(2,1)}, u32[]{:S(2)}, u32[]{:S(2)}) collective-permute-start(bf16[272,1792]{1,0:T(8,128)(2,1)} %join_columns.2.refs_6_.refs_0_), channel_id=1, source_target_pairs={{0,2},{1,3},{2,0},{3,1},{4,6},{5,7},{6,4},{7,5},{8,10},{9,11},{10,... | collective-permute-start | bytes 2924552 | tf_op jit(solution)/shard_map/ppermute | solution.py:484
  57.0 34.9 %collective-permute-start.6 = (bf16[320,1024]{1,0:T(8,128)(2,1)}, bf16[320,1024]{1,0:T(8,128)(2,1)}, u32[]{:S(2)}, u32[]{:S(2)}) collective-permute-start(bf16[320,1024]{1,0:T(8,128)(2,1)} %get-tuple-element.36.refs_2_.refs_4_.refs_3_), channel_id=1, source_target_pairs={{0,8},{12,4},{1,9},{13,5},{2,10},{14,6},{3,11},{15,7},{16,24},{28,... | collective-permute-start | bytes 1966088 | tf_op jit(solution)/shard_map/ppermute | solution.py:487
  65.5 26.4 %collective-permute-start.7 = (bf16[320,1024]{1,0:T(8,128)(2,1)}, bf16[320,1024]{1,0:T(8,128)(2,1)}, u32[]{:S(2)}, u32[]{:S(2)}) collective-permute-start(bf16[320,1024]{1,0:T(8,128)(2,1)} %get-tuple-element.36.refs_2_.refs_4_.refs_3_), channel_id=1, source_target_pairs={{4,8},{8,4},{5,9},{9,5},{6,10},{10,6},{7,11},{11,7},{20,24},{24,20... | collective-permute-start | bytes 1966088 | tf_op jit(solution)/shard_map/ppermute | solution.py:487
  67.0 26.2 %collective-permute-start.8 = (bf16[320,1024]{1,0:T(8,128)(2,1)}, bf16[320,1024]{1,0:T(8,128)(2,1)}, u32[]{:S(2)}, u32[]{:S(2)}) collective-permute-start(bf16[320,1024]{1,0:T(8,128)(2,1)} %get-tuple-element.36.refs_2_.refs_4_.refs_3_), channel_id=1, source_target_pairs={{0,4},{12,8},{1,5},{13,9},{2,6},{14,10},{3,7},{15,11},{16,20},{28,... | collective-permute-start | bytes 1966088 | tf_op jit(solution)/shard_map/ppermute | solution.py:487
  83.5 1.5 copy-start.4
  89.3 2.6 %copy-start.2 = (bf16[1792,640]{1,0:T(8,128)(2,1)}, bf16[1792,640]{1,0:T(8,128)(2,1)S(1)}, u32[]{:S(2)}) copy-start(bf16[1792,640]{1,0:T(8,128)(2,1)S(1)} %pick_rows.3.refs_3_.refs_0_) | copy-start | bytes 6881284
  93.3 9.7 %collective-permute-start.11 = (bf16[272,1792]{1,0:T(8,128)(2,1)}, bf16[272,1792]{1,0:T(8,128)(2,1)S(1)}, u32[]{:S(2)}, u32[]{:S(2)}) collective-permute-start(bf16[272,1792]{1,0:T(8,128)(2,1)} %collective-permute-done.10.refs_2_), channel_id=1, source_target_pairs={{0,1},{1,0},{2,3},{3,2},{4,5},{5,4},{6,7},{7,6},{8,9},{9,8},{10,11... | collective-permute-start | bytes 2924552 | tf_op jit(solution)/shard_map/ppermute | solution.py:481
  93.3 30.3 %collective-permute-start.9 = (bf16[272,1792]{1,0:T(8,128)(2,1)}, bf16[272,1792]{1,0:T(8,128)(2,1)}, u32[]{:S(2)}, u32[]{:S(2)}) collective-permute-start(bf16[272,1792]{1,0:T(8,128)(2,1)} %join_columns.2.refs_6_.refs_0_), channel_id=1, source_target_pairs={{0,1},{1,0},{2,3},{3,2},{4,5},{5,4},{6,7},{7,6},{8,9},{9,8},{10,11... | collective-permute-start | bytes 2924552 | tf_op jit(solution)/shard_map/ppermute | solution.py:481
  93.8 38.8 %collective-permute-start.19 = (bf16[272,2688]{1,0:T(8,128)(2,1)}, bf16[272,2688]{1,0:T(8,128)(2,1)}, u32[]{:S(2)}, u32[]{:S(2)}) collective-permute-start(bf16[272,2688]{1,0:T(8,128)(2,1)} %join_columns.3.refs_9_.refs_0_), channel_id=1, source_target_pairs={{0,2},{1,3},{2,0},{3,1},{4,6},{5,7},{6,4},{7,5},{8,10},{9,11},{10,... | collective-permute-start | bytes 4386824 | tf_op jit(solution)/shard_map/ppermute | solution.py:484
  95.3 36.7 %collective-permute-start.12 = (bf16[320,1024]{1,0:T(8,128)(2,1)}, bf16[320,1024]{1,0:T(8,128)(2,1)}, u32[]{:S(2)}, u32[]{:S(2)}) collective-permute-start(bf16[320,1024]{1,0:T(8,128)(2,1)} %get-tuple-element.41.refs_8_.refs_2_.refs_4_.refs_5_), channel_id=1, source_target_pairs={{0,8},{12,4},{1,9},{13,5},{2,10},{14,6},{3,11},{15,7},{16,24},{28,... | collective-permute-start | bytes 1966088 | tf_op jit(solution)/shard_map/ppermute | solution.py:487
  101.4 30.6 %collective-permute-start.13 = (bf16[320,1024]{1,0:T(8,128)(2,1)}, bf16[320,1024]{1,0:T(8,128)(2,1)}, u32[]{:S(2)}, u32[]{:S(2)}) collective-permute-start(bf16[320,1024]{1,0:T(8,128)(2,1)} %get-tuple-element.41.refs_8_.refs_2_.refs_4_.refs_5_), channel_id=1, source_target_pairs={{4,8},{8,4},{5,9},{9,5},{6,10},{10,6},{7,11},{11,7},{20,24},{24,20... | collective-permute-start | bytes 1966088 | tf_op jit(solution)/shard_map/ppermute | solution.py:487
  102.9 0.9 copy-start.13
  103.8 28.2 %collective-permute-start.14 = (bf16[320,1024]{1,0:T(8,128)(2,1)}, bf16[320,1024]{1,0:T(8,128)(2,1)}, u32[]{:S(2)}, u32[]{:S(2)}) collective-permute-start(bf16[320,1024]{1,0:T(8,128)(2,1)} %get-tuple-element.41.refs_8_.refs_2_.refs_4_.refs_5_), channel_id=1, source_target_pairs={{0,4},{12,8},{1,5},{13,9},{2,6},{14,10},{3,7},{15,11},{16,20},{28,... | collective-permute-start | bytes 1966088 | tf_op jit(solution)/shard_map/ppermute | solution.py:487
  119.8 43.1 %all-to-all-start = ((bf16[4,160,2048]{2,1,0:T(8,128)(2,1)}), bf16[4,160,2048]{2,1,0:T(8,128)(2,1)S(1)}, u32[]{:S(2)}, u32[]{:S(2)}) async-start(bf16[4,160,2048]{2,1,0:T(8,128)(2,1)} %bitcast.49), calls=%async_computation | async-start | bytes 5242880 | tf_op jit(solution)/shard_map/all_to_all | solution.py:490
  123.6 1.5 copy-start.8
  125.1 1.2 copy-start.14
  126.3 6.3 %copy-start.17 = (bf16[640,512]{1,0:T(8,128)(2,1)S(1)}, bf16[640,512]{1,0:T(8,128)(2,1)}, u32[]{:S(2)}) copy-start(bf16[640,512]{1,0:T(8,128)(2,1)} %get-tuple-element.42.refs_3_.refs_4_) | copy-start | bytes 1966084
  130.6 1.4 copy-start.1
  132.0 15.1 %collective-permute-start.18 = (bf16[272,2688]{1,0:T(8,128)(2,1)}, bf16[272,2688]{1,0:T(8,128)(2,1)}, u32[]{:S(2)}, u32[]{:S(2)}) collective-permute-start(bf16[272,2688]{1,0:T(8,128)(2,1)} %join_columns.3.refs_9_.refs_0_), channel_id=1, source_target_pairs={{0,1},{1,0},{2,3},{3,2},{4,5},{5,4},{6,7},{7,6},{8,9},{9,8},{10,11... | collective-permute-start | bytes 4386824 | tf_op jit(solution)/shard_map/ppermute | solution.py:481
  132.6 16.1 %collective-permute-start.20 = (bf16[272,2688]{1,0:T(8,128)(2,1)}, bf16[272,2688]{1,0:T(8,128)(2,1)}, u32[]{:S(2)}, u32[]{:S(2)}) collective-permute-start(bf16[272,2688]{1,0:T(8,128)(2,1)} %collective-permute-done.19.refs_2_), channel_id=1, source_target_pairs={{0,1},{1,0},{2,3},{3,2},{4,5},{5,4},{6,7},{7,6},{8,9},{9,8},{10,11... | collective-permute-start | bytes 4386824 | tf_op jit(solution)/shard_map/ppermute | solution.py:481
  132.7 25.1 %collective-permute-start.15 = (bf16[640,512]{1,0:T(8,128)(2,1)S(1)}, bf16[640,512]{1,0:T(8,128)(2,1)}, u32[]{:S(2)}, u32[]{:S(2)}) collective-permute-start(bf16[640,512]{1,0:T(8,128)(2,1)S(1)} %copy-done.17), channel_id=1, source_target_pairs={{0,8},{12,4},{1,9},{13,5},{2,10},{14,6},{3,11},{15,7},{16,24},{28,... | collective-permute-start | bytes 1966088 | tf_op jit(solution)/shard_map/ppermute | solution.py:487
  135.5 22.3 %collective-permute-start.16 = (bf16[640,512]{1,0:T(8,128)(2,1)S(1)}, bf16[640,512]{1,0:T(8,128)(2,1)}, u32[]{:S(2)}, u32[]{:S(2)}) collective-permute-start(bf16[640,512]{1,0:T(8,128)(2,1)S(1)} %copy-done.17), channel_id=1, source_target_pairs={{4,8},{8,4},{5,9},{9,5},{6,10},{10,6},{7,11},{11,7},{20,24},{24,20... | collective-permute-start | bytes 1966088 | tf_op jit(solution)/shard_map/ppermute | solution.py:487
  137.1 25.8 %collective-permute-start.17 = (bf16[640,512]{1,0:T(8,128)(2,1)S(1)}, bf16[640,512]{1,0:T(8,128)(2,1)}, u32[]{:S(2)}, u32[]{:S(2)}) collective-permute-start(bf16[640,512]{1,0:T(8,128)(2,1)S(1)} %copy-done.17), channel_id=1, source_target_pairs={{0,4},{12,8},{1,5},{13,9},{2,6},{14,10},{3,7},{15,11},{16,20},{28,... | collective-permute-start | bytes 1966088 | tf_op jit(solution)/shard_map/ppermute | solution.py:487
  147.1 43.9 %collective-permute-start.26 = (bf16[896,1024]{1,0:T(8,128)(2,1)}, bf16[896,1024]{1,0:T(8,128)(2,1)}, u32[]{:S(2)}, u32[]{:S(2)}) collective-permute-start(bf16[896,1024]{1,0:T(8,128)(2,1)} %for_end.3.refs_4_), channel_id=1, source_target_pairs={{4,0},{8,12},{5,1},{9,13},{6,2},{10,14},{7,3},{11,15},{20,16},{24,... | collective-permute-start | bytes 5505032 | tf_op jit(solution)/shard_map/ppermute | solution.py:499
  148.7 1.5 copy-start.9
  156.1 1.7 copy-start
  162.9 1.5 copy-start.6
  164.5 45.6 %all-to-all-start.1 = ((bf16[4,160,1536]{2,1,0:T(8,128)(2,1)}), bf16[4,160,1536]{2,1,0:T(8,128)(2,1)}, u32[]{:S(2)}, u32[]{:S(2)}) async-start(bf16[4,160,1536]{2,1,0:T(8,128)(2,1)} %bitcast.33), calls=%async_computation.1 | async-start | bytes 3932160 | tf_op jit(solution)/shard_map/all_to_all | solution.py:490
  168.9 15.5 %copy-start.7 = (bf16[4,160,2048]{2,1,0:T(8,128)(2,1)S(1)}, bf16[4,160,2048]{2,1,0:T(8,128)(2,1)}, u32[]{:S(2)}) copy-start(bf16[4,160,2048]{2,1,0:T(8,128)(2,1)} %copy-done.6) | copy-start | bytes 7864324
  168.9 15.5 %copy-start.16 = (s32[1,256,2]{1,2,0:T(2,128)S(1)}, s32[1,256,2]{1,2,0:T(2,128)}, u32[]{:S(2)}) copy-start(s32[1,256,2]{1,2,0:T(2,128)} %param.6) | copy-start | bytes 6148
  168.9 33.2 %collective-permute-start.22 = (bf16[640,512]{1,0:T(8,128)(2,1)}, bf16[640,512]{1,0:T(8,128)(2,1)}, u32[]{:S(2)}, u32[]{:S(2)}) collective-permute-start(bf16[640,512]{1,0:T(8,128)(2,1)} %get-tuple-element.46.refs_4_.refs_3_), channel_id=1, source_target_pairs={{0,8},{12,4},{1,9},{13,5},{2,10},{14,6},{3,11},{15,7},{16,24},{28,... | collective-permute-start | bytes 1966088 | tf_op jit(solution)/shard_map/ppermute | solution.py:487
  175.4 26.8 %collective-permute-start.23 = (bf16[640,512]{1,0:T(8,128)(2,1)}, bf16[640,512]{1,0:T(8,128)(2,1)}, u32[]{:S(2)}, u32[]{:S(2)}) collective-permute-start(bf16[640,512]{1,0:T(8,128)(2,1)} %get-tuple-element.46.refs_4_.refs_3_), channel_id=1, source_target_pairs={{4,8},{8,4},{5,9},{9,5},{6,10},{10,6},{7,11},{11,7},{20,24},{24,20... | collective-permute-start | bytes 1966088 | tf_op jit(solution)/shard_map/ppermute | solution.py:487
  176.9 26.7 %collective-permute-start.24 = (bf16[640,512]{1,0:T(8,128)(2,1)}, bf16[640,512]{1,0:T(8,128)(2,1)}, u32[]{:S(2)}, u32[]{:S(2)}) collective-permute-start(bf16[640,512]{1,0:T(8,128)(2,1)} %get-tuple-element.46.refs_4_.refs_3_), channel_id=1, source_target_pairs={{0,4},{12,8},{1,5},{13,9},{2,6},{14,10},{3,7},{15,11},{16,20},{28,... | collective-permute-start | bytes 1966088 | tf_op jit(solution)/shard_map/ppermute | solution.py:487
  186.6 5.8 %copy-start.10 = (bf16[256,2048]{1,0:T(8,128)(2,1)}, bf16[256,2048]{1,0:T(8,128)(2,1)S(1)}, u32[]{:S(2)}) copy-start(bf16[256,2048]{1,0:T(8,128)(2,1)S(1)} %combine.2.refs_13_) | copy-start | bytes 3145732
  186.6 42.2 %collective-permute-start.21 = (bf16[256,2048]{1,0:T(8,128)(2,1)S(1)}, bf16[256,2048]{1,0:T(8,128)(2,1)S(1)}, u32[]{:S(2)}, u32[]{:S(2)}) collective-permute-start(bf16[256,2048]{1,0:T(8,128)(2,1)S(1)} %combine.2.refs_13_), channel_id=1, source_target_pairs={{0,16},{16,0},{1,17},{17,1},{2,18},{18,2},{3,19},{19,3},{4,20},{20... | collective-permute-start | bytes 3145736 | tf_op jit(solution)/shard_map/ppermute | solution.py:496
  191.0 25.0 %collective-permute-start.25 = (bf16[896,512]{1,0:T(8,128)(2,1)}, bf16[896,512]{1,0:T(8,128)(2,1)}, u32[]{:S(2)}, u32[]{:S(2)}) collective-permute-start(bf16[896,512]{1,0:T(8,128)(2,1)} %for_end.4.refs_2_), channel_id=1, source_target_pairs={{4,0},{8,12},{5,1},{9,13},{6,2},{10,14},{7,3},{11,15},{20,16},{24,... | collective-permute-start | bytes 2752520 | tf_op jit(solution)/shard_map/ppermute | solution.py:499
  208.8 25.3 %collective-permute-start.28 = (bf16[896,512]{1,0:T(8,128)(2,1)}, bf16[896,512]{1,0:T(8,128)(2,1)}, u32[]{:S(2)}, u32[]{:S(2)}) collective-permute-start(bf16[896,512]{1,0:T(8,128)(2,1)} %for_end.5.refs_2_), channel_id=1, source_target_pairs={{4,0},{8,12},{5,1},{9,13},{6,2},{10,14},{7,3},{11,15},{20,16},{24,... | collective-permute-start | bytes 2752520 | tf_op jit(solution)/shard_map/ppermute | solution.py:499
  210.1 1.2 copy-start.11
  214.5 1.6 copy-start.12
  214.5 22.4 %collective-permute-start.27 = (bf16[256,1536]{1,0:T(8,128)(2,1)S(1)}, bf16[256,1536]{1,0:T(8,128)(2,1)S(1)}, u32[]{:S(2)}, u32[]{:S(2)}) collective-permute-start(bf16[256,1536]{1,0:T(8,128)(2,1)S(1)} %combine.3.refs_9_), channel_id=1, source_target_pairs={{0,16},{16,0},{1,17},{17,1},{2,18},{18,2},{3,19},{19,3},{4,20},{20... | collective-permute-start | bytes 2359304 | tf_op jit(solution)/shard_map/ppermute | solution.py:496

commit v6 on v5

--- a/solution.py
+++ b/solution.py
@@ -115,7 +115,7 @@
         held = jnp.concatenate([ins[0][...].astype(F32), jnp.zeros((ROUTE_ROWS - 2, token_count), F32)], axis=0)
         for i, o in zip(ins[1:], outs):
             o[:token_count] = i[...]
-            o[token_count:] = jnp.zeros((ROUTE_ROWS, block), BF16)
+            o[token_count:] = jnp.zeros((ROUTE_ROWS, o.shape[1]), BF16)
             o[token_count:, :token_count] = held.astype(BF16)
 
     def from_block(k):
@@ -128,17 +128,15 @@
         "cut_columns",
         scalars,
         [pair] + [rows] * (count + 1),
-        [whole(pair.shape), pl.BlockSpec((token_count, block), lambda j, s: (0, j))]
+        [whole(pair.shape), pl.BlockSpec((token_count, width // 2), lambda j, s: (0, j))]
         + [pl.BlockSpec((token_count, block), from_block(k)) for k in range(count)],
         [((lines, width), BF16)] + [((lines, block * (1 if k == 0 else 2)), BF16) for k in range(count)],
-        [pl.BlockSpec((lines, block), lambda j, s: (0, j))]
+        [pl.BlockSpec((lines, width // 2), lambda j, s: (0, j))]
         + [
-            pl.BlockSpec(
-                (lines, block), (lambda j, s: (0, 0)) if k == 0 else (lambda j, s: (0, jnp.minimum(j, 1)))
-            )
+            pl.BlockSpec((lines, block), (lambda j, s: (0, 0)) if k == 0 else (lambda j, s: (0, j)))
             for k in range(count)
         ],
-        (groups,),
+        (2,),
     )
 
 

time: 240 us -> 239 us (level)
  no operation moved by 1% of the time
where the time goes in v6:
time: 239 us; the launch traced here: 238 us
  Pallas kernels  124 us (52%)
  starting transfers between devices  69.8 us (29%)
  waiting for transfers between devices  24.6 us (10%)
  local copies, waits for them, and re-layouts  14.8 us (6%)
  other arithmetic  3.5 us (1%)
    pallas_call x19, Pallas kernels, call(): pl.pallas_call(kernel, name=name, out_shape=[jax.ShapeDtypeStruct(shape,...  124 us
    ppermute x15, starting transfers between devices, over_groups(): return lax.ppermute(value, 'dp', pairs)  47.2 us
    unnamed x36, local copies, waits for them, and re-layouts  14.8 us
    ppermute x15, waiting for transfers between devices, over_groups(): return lax.ppermute(value, 'dp', pairs)  9.5 us
    ppermute x3, waiting for transfers between devices, to_ends(): return lax.ppermute(value, 'dp', [(1, 0), (groups - 2, groups - 1)])  8.25 us
    all_to_all x2, starting transfers between devices, to_sources(): lax.all_to_all(value.reshape(experts, capacity, value.shape[1]), 'expert'...  8.07 us
    ppermute x3, waiting for transfers between devices, shift(): lax.ppermute(value, 'expert', [(s, (s + 2 * by) % experts) for s in range...  6.84 us
    ppermute x3, starting transfers between devices, shift(): lax.ppermute(value, 'expert', [(s, (s + 2 * by) % experts) for s in range...  5.78 us
  transfers between devices with their start and end apart: 31, of which 7 were waited for; matrix products, arithmetic and copies ran while one was open for 1% of the time, Pallas kernels for 51%

profile of v6, /device:TPU:0, one launch (start us, length us, event | category | flops | bytes accessed | tf_op | source)
XLA Modules:
  0.0 237.7 jit_solution(9869899623878377017)
XLA Ops:
  0.8 1.5 copy-done.5
  2.3 0.7 copy-done.15
  2.9 3.1 %cut_columns.1 = (bf16[272,3584]{1,0:T(8,128)(2,1)}, bf16[272,896]{1,0:T(8,128)(2,1)}, bf16[272,1792]{1,0:T(8,128)(2,1)}, bf16[272,1792]{1,0:T(8,128)(2,1)}) custom-call(s32[5]{0:T(128)S(1)} %stack.82.scalar_ref, s32[2,256]{1,0:T(2,128)S(1)} %bitcast.34, bf16[256,3584]{1,0:T(8,128)(2,1)S(1)} %bitcast.27, bf16[256,3584]{1,0:T(8,128)(2,1)S(1)} %bitcast.28, ...), custom_call_target="tpu_custom_call" | custom-call | flops 1 | bytes 1 | tf_op jit(solution)/shard_map/cut_columns/pallas_call | solution.py:48
  6.4 2.5 %collective-permute-start = (bf16[272,3584]{1,0:T(8,128)(2,1)}, bf16[272,3584]{1,0:T(8,128)(2,1)S(1)}, u32[]{:S(2)}, u32[]{:S(2)}) collective-permute-start(bf16[272,3584]{1,0:T(8,128)(2,1)} %get-tuple-element.26.refs_0_.refs_4_), channel_id=1, source_target_pairs={{0,2},{1,3},{2,0},{3,1},{4,6},{5,7},{6,4},{7,5},{8,10},{9,11},{10,... | collective-permute-start | bytes 5849096 | tf_op jit(solution)/shard_map/ppermute | solution.py:482
  9.0 4.5 %collective-permute-start.1 = (bf16[272,1792]{1,0:T(8,128)(2,1)}, bf16[272,1792]{1,0:T(8,128)(2,1)S(1)}, u32[]{:S(2)}, u32[]{:S(2)}) collective-permute-start(bf16[272,1792]{1,0:T(8,128)(2,1)} %get-tuple-element.27), channel_id=1, source_target_pairs={{0,8},{12,4},{1,9},{13,5},{2,10},{14,6},{3,11},{15,7},{16,24},{28,... | collective-permute-start | bytes 2924552 | tf_op jit(solution)/shard_map/ppermute | solution.py:485
  13.5 1.6 collective-permute-start.2
  15.1 2.1 collective-permute-start.3
  17.9 0.7 pad_add_fusion.scalar_ref
  18.6 13.2 %forward_first.1 = (bf16[320,1024]{1,0:T(8,128)(2,1)}, bf16[320,1024]{1,0:T(8,128)(2,1)}) custom-call(s32[3]{0:T(128)} %pad_add_fusion.2.scalar_ref, bf16[272,3584]{1,0:T(8,128)(2,1)} %get-tuple-element.26.refs_0_.refs_4_, bf16[272,3584]{1,0:T(8,128)(2,1)} %collective-permute-done.4.refs_1_.refs_5_, bf16[640,1024]{1,0:T(8,128)(2,1)} %bitcast.47, ...), custom_call_target="tpu_custom_call" | custom-call | flops 1 | bytes 1 | tf_op jit(solution)/shard_map/forward_first/pallas_call | solution.py:48
  31.8 12.0 %near_gradients.1.refs_5_ = bf16[320,3584]{1,0:T(8,128)(2,1)} custom-call(s32[4]{0:T(128)} %pad_add_fusion.scalar_ref, bf16[3584,1024]{1,0:T(8,128)(2,1)} %bitcast.38, bf16[3584,1024]{1,0:T(8,128)(2,1)} %bitcast.42, bf16[320,1024]{1,0:T(8,128)(2,1)} %get-tuple-element.36.refs_2_.refs_4_.refs_3_, bf16[320,1024]{1,0:T(8,128)(2,1)} %get-tuple-element.31.refs_3_.refs_5_, ...), custom_call_target="tpu_custom_call" | custom-call | flops 1 | bytes 1 | tf_op jit(solution)/shard_map/near_gradients/pallas_call | solution.py:48
  43.8 1.7 collective-permute-done.3.refs_4_.refs_0_
  45.5 6.8 %collective-permute-done.refs_5_.refs_0_.refs_2_.refs_6_ = bf16[272,3584]{1,0:T(8,128)(2,1)S(1)} collective-permute-done((bf16[272,3584]{1,0:T(8,128)(2,1)}, bf16[272,3584]{1,0:T(8,128)(2,1)S(1)}, u32[]{:S(2)}, u32[]{:S(2)}) %collective-permute-start) | collective-permute-done | bytes 1949728 | tf_op jit(solution)/shard_map/ppermute | solution.py:482
  52.3 2.4 %join_columns.2.refs_6_.refs_0_ = bf16[272,1792]{1,0:T(8,128)(2,1)} custom-call(s32[1]{0:T(128)} %constant.31.clone.1.scalar_ref, bf16[272,1792]{1,0:T(8,128)(2,1)} %collective-permute-done.2.refs_0_.refs_3_.refs_1_, bf16[272,1792]{1,0:T(8,128)(2,1)S(1)} %collective-permute-done.1.refs_1_.refs_2_, ...), custom_call_target="tpu_custom_call" | custom-call | flops 1 | bytes 1 | tf_op jit(solution)/shard_map/join_columns/pallas_call | solution.py:48
  54.7 1.7 collective-permute-start.10
  56.5 8.5 %collective-permute-start.6 = (bf16[320,1024]{1,0:T(8,128)(2,1)}, bf16[320,1024]{1,0:T(8,128)(2,1)}, u32[]{:S(2)}, u32[]{:S(2)}) collective-permute-start(bf16[320,1024]{1,0:T(8,128)(2,1)} %get-tuple-element.36.refs_2_.refs_4_.refs_3_), channel_id=1, source_target_pairs={{0,8},{12,4},{1,9},{13,5},{2,10},{14,6},{3,11},{15,7},{16,24},{28,... | collective-permute-start | bytes 1966088 | tf_op jit(solution)/shard_map/ppermute | solution.py:485
  65.0 1.5 collective-permute-start.7
  66.5 2.3 collective-permute-start.8
  69.4 13.5 %forward_rest.1 = (bf16[320,1024]{1,0:T(8,128)(2,1)}, bf16[640,512]{1,0:T(8,128)(2,1)}, bf16[640,512]{1,0:T(8,128)(2,1)}) custom-call(s32[3]{0:T(128)} %pad_add_fusion.1.scalar_ref, bf16[272,3584]{1,0:T(8,128)(2,1)} %copy-done.3, bf16[272,3584]{1,0:T(8,128)(2,1)} %collective-permute-done.5.refs_1_.refs_3_.refs_7_, bf16[640,1024]{1,0:T(8,128)(2,1)} %bitcast.48, ...), custom_call_target="tpu_custom_call" | custom-call | flops 1 | bytes 1 | tf_op jit(solution)/shard_map/forward_rest/pallas_call | solution.py:48
  82.9 1.5 copy-done.4
  84.4 4.3 %pick_rows.3.refs_3_.refs_0_ = bf16[1792,640]{1,0:T(8,128)(2,1)S(1)} custom-call(s32[3]{0:T(128)S(1)} %pad_add_fusion.3.scalar_ref, bf16[272,3584]{1,0:T(8,128)(2,1)} %get-tuple-element.26.refs_0_.refs_4_, bf16[272,3584]{1,0:T(8,128)(2,1)} %collective-permute-done.4.refs_1_.refs_5_, bf16[272,3584]{1,0:T(8,128)(2,1)S(1)} %copy-done.4, ...), custom_call_target="tpu_custom_call" | custom-call | flops 1 | bytes 1 | tf_op jit(solution)/shard_map/pick_rows/pallas_call | solution.py:48
  88.8 2.6 %join_columns.3.refs_9_.refs_0_ = bf16[272,2688]{1,0:T(8,128)(2,1)} custom-call(s32[1]{0:T(128)} %constant.31.clone.1.scalar_ref, bf16[272,896]{1,0:T(8,128)(2,1)S(1)} %collective-permute-done.3.refs_4_.refs_0_, bf16[272,1792]{1,0:T(8,128)(2,1)} %collective-permute-done.2.refs_0_.refs_3_.refs_1_, ...), custom_call_target="tpu_custom_call" | custom-call | flops 1 | bytes 1 | tf_op jit(solution)/shard_map/join_columns/pallas_call | solution.py:48
  91.4 1.3 collective-permute-done.8.refs_8_.refs_10_
  93.2 1.5 collective-permute-start.19
  94.7 6.1 %collective-permute-start.12 = (bf16[320,1024]{1,0:T(8,128)(2,1)}, bf16[320,1024]{1,0:T(8,128)(2,1)}, u32[]{:S(2)}, u32[]{:S(2)}) collective-permute-start(bf16[320,1024]{1,0:T(8,128)(2,1)} %get-tuple-element.41.refs_8_.refs_2_.refs_4_.refs_5_), channel_id=1, source_target_pairs={{0,8},{12,4},{1,9},{13,5},{2,10},{14,6},{3,11},{15,7},{16,24},{28,... | collective-permute-start | bytes 1966088 | tf_op jit(solution)/shard_map/ppermute | solution.py:485
  100.8 1.5 collective-permute-start.13
  102.4 0.9 copy-done.13
  103.3 2.2 collective-permute-start.14
  105.5 13.7 %slot_gradients.1 = (bf16[640,2048]{1,0:T(8,128)(2,1)}, bf16[640,1536]{1,0:T(8,128)(2,1)}) custom-call(s32[4]{0:T(128)} %pad_add_fusion.scalar_ref, bf16[3584,1024]{1,0:T(8,128)(2,1)} %bitcast.40, bf16[3584,1024]{1,0:T(8,128)(2,1)} %bitcast.44, bf16[320,1024]{1,0:T(8,128)(2,1)} %get-tuple-element.41.refs_8_.refs_2_.refs_4_.refs_5_, ...), custom_call_target="tpu_custom_call" | custom-call | flops 1 | bytes 1 | tf_op jit(solution)/shard_map/slot_gradients/pallas_call | solution.py:48
  119.3 3.7 %all-to-all-start = ((bf16[4,160,2048]{2,1,0:T(8,128)(2,1)}), bf16[4,160,2048]{2,1,0:T(8,128)(2,1)S(1)}, u32[]{:S(2)}, u32[]{:S(2)}) async-start(bf16[4,160,2048]{2,1,0:T(8,128)(2,1)} %bitcast.49), calls=%async_computation | async-start | bytes 5242880 | tf_op jit(solution)/shard_map/all_to_all | solution.py:488
  123.0 1.5 copy-done.8
  124.6 1.2 copy-done.14
  125.8 4.3 %pick_rows.4.refs_1_.refs_2_.refs_12_ = bf16[1792,640]{1,0:T(8,128)(2,1)S(1)} custom-call(s32[3]{0:T(128)S(1)} %pad_add_fusion.4.scalar_ref, bf16[272,1792]{1,0:T(8,128)(2,1)} %join_columns.2.refs_6_.refs_0_, bf16[272,1792]{1,0:T(8,128)(2,1)} %collective-permute-done.9.refs_1_, bf16[272,1792]{1,0:T(8,128)(2,1)} %collective-permute-done.10.refs_2_, ...), custom_call_target="tpu_custom_call" | custom-call | flops 1 | bytes 1 | tf_op jit(solution)/shard_map/pick_rows/pallas_call | solution.py:48
  130.1 1.4 copy-done.1
  132.1 2.9 %collective-permute-start.15 = (bf16[640,512]{1,0:T(8,128)(2,1)S(1)}, bf16[640,512]{1,0:T(8,128)(2,1)}, u32[]{:S(2)}, u32[]{:S(2)}) collective-permute-start(bf16[640,512]{1,0:T(8,128)(2,1)S(1)} %copy-done.17), channel_id=1, source_target_pairs={{0,8},{12,4},{1,9},{13,5},{2,10},{14,6},{3,11},{15,7},{16,24},{28,... | collective-permute-start | bytes 1966088 | tf_op jit(solution)/shard_map/ppermute | solution.py:485
  135.0 1.6 collective-permute-start.16
  136.6 2.1 collective-permute-start.17
  138.7 7.9 %for_end.3.refs_4_ = bf16[896,1024]{1,0:T(8,128)(2,1)} custom-call(s32[1]{0:T(128)} %constant.31.clone.1.scalar_ref, bf16[1792,640]{1,0:T(8,128)(2,1)} %copy-done.2, bf16[1792,640]{1,0:T(8,128)(2,1)} %copy-done.1, bf16[1792,640]{1,0:T(8,128)(2,1)} %copy-done.1, bf16[320,1024]{1,0:T(8,128)(2,1)} %get-tuple-element.36.refs_2_.refs_4_.refs_3_, ...), custom_call_target="tpu_custom_call" | custom-call | flops 1 | bytes 1 | tf_op jit(solution)/shard_map/for_end/pallas_call | solution.py:48
  146.6 1.5 collective-permute-start.26
  148.1 1.5 copy-done.9
  149.6 5.9 %pick_rows.5.refs_9_.refs_1_.refs_2_.refs_3_ = bf16[2688,640]{1,0:T(8,128)(2,1)S(1)} custom-call(s32[4]{0:T(128)S(1)} %pad_add_fusion.5.scalar_ref, bf16[272,2688]{1,0:T(8,128)(2,1)} %join_columns.3.refs_9_.refs_0_, bf16[272,2688]{1,0:T(8,128)(2,1)} %collective-permute-done.18.refs_1_, bf16[272,2688]{1,0:T(8,128)(2,1)} %collective-permute-done.19.refs_2_, ...), custom_call_target="tpu_custom_call" | custom-call | flops 1 | bytes 1 | tf_op jit(solution)/shard_map/pick_rows/pallas_call | solution.py:48
  155.5 1.7 copy-done
  157.2 5.2 %collective-permute-done.17.refs_8_.refs_7_ = bf16[640,512]{1,0:T(8,128)(2,1)} collective-permute-done((bf16[640,512]{1,0:T(8,128)(2,1)S(1)}, bf16[640,512]{1,0:T(8,128)(2,1)}, u32[]{:S(2)}, u32[]{:S(2)}) %collective-permute-start.17) | collective-permute-done | bytes 655392 | tf_op jit(solution)/shard_map/ppermute | solution.py:485
  162.4 1.5 copy-done.6
  163.9 4.4 %all-to-all-start.1 = ((bf16[4,160,1536]{2,1,0:T(8,128)(2,1)}), bf16[4,160,1536]{2,1,0:T(8,128)(2,1)}, u32[]{:S(2)}, u32[]{:S(2)}) async-start(bf16[4,160,1536]{2,1,0:T(8,128)(2,1)} %bitcast.33), calls=%async_computation.1 | async-start | bytes 3932160 | tf_op jit(solution)/shard_map/all_to_all | solution.py:488
  168.4 6.5 %collective-permute-start.22 = (bf16[640,512]{1,0:T(8,128)(2,1)}, bf16[640,512]{1,0:T(8,128)(2,1)}, u32[]{:S(2)}, u32[]{:S(2)}) collective-permute-start(bf16[640,512]{1,0:T(8,128)(2,1)} %get-tuple-element.46.refs_4_.refs_3_), channel_id=1, source_target_pairs={{0,8},{12,4},{1,9},{13,5},{2,10},{14,6},{3,11},{15,7},{16,24},{28,... | collective-permute-start | bytes 1966088 | tf_op jit(solution)/shard_map/ppermute | solution.py:485
  174.8 1.5 collective-permute-start.23
  176.3 2.3 collective-permute-start.24
  178.6 5.3 %for_end.4.refs_2_ = bf16[896,512]{1,0:T(8,128)(2,1)} custom-call(s32[1]{0:T(128)} %constant.31.clone.1.scalar_ref, bf16[1792,640]{1,0:T(8,128)(2,1)} %copy-done.2, bf16[1792,640]{1,0:T(8,128)(2,1)} %copy-done.1, bf16[1792,640]{1,0:T(8,128)(2,1)} %copy-done.1, bf16[640,512]{1,0:T(8,128)(2,1)} %get-tuple-element.42.refs_3_.refs_4_, ...), custom_call_target="tpu_custom_call" | custom-call | flops 1 | bytes 1 | tf_op jit(solution)/shard_map/for_end/pallas_call | solution.py:48
  183.9 2.1 combine.2.refs_13_
  186.0 1.6 collective-permute-start.21
  187.6 2.9 %collective-permute-done.26.refs_12_ = bf16[896,1024]{1,0:T(8,128)(2,1)} collective-permute-done((bf16[896,1024]{1,0:T(8,128)(2,1)}, bf16[896,1024]{1,0:T(8,128)(2,1)}, u32[]{:S(2)}, u32[]{:S(2)}) %collective-permute-start.26) | collective-permute-done | bytes 1835040 | tf_op jit(solution)/shard_map/ppermute | solution.py:497
  190.5 1.3 collective-permute-start.25
  191.8 9.8 %for_own.3.refs_9_ = bf16[896,1024]{1,0:T(8,128)(2,1)} custom-call(s32[1]{0:T(128)} %constant.31.clone.1.scalar_ref, bf16[1792,640]{1,0:T(8,128)(2,1)} %copy-done.2, bf16[2688,640]{1,0:T(8,128)(2,1)} %copy-done, bf16[2688,640]{1,0:T(8,128)(2,1)} %copy-done, bf16[2688,640]{1,0:T(8,128)(2,1)} %copy-done, ...), custom_call_target="tpu_custom_call" | custom-call | flops 1 | bytes 1 | tf_op jit(solution)/shard_map/for_own/pallas_call | solution.py:48
  201.6 1.3 collective-permute-done.24.refs_8_.refs_7_
  203.0 5.2 %for_end.5.refs_2_ = bf16[896,512]{1,0:T(8,128)(2,1)} custom-call(s32[1]{0:T(128)} %constant.31.clone.1.scalar_ref, bf16[1792,640]{1,0:T(8,128)(2,1)} %copy-done.2, bf16[1792,640]{1,0:T(8,128)(2,1)} %copy-done.1, bf16[1792,640]{1,0:T(8,128)(2,1)} %copy-done.1, bf16[640,512]{1,0:T(8,128)(2,1)} %get-tuple-element.46.refs_4_.refs_3_, ...), custom_call_target="tpu_custom_call" | custom-call | flops 1 | bytes 1 | tf_op jit(solution)/shard_map/for_end/pallas_call | solution.py:48
  208.2 1.3 collective-permute-start.28
  209.5 1.2 copy-done.11
  210.7 3.2 %combine.3.refs_9_ = bf16[256,1536]{1,0:T(8,128)(2,1)S(1)} custom-call(s32[1]{0:T(128)} %constant.31.clone.1.scalar_ref, s32[2,256]{1,0:T(2,128)S(1)} %bitcast.36, bf16[640,1536]{1,0:T(8,128)(2,1)} %bitcast.22.refs_1_, bf16[896,512]{1,0:T(8,128)(2,1)S(1)} %copy-done.11), custom_call_target="tpu_custom_call" | custom-call | flops 1 | bytes 1 | tf_op jit(solution)/shard_map/combine/pallas_call | solution.py:48
  214.0 1.6 collective-permute-start.27
  215.5 6.4 %for_own.4.refs_8_.refs_2_ = bf16[896,1024]{1,0:T(8,128)(2,1)} custom-call(s32[1]{0:T(128)} %constant.31.clone.1.scalar_ref, bf16[1792,640]{1,0:T(8,128)(2,1)} %copy-done.2, bf16[2688,640]{1,0:T(8,128)(2,1)} %copy-done, bf16[2688,640]{1,0:T(8,128)(2,1)} %copy-done, bf16[2688,640]{1,0:T(8,128)(2,1)} %copy-done, ...), custom_call_target="tpu_custom_call" | custom-call | flops 1 | bytes 1 | tf_op jit(solution)/shard_map/for_own/pallas_call | solution.py:48
  221.9 6.2 %for_own.5.refs_0_ = f32[896,512]{1,0:T(8,128)} custom-call(s32[1]{0:T(128)} %constant.31.clone.1.scalar_ref, bf16[1792,640]{1,0:T(8,128)(2,1)} %copy-done.2, bf16[2688,640]{1,0:T(8,128)(2,1)} %copy-done, bf16[2688,640]{1,0:T(8,128)(2,1)} %copy-done, bf16[2688,640]{1,0:T(8,128)(2,1)} %copy-done, bf16[640,512]{1,0:T(8,128)(2,1)} %get-tuple-element.46.refs_4_.refs_3_, ...), custom_call_target="tpu_custom_call" | custom-call | flops 1 | bytes 1 | tf_op jit(solution)/shard_map/for_own/pallas_call | solution.py:48
  228.2 5.3 %collective-permute-done.28.refs_1_ = bf16[896,512]{1,0:T(8,128)(2,1)} collective-permute-done((bf16[896,512]{1,0:T(8,128)(2,1)}, bf16[896,512]{1,0:T(8,128)(2,1)}, u32[]{:S(2)}, u32[]{:S(2)}) %collective-permute-start.28) | collective-permute-done | bytes 917536 | tf_op jit(solution)/shard_map/ppermute | solution.py:497
  233.5 2.8 %finish.1 = bf16[896,1024]{1,0:T(8,128)(2,1)} custom-call(s32[1]{0:T(128)} %constant.31.clone.1.scalar_ref, f32[896,512]{1,0:T(8,128)} %for_own.5.refs_0_, bf16[896,512]{1,0:T(8,128)(2,1)} %collective-permute-done.28.refs_1_, bf16[896,1024]{1,0:T(8,128)(2,1)} %for_own.4.refs_8_.refs_2_), custom_call_target="tpu_custom_call", output_to_operand_aliasing={{}: (3, {})} | custom-call | flops 1 | bytes 1 | tf_op jit(solution)/shard_map/finish/pallas_call | solution.py:48
  236.3 1.4 maximum_bitcast_fusion
  (61 shorter events, 3.3 us)
Async XLA Ops:
  0.7 1.5 copy-start.5
  2.2 0.7 copy-start.15
  6.0 12.6 %collective-permute-start.4 = (bf16[272,3584]{1,0:T(8,128)(2,1)}, bf16[272,3584]{1,0:T(8,128)(2,1)}, u32[]{:S(2)}, u32[]{:S(2)}) collective-permute-start(bf16[272,3584]{1,0:T(8,128)(2,1)} %get-tuple-element.26.refs_0_.refs_4_), channel_id=1, source_target_pairs={{0,1},{1,0},{2,3},{3,2},{4,5},{5,4},{6,7},{7,6},{8,9},{9,8},{10,11... | collective-permute-start | bytes 5849096 | tf_op jit(solution)/shard_map/ppermute | solution.py:479
  6.4 45.9 %collective-permute-start = (bf16[272,3584]{1,0:T(8,128)(2,1)}, bf16[272,3584]{1,0:T(8,128)(2,1)S(1)}, u32[]{:S(2)}, u32[]{:S(2)}) collective-permute-start(bf16[272,3584]{1,0:T(8,128)(2,1)} %get-tuple-element.26.refs_0_.refs_4_), channel_id=1, source_target_pairs={{0,2},{1,3},{2,0},{3,1},{4,6},{5,7},{6,4},{7,5},{8,10},{9,11},{10,... | collective-permute-start | bytes 5849096 | tf_op jit(solution)/shard_map/ppermute | solution.py:482
  9.0 36.5 %collective-permute-start.1 = (bf16[272,1792]{1,0:T(8,128)(2,1)}, bf16[272,1792]{1,0:T(8,128)(2,1)S(1)}, u32[]{:S(2)}, u32[]{:S(2)}) collective-permute-start(bf16[272,1792]{1,0:T(8,128)(2,1)} %get-tuple-element.27), channel_id=1, source_target_pairs={{0,8},{12,4},{1,9},{13,5},{2,10},{14,6},{3,11},{15,7},{16,24},{28,... | collective-permute-start | bytes 2924552 | tf_op jit(solution)/shard_map/ppermute | solution.py:485
  13.5 32.0 %collective-permute-start.2 = (bf16[272,1792]{1,0:T(8,128)(2,1)}, bf16[272,1792]{1,0:T(8,128)(2,1)}, u32[]{:S(2)}, u32[]{:S(2)}) collective-permute-start(bf16[272,1792]{1,0:T(8,128)(2,1)} %get-tuple-element.28), channel_id=1, source_target_pairs={{4,8},{8,4},{5,9},{9,5},{6,10},{10,6},{7,11},{11,7},{20,24},{24,20... | collective-permute-start | bytes 2924552 | tf_op jit(solution)/shard_map/ppermute | solution.py:485
  15.1 30.3 %collective-permute-start.3 = (bf16[272,896]{1,0:T(8,128)(2,1)}, bf16[272,896]{1,0:T(8,128)(2,1)S(1)}, u32[]{:S(2)}, u32[]{:S(2)}) collective-permute-start(bf16[272,896]{1,0:T(8,128)(2,1)} %get-tuple-element.29), channel_id=1, source_target_pairs={{0,4},{12,8},{1,5},{13,9},{2,6},{14,10},{3,7},{15,11},{16,20},{28,... | collective-permute-start | bytes 1462280 | tf_op jit(solution)/shard_map/ppermute | solution.py:485
  52.3 2.4 %copy-start.3 = (bf16[272,3584]{1,0:T(8,128)(2,1)}, bf16[272,3584]{1,0:T(8,128)(2,1)S(1)}, u32[]{:S(2)}) copy-start(bf16[272,3584]{1,0:T(8,128)(2,1)S(1)} %collective-permute-done.refs_5_.refs_0_.refs_2_.refs_6_) | copy-start | bytes 5849092
  52.3 17.1 %collective-permute-start.5 = (bf16[272,3584]{1,0:T(8,128)(2,1)S(1)}, bf16[272,3584]{1,0:T(8,128)(2,1)}, u32[]{:S(2)}, u32[]{:S(2)}) collective-permute-start(bf16[272,3584]{1,0:T(8,128)(2,1)S(1)} %collective-permute-done.refs_5_.refs_0_.refs_2_.refs_6_), channel_id=1, source_target_pairs={{0,1},{1,0},{2,3},{3,2},{4,5},{5,4},{6,7},{7,6},{8,9},{9,8},{10,11... | collective-permute-start | bytes 5849096 | tf_op jit(solution)/shard_map/ppermute | solution.py:479
  54.7 38.0 %collective-permute-start.10 = (bf16[272,1792]{1,0:T(8,128)(2,1)}, bf16[272,1792]{1,0:T(8,128)(2,1)}, u32[]{:S(2)}, u32[]{:S(2)}) collective-permute-start(bf16[272,1792]{1,0:T(8,128)(2,1)} %join_columns.2.refs_6_.refs_0_), channel_id=1, source_target_pairs={{0,2},{1,3},{2,0},{3,1},{4,6},{5,7},{6,4},{7,5},{8,10},{9,11},{10,... | collective-permute-start | bytes 2924552 | tf_op jit(solution)/shard_map/ppermute | solution.py:482
  56.5 34.9 %collective-permute-start.6 = (bf16[320,1024]{1,0:T(8,128)(2,1)}, bf16[320,1024]{1,0:T(8,128)(2,1)}, u32[]{:S(2)}, u32[]{:S(2)}) collective-permute-start(bf16[320,1024]{1,0:T(8,128)(2,1)} %get-tuple-element.36.refs_2_.refs_4_.refs_3_), channel_id=1, source_target_pairs={{0,8},{12,4},{1,9},{13,5},{2,10},{14,6},{3,11},{15,7},{16,24},{28,... | collective-permute-start | bytes 1966088 | tf_op jit(solution)/shard_map/ppermute | solution.py:485
  65.0 26.4 %collective-permute-start.7 = (bf16[320,1024]{1,0:T(8,128)(2,1)}, bf16[320,1024]{1,0:T(8,128)(2,1)}, u32[]{:S(2)}, u32[]{:S(2)}) collective-permute-start(bf16[320,1024]{1,0:T(8,128)(2,1)} %get-tuple-element.36.refs_2_.refs_4_.refs_3_), channel_id=1, source_target_pairs={{4,8},{8,4},{5,9},{9,5},{6,10},{10,6},{7,11},{11,7},{20,24},{24,20... | collective-permute-start | bytes 1966088 | tf_op jit(solution)/shard_map/ppermute | solution.py:485
  66.5 26.2 %collective-permute-start.8 = (bf16[320,1024]{1,0:T(8,128)(2,1)}, bf16[320,1024]{1,0:T(8,128)(2,1)}, u32[]{:S(2)}, u32[]{:S(2)}) collective-permute-start(bf16[320,1024]{1,0:T(8,128)(2,1)} %get-tuple-element.36.refs_2_.refs_4_.refs_3_), channel_id=1, source_target_pairs={{0,4},{12,8},{1,5},{13,9},{2,6},{14,10},{3,7},{15,11},{16,20},{28,... | collective-permute-start | bytes 1966088 | tf_op jit(solution)/shard_map/ppermute | solution.py:485
  82.9 1.5 copy-start.4
  88.8 2.6 %copy-start.2 = (bf16[1792,640]{1,0:T(8,128)(2,1)}, bf16[1792,640]{1,0:T(8,128)(2,1)S(1)}, u32[]{:S(2)}) copy-start(bf16[1792,640]{1,0:T(8,128)(2,1)S(1)} %pick_rows.3.refs_3_.refs_0_) | copy-start | bytes 6881284
  92.7 9.7 %collective-permute-start.11 = (bf16[272,1792]{1,0:T(8,128)(2,1)}, bf16[272,1792]{1,0:T(8,128)(2,1)S(1)}, u32[]{:S(2)}, u32[]{:S(2)}) collective-permute-start(bf16[272,1792]{1,0:T(8,128)(2,1)} %collective-permute-done.10.refs_2_), channel_id=1, source_target_pairs={{0,1},{1,0},{2,3},{3,2},{4,5},{5,4},{6,7},{7,6},{8,9},{9,8},{10,11... | collective-permute-start | bytes 2924552 | tf_op jit(solution)/shard_map/ppermute | solution.py:479
  92.7 30.3 %collective-permute-start.9 = (bf16[272,1792]{1,0:T(8,128)(2,1)}, bf16[272,1792]{1,0:T(8,128)(2,1)}, u32[]{:S(2)}, u32[]{:S(2)}) collective-permute-start(bf16[272,1792]{1,0:T(8,128)(2,1)} %join_columns.2.refs_6_.refs_0_), channel_id=1, source_target_pairs={{0,1},{1,0},{2,3},{3,2},{4,5},{5,4},{6,7},{7,6},{8,9},{9,8},{10,11... | collective-permute-start | bytes 2924552 | tf_op jit(solution)/shard_map/ppermute | solution.py:479
  93.2 38.8 %collective-permute-start.19 = (bf16[272,2688]{1,0:T(8,128)(2,1)}, bf16[272,2688]{1,0:T(8,128)(2,1)}, u32[]{:S(2)}, u32[]{:S(2)}) collective-permute-start(bf16[272,2688]{1,0:T(8,128)(2,1)} %join_columns.3.refs_9_.refs_0_), channel_id=1, source_target_pairs={{0,2},{1,3},{2,0},{3,1},{4,6},{5,7},{6,4},{7,5},{8,10},{9,11},{10,... | collective-permute-start | bytes 4386824 | tf_op jit(solution)/shard_map/ppermute | solution.py:482
  94.7 36.7 %collective-permute-start.12 = (bf16[320,1024]{1,0:T(8,128)(2,1)}, bf16[320,1024]{1,0:T(8,128)(2,1)}, u32[]{:S(2)}, u32[]{:S(2)}) collective-permute-start(bf16[320,1024]{1,0:T(8,128)(2,1)} %get-tuple-element.41.refs_8_.refs_2_.refs_4_.refs_5_), channel_id=1, source_target_pairs={{0,8},{12,4},{1,9},{13,5},{2,10},{14,6},{3,11},{15,7},{16,24},{28,... | collective-permute-start | bytes 1966088 | tf_op jit(solution)/shard_map/ppermute | solution.py:485
  100.8 30.6 %collective-permute-start.13 = (bf16[320,1024]{1,0:T(8,128)(2,1)}, bf16[320,1024]{1,0:T(8,128)(2,1)}, u32[]{:S(2)}, u32[]{:S(2)}) collective-permute-start(bf16[320,1024]{1,0:T(8,128)(2,1)} %get-tuple-element.41.refs_8_.refs_2_.refs_4_.refs_5_), channel_id=1, source_target_pairs={{4,8},{8,4},{5,9},{9,5},{6,10},{10,6},{7,11},{11,7},{20,24},{24,20... | collective-permute-start | bytes 1966088 | tf_op jit(solution)/shard_map/ppermute | solution.py:485
  102.4 0.9 copy-start.13
  103.3 28.2 %collective-permute-start.14 = (bf16[320,1024]{1,0:T(8,128)(2,1)}, bf16[320,1024]{1,0:T(8,128)(2,1)}, u32[]{:S(2)}, u32[]{:S(2)}) collective-permute-start(bf16[320,1024]{1,0:T(8,128)(2,1)} %get-tuple-element.41.refs_8_.refs_2_.refs_4_.refs_5_), channel_id=1, source_target_pairs={{0,4},{12,8},{1,5},{13,9},{2,6},{14,10},{3,7},{15,11},{16,20},{28,... | collective-permute-start | bytes 1966088 | tf_op jit(solution)/shard_map/ppermute | solution.py:485
  119.3 43.1 %all-to-all-start = ((bf16[4,160,2048]{2,1,0:T(8,128)(2,1)}), bf16[4,160,2048]{2,1,0:T(8,128)(2,1)S(1)}, u32[]{:S(2)}, u32[]{:S(2)}) async-start(bf16[4,160,2048]{2,1,0:T(8,128)(2,1)} %bitcast.49), calls=%async_computation | async-start | bytes 5242880 | tf_op jit(solution)/shard_map/all_to_all | solution.py:488
  123.0 1.5 copy-start.8
  124.6 1.2 copy-start.14
  125.8 6.3 %copy-start.17 = (bf16[640,512]{1,0:T(8,128)(2,1)S(1)}, bf16[640,512]{1,0:T(8,128)(2,1)}, u32[]{:S(2)}) copy-start(bf16[640,512]{1,0:T(8,128)(2,1)} %get-tuple-element.42.refs_3_.refs_4_) | copy-start | bytes 1966084
  130.1 1.4 copy-start.1
  131.5 15.1 %collective-permute-start.18 = (bf16[272,2688]{1,0:T(8,128)(2,1)}, bf16[272,2688]{1,0:T(8,128)(2,1)}, u32[]{:S(2)}, u32[]{:S(2)}) collective-permute-start(bf16[272,2688]{1,0:T(8,128)(2,1)} %join_columns.3.refs_9_.refs_0_), channel_id=1, source_target_pairs={{0,1},{1,0},{2,3},{3,2},{4,5},{5,4},{6,7},{7,6},{8,9},{9,8},{10,11... | collective-permute-start | bytes 4386824 | tf_op jit(solution)/shard_map/ppermute | solution.py:479
  132.0 16.1 %collective-permute-start.20 = (bf16[272,2688]{1,0:T(8,128)(2,1)}, bf16[272,2688]{1,0:T(8,128)(2,1)}, u32[]{:S(2)}, u32[]{:S(2)}) collective-permute-start(bf16[272,2688]{1,0:T(8,128)(2,1)} %collective-permute-done.19.refs_2_), channel_id=1, source_target_pairs={{0,1},{1,0},{2,3},{3,2},{4,5},{5,4},{6,7},{7,6},{8,9},{9,8},{10,11... | collective-permute-start | bytes 4386824 | tf_op jit(solution)/shard_map/ppermute | solution.py:479
  132.1 25.1 %collective-permute-start.15 = (bf16[640,512]{1,0:T(8,128)(2,1)S(1)}, bf16[640,512]{1,0:T(8,128)(2,1)}, u32[]{:S(2)}, u32[]{:S(2)}) collective-permute-start(bf16[640,512]{1,0:T(8,128)(2,1)S(1)} %copy-done.17), channel_id=1, source_target_pairs={{0,8},{12,4},{1,9},{13,5},{2,10},{14,6},{3,11},{15,7},{16,24},{28,... | collective-permute-start | bytes 1966088 | tf_op jit(solution)/shard_map/ppermute | solution.py:485
  135.0 22.3 %collective-permute-start.16 = (bf16[640,512]{1,0:T(8,128)(2,1)S(1)}, bf16[640,512]{1,0:T(8,128)(2,1)}, u32[]{:S(2)}, u32[]{:S(2)}) collective-permute-start(bf16[640,512]{1,0:T(8,128)(2,1)S(1)} %copy-done.17), channel_id=1, source_target_pairs={{4,8},{8,4},{5,9},{9,5},{6,10},{10,6},{7,11},{11,7},{20,24},{24,20... | collective-permute-start | bytes 1966088 | tf_op jit(solution)/shard_map/ppermute | solution.py:485
  136.6 25.8 %collective-permute-start.17 = (bf16[640,512]{1,0:T(8,128)(2,1)S(1)}, bf16[640,512]{1,0:T(8,128)(2,1)}, u32[]{:S(2)}, u32[]{:S(2)}) collective-permute-start(bf16[640,512]{1,0:T(8,128)(2,1)S(1)} %copy-done.17), channel_id=1, source_target_pairs={{0,4},{12,8},{1,5},{13,9},{2,6},{14,10},{3,7},{15,11},{16,20},{28,... | collective-permute-start | bytes 1966088 | tf_op jit(solution)/shard_map/ppermute | solution.py:485
  146.6 43.9 %collective-permute-start.26 = (bf16[896,1024]{1,0:T(8,128)(2,1)}, bf16[896,1024]{1,0:T(8,128)(2,1)}, u32[]{:S(2)}, u32[]{:S(2)}) collective-permute-start(bf16[896,1024]{1,0:T(8,128)(2,1)} %for_end.3.refs_4_), channel_id=1, source_target_pairs={{4,0},{8,12},{5,1},{9,13},{6,2},{10,14},{7,3},{11,15},{20,16},{24,... | collective-permute-start | bytes 5505032 | tf_op jit(solution)/shard_map/ppermute | solution.py:497
  148.1 1.5 copy-start.9
  155.5 1.7 copy-start
  162.4 1.5 copy-start.6
  163.9 45.6 %all-to-all-start.1 = ((bf16[4,160,1536]{2,1,0:T(8,128)(2,1)}), bf16[4,160,1536]{2,1,0:T(8,128)(2,1)}, u32[]{:S(2)}, u32[]{:S(2)}) async-start(bf16[4,160,1536]{2,1,0:T(8,128)(2,1)} %bitcast.33), calls=%async_computation.1 | async-start | bytes 3932160 | tf_op jit(solution)/shard_map/all_to_all | solution.py:488
  168.4 15.5 %copy-start.7 = (bf16[4,160,2048]{2,1,0:T(8,128)(2,1)S(1)}, bf16[4,160,2048]{2,1,0:T(8,128)(2,1)}, u32[]{:S(2)}) copy-start(bf16[4,160,2048]{2,1,0:T(8,128)(2,1)} %copy-done.6) | copy-start | bytes 7864324
  168.4 15.5 %copy-start.16 = (s32[1,256,2]{1,2,0:T(2,128)S(1)}, s32[1,256,2]{1,2,0:T(2,128)}, u32[]{:S(2)}) copy-start(s32[1,256,2]{1,2,0:T(2,128)} %param.6) | copy-start | bytes 6148
  168.4 33.2 %collective-permute-start.22 = (bf16[640,512]{1,0:T(8,128)(2,1)}, bf16[640,512]{1,0:T(8,128)(2,1)}, u32[]{:S(2)}, u32[]{:S(2)}) collective-permute-start(bf16[640,512]{1,0:T(8,128)(2,1)} %get-tuple-element.46.refs_4_.refs_3_), channel_id=1, source_target_pairs={{0,8},{12,4},{1,9},{13,5},{2,10},{14,6},{3,11},{15,7},{16,24},{28,... | collective-permute-start | bytes 1966088 | tf_op jit(solution)/shard_map/ppermute | solution.py:485
  174.8 26.8 %collective-permute-start.23 = (bf16[640,512]{1,0:T(8,128)(2,1)}, bf16[640,512]{1,0:T(8,128)(2,1)}, u32[]{:S(2)}, u32[]{:S(2)}) collective-permute-start(bf16[640,512]{1,0:T(8,128)(2,1)} %get-tuple-element.46.refs_4_.refs_3_), channel_id=1, source_target_pairs={{4,8},{8,4},{5,9},{9,5},{6,10},{10,6},{7,11},{11,7},{20,24},{24,20... | collective-permute-start | bytes 1966088 | tf_op jit(solution)/shard_map/ppermute | solution.py:485
  176.3 26.7 %collective-permute-start.24 = (bf16[640,512]{1,0:T(8,128)(2,1)}, bf16[640,512]{1,0:T(8,128)(2,1)}, u32[]{:S(2)}, u32[]{:S(2)}) collective-permute-start(bf16[640,512]{1,0:T(8,128)(2,1)} %get-tuple-element.46.refs_4_.refs_3_), channel_id=1, source_target_pairs={{0,4},{12,8},{1,5},{13,9},{2,6},{14,10},{3,7},{15,11},{16,20},{28,... | collective-permute-start | bytes 1966088 | tf_op jit(solution)/shard_map/ppermute | solution.py:485
  186.0 5.8 %copy-start.10 = (bf16[256,2048]{1,0:T(8,128)(2,1)}, bf16[256,2048]{1,0:T(8,128)(2,1)S(1)}, u32[]{:S(2)}) copy-start(bf16[256,2048]{1,0:T(8,128)(2,1)S(1)} %combine.2.refs_13_) | copy-start | bytes 3145732
  186.0 42.2 %collective-permute-start.21 = (bf16[256,2048]{1,0:T(8,128)(2,1)S(1)}, bf16[256,2048]{1,0:T(8,128)(2,1)S(1)}, u32[]{:S(2)}, u32[]{:S(2)}) collective-permute-start(bf16[256,2048]{1,0:T(8,128)(2,1)S(1)} %combine.2.refs_13_), channel_id=1, source_target_pairs={{0,16},{16,0},{1,17},{17,1},{2,18},{18,2},{3,19},{19,3},{4,20},{20... | collective-permute-start | bytes 3145736 | tf_op jit(solution)/shard_map/ppermute | solution.py:494
  190.5 25.0 %collective-permute-start.25 = (bf16[896,512]{1,0:T(8,128)(2,1)}, bf16[896,512]{1,0:T(8,128)(2,1)}, u32[]{:S(2)}, u32[]{:S(2)}) collective-permute-start(bf16[896,512]{1,0:T(8,128)(2,1)} %for_end.4.refs_2_), channel_id=1, source_target_pairs={{4,0},{8,12},{5,1},{9,13},{6,2},{10,14},{7,3},{11,15},{20,16},{24,... | collective-permute-start | bytes 2752520 | tf_op jit(solution)/shard_map/ppermute | solution.py:497
  208.2 25.3 %collective-permute-start.28 = (bf16[896,512]{1,0:T(8,128)(2,1)}, bf16[896,512]{1,0:T(8,128)(2,1)}, u32[]{:S(2)}, u32[]{:S(2)}) collective-permute-start(bf16[896,512]{1,0:T(8,128)(2,1)} %for_end.5.refs_2_), channel_id=1, source_target_pairs={{4,0},{8,12},{5,1},{9,13},{6,2},{10,14},{7,3},{11,15},{20,16},{24,... | collective-permute-start | bytes 2752520 | tf_op jit(solution)/shard_map/ppermute | solution.py:497
  209.5 1.2 copy-start.11
  214.0 1.6 copy-start.12
  214.0 22.4 %collective-permute-start.27 = (bf16[256,1536]{1,0:T(8,128)(2,1)S(1)}, bf16[256,1536]{1,0:T(8,128)(2,1)S(1)}, u32[]{:S(2)}, u32[]{:S(2)}) collective-permute-start(bf16[256,1536]{1,0:T(8,128)(2,1)S(1)} %combine.3.refs_9_), channel_id=1, source_target_pairs={{0,16},{16,0},{1,17},{17,1},{2,18},{18,2},{3,19},{19,3},{4,20},{20... | collective-permute-start | bytes 2359304 | tf_op jit(solution)/shard_map/ppermute | solution.py:494

commit v7 on v6

--- a/solution.py
+++ b/solution.py
@@ -313,7 +313,7 @@
         out_specs,
         (steps,),
         after=after,
-        vmem=60,
+        vmem=63,
     )
     return out[0] if near is None else out
 
@@ -499,7 +499,7 @@
     chips = range(1, experts // 2)
     places = [jnp.bitwise_xor((expert - 2 * (r // 2)) % experts, r % 2) for r in range(experts)]
     targets = [target_in(pairs, group) for pairs in sets]
-    order = list(range(2, len(sets))) + [1, 0]
+    order = list(range(2, len(sets))) + [0, 1]
 
     pair = routes[0].T
     own, *cut = cut_columns(rows, pair, group, targets, groups, block)

time: 239 us -> 239 us (level)
  local copies, waits for them, and re-layouts: 14.8 us -> 19 us
  waiting for transfers between devices: 24.6 us -> 21.4 us
    unnamed x36 -> x40, local copies, waits for them, and re-layouts: 14.8 us -> 19 us
    ppermute x15, waiting for transfers between devices: 9.5 us -> 6.59 us  [over_groups(): return lax.ppermute(value, 'dp', pairs)]
  transfers between devices with their start and end apart: 31 -> 31, of which waited for: 7 -> 5; matrix products, arithmetic and copies ran while one was open for 1% -> 1% of each run, Pallas kernels for 51% -> 51%
where the time goes in v7:
time: 239 us; the launch traced here: 237 us
  Pallas kernels  124 us (52%)
  starting transfers between devices  68.7 us (29%)
  waiting for transfers between devices  21.4 us (9%)
  local copies, waits for them, and re-layouts  19 us (8%)
  other arithmetic  3.44 us (1%)
    pallas_call x19, Pallas kernels, call(): pl.pallas_call(kernel, name=name, out_shape=[jax.ShapeDtypeStruct(shape,...  124 us
    ppermute x15, starting transfers between devices, over_groups(): return lax.ppermute(value, 'dp', pairs)  46 us
    unnamed x40, local copies, waits for them, and re-layouts  19 us
    ppermute x3, waiting for transfers between devices, to_ends(): return lax.ppermute(value, 'dp', [(1, 0), (groups - 2, groups - 1)])  8.27 us
    all_to_all x2, starting transfers between devices, to_sources(): lax.all_to_all(value.reshape(experts, capacity, value.shape[1]), 'expert'...  8.06 us
    ppermute x15, waiting for transfers between devices, over_groups(): return lax.ppermute(value, 'dp', pairs)  6.59 us
    ppermute x3, waiting for transfers between devices, shift(): lax.ppermute(value, 'expert', [(s, (s + 2 * by) % experts) for s in range...  6.5 us
    ppermute x3, starting transfers between devices, shift(): lax.ppermute(value, 'expert', [(s, (s + 2 * by) % experts) for s in range...  5.81 us
  transfers between devices with their start and end apart: 31, of which 5 were waited for; matrix products, arithmetic and copies ran while one was open for 1% of the time, Pallas kernels for 51%

profile of v7, /device:TPU:0, one launch (start us, length us, event | category | flops | bytes accessed | tf_op | source)
XLA Modules:
  0.0 237.5 jit_solution(7287027225440344067)
XLA Ops:
  0.8 1.5 copy-done.3
  2.3 0.7 copy-done.17
  2.9 3.1 %cut_columns.1 = (bf16[272,3584]{1,0:T(8,128)(2,1)}, bf16[272,896]{1,0:T(8,128)(2,1)}, bf16[272,1792]{1,0:T(8,128)(2,1)}, bf16[272,1792]{1,0:T(8,128)(2,1)}) custom-call(s32[5]{0:T(128)S(1)} %stack.82.scalar_ref, s32[2,256]{1,0:T(2,128)S(1)} %bitcast.34, bf16[256,3584]{1,0:T(8,128)(2,1)S(1)} %bitcast.27, bf16[256,3584]{1,0:T(8,128)(2,1)S(1)} %bitcast.28, ...), custom_call_target="tpu_custom_call" | custom-call | flops 1 | bytes 1 | tf_op jit(solution)/shard_map/cut_columns/pallas_call | solution.py:48
  6.4 2.5 %collective-permute-start = (bf16[272,3584]{1,0:T(8,128)(2,1)}, bf16[272,3584]{1,0:T(8,128)(2,1)}, u32[]{:S(2)}, u32[]{:S(2)}) collective-permute-start(bf16[272,3584]{1,0:T(8,128)(2,1)} %get-tuple-element.26.refs_0_.refs_4_), channel_id=1, source_target_pairs={{0,2},{1,3},{2,0},{3,1},{4,6},{5,7},{6,4},{7,5},{8,10},{9,11},{10,... | collective-permute-start | bytes 5849096 | tf_op jit(solution)/shard_map/ppermute | solution.py:482
  9.0 4.5 %collective-permute-start.1 = (bf16[272,1792]{1,0:T(8,128)(2,1)}, bf16[272,1792]{1,0:T(8,128)(2,1)S(1)}, u32[]{:S(2)}, u32[]{:S(2)}) collective-permute-start(bf16[272,1792]{1,0:T(8,128)(2,1)} %get-tuple-element.27), channel_id=1, source_target_pairs={{0,8},{12,4},{1,9},{13,5},{2,10},{14,6},{3,11},{15,7},{16,24},{28,... | collective-permute-start | bytes 2924552 | tf_op jit(solution)/shard_map/ppermute | solution.py:485
  13.5 1.6 collective-permute-start.3
  15.2 2.9 %collective-permute-start.2 = (bf16[272,896]{1,0:T(8,128)(2,1)}, bf16[272,896]{1,0:T(8,128)(2,1)}, u32[]{:S(2)}, u32[]{:S(2)}) collective-permute-start(bf16[272,896]{1,0:T(8,128)(2,1)} %get-tuple-element.28), channel_id=1, source_target_pairs={{0,4},{12,8},{1,5},{13,9},{2,6},{14,10},{3,7},{15,11},{16,20},{28,... | collective-permute-start | bytes 1462280 | tf_op jit(solution)/shard_map/ppermute | solution.py:485
  19.4 1.4 copy-done.8
  20.7 13.2 %forward_first.1 = (bf16[320,1024]{1,0:T(8,128)(2,1)}, bf16[320,1024]{1,0:T(8,128)(2,1)}) custom-call(s32[3]{0:T(128)} %pad_add_fusion.2.scalar_ref, bf16[272,3584]{1,0:T(8,128)(2,1)} %get-tuple-element.26.refs_0_.refs_4_, bf16[272,3584]{1,0:T(8,128)(2,1)} %copy-done.8, bf16[640,1024]{1,0:T(8,128)(2,1)} %bitcast.47, bf16[3584,1024]{1,0:T(8,128)(2,1)} %bitcast.37, ...), custom_call_target="tpu_custom_call" | custom-call | flops 1 | bytes 1 | tf_op jit(solution)/shard_map/forward_first/pallas_call | solution.py:48
  33.9 12.0 %near_gradients.1.refs_5_ = bf16[320,3584]{1,0:T(8,128)(2,1)} custom-call(s32[4]{0:T(128)} %pad_add_fusion.scalar_ref, bf16[3584,1024]{1,0:T(8,128)(2,1)} %bitcast.38, bf16[3584,1024]{1,0:T(8,128)(2,1)} %bitcast.42, bf16[320,1024]{1,0:T(8,128)(2,1)} %get-tuple-element.36.refs_2_.refs_4_.refs_3_, bf16[320,1024]{1,0:T(8,128)(2,1)} %get-tuple-element.31.refs_3_.refs_5_, ...), custom_call_target="tpu_custom_call" | custom-call | flops 1 | bytes 1 | tf_op jit(solution)/shard_map/near_gradients/pallas_call | solution.py:48
  45.9 6.5 %collective-permute-done.refs_5_.refs_0_.refs_2_.refs_6_ = bf16[272,3584]{1,0:T(8,128)(2,1)} collective-permute-done((bf16[272,3584]{1,0:T(8,128)(2,1)}, bf16[272,3584]{1,0:T(8,128)(2,1)}, u32[]{:S(2)}, u32[]{:S(2)}) %collective-permute-start) | collective-permute-done | bytes 1949728 | tf_op jit(solution)/shard_map/ppermute | solution.py:482
  52.4 2.0 join_columns.2.refs_6_.refs_0_
  54.5 1.7 collective-permute-start.10
  56.2 8.4 %collective-permute-start.6 = (bf16[320,1024]{1,0:T(8,128)(2,1)}, bf16[320,1024]{1,0:T(8,128)(2,1)}, u32[]{:S(2)}, u32[]{:S(2)}) collective-permute-start(bf16[320,1024]{1,0:T(8,128)(2,1)} %get-tuple-element.36.refs_2_.refs_4_.refs_3_), channel_id=1, source_target_pairs={{0,8},{12,4},{1,9},{13,5},{2,10},{14,6},{3,11},{15,7},{16,24},{28,... | collective-permute-start | bytes 1966088 | tf_op jit(solution)/shard_map/ppermute | solution.py:485
  64.6 2.1 collective-permute-start.7
  66.7 1.5 collective-permute-start.8
  68.9 1.3 copy-done.6
  70.2 13.5 %forward_rest.1 = (bf16[320,1024]{1,0:T(8,128)(2,1)}, bf16[640,512]{1,0:T(8,128)(2,1)}, bf16[640,512]{1,0:T(8,128)(2,1)}) custom-call(s32[3]{0:T(128)} %pad_add_fusion.1.scalar_ref, bf16[272,3584]{1,0:T(8,128)(2,1)} %collective-permute-done.refs_5_.refs_0_.refs_2_.refs_6_, bf16[272,3584]{1,0:T(8,128)(2,1)} %copy-done.6, bf16[640,1024]{1,0:T(8,128)(2,1)} %bitcast.48, ...), custom_call_target="tpu_custom_call" | custom-call | flops 1 | bytes 1 | tf_op jit(solution)/shard_map/forward_rest/pallas_call | solution.py:48
  83.7 1.5 copy-done.7
  85.2 1.5 copy-done.9
  86.8 4.2 %pick_rows.3.refs_3_.refs_0_ = bf16[1792,640]{1,0:T(8,128)(2,1)S(1)} custom-call(s32[3]{0:T(128)S(1)} %pad_add_fusion.3.scalar_ref, bf16[272,3584]{1,0:T(8,128)(2,1)} %get-tuple-element.26.refs_0_.refs_4_, bf16[272,3584]{1,0:T(8,128)(2,1)S(1)} %copy-done.9, bf16[272,3584]{1,0:T(8,128)(2,1)} %collective-permute-done.refs_5_.refs_0_.refs_2_.refs_6_, ...), custom_call_target="tpu_custom_call" | custom-call | flops 1 | bytes 1 | tf_op jit(solution)/shard_map/pick_rows/pallas_call | solution.py:48
  90.9 3.1 %join_columns.3.refs_9_.refs_0_ = bf16[272,2688]{1,0:T(8,128)(2,1)} custom-call(s32[1]{0:T(128)} %constant.31.clone.1.scalar_ref, bf16[272,896]{1,0:T(8,128)(2,1)} %collective-permute-done.2.refs_3_.refs_0_, bf16[272,1792]{1,0:T(8,128)(2,1)} %collective-permute-done.3.refs_0_.refs_4_.refs_1_, bf16[272,1792]{1,0:T(8,128)(2,1)S(1)} %collective-permute-done.1.refs_1_.refs_2_, ...), custom_call_target="tpu_custom_call" | custom-call | flops 1 | bytes 1 | tf_op jit(solution)/shard_map/join_columns/pallas_call | solution.py:48
  94.7 1.5 collective-permute-start.19
  96.2 4.4 %collective-permute-start.12 = (bf16[320,1024]{1,0:T(8,128)(2,1)}, bf16[320,1024]{1,0:T(8,128)(2,1)}, u32[]{:S(2)}, u32[]{:S(2)}) collective-permute-start(bf16[320,1024]{1,0:T(8,128)(2,1)} %get-tuple-element.41.refs_8_.refs_2_.refs_4_.refs_5_), channel_id=1, source_target_pairs={{0,8},{12,4},{1,9},{13,5},{2,10},{14,6},{3,11},{15,7},{16,24},{28,... | collective-permute-start | bytes 1966088 | tf_op jit(solution)/shard_map/ppermute | solution.py:485
  100.6 2.1 collective-permute-start.13
  102.7 0.9 copy-done.15
  103.7 1.5 collective-permute-start.14
  105.2 13.8 %slot_gradients.1 = (bf16[640,2048]{1,0:T(8,128)(2,1)}, bf16[640,1536]{1,0:T(8,128)(2,1)}) custom-call(s32[4]{0:T(128)} %pad_add_fusion.scalar_ref, bf16[3584,1024]{1,0:T(8,128)(2,1)} %bitcast.40, bf16[3584,1024]{1,0:T(8,128)(2,1)} %bitcast.44, bf16[320,1024]{1,0:T(8,128)(2,1)} %get-tuple-element.41.refs_8_.refs_2_.refs_4_.refs_5_, ...), custom_call_target="tpu_custom_call" | custom-call | flops 1 | bytes 1 | tf_op jit(solution)/shard_map/slot_gradients/pallas_call | solution.py:48
  119.0 3.7 %all-to-all-start = ((bf16[4,160,2048]{2,1,0:T(8,128)(2,1)}), bf16[4,160,2048]{2,1,0:T(8,128)(2,1)S(1)}, u32[]{:S(2)}, u32[]{:S(2)}) async-start(bf16[4,160,2048]{2,1,0:T(8,128)(2,1)} %bitcast.49), calls=%async_computation | async-start | bytes 5242880 | tf_op jit(solution)/shard_map/all_to_all | solution.py:488
  122.7 1.5 copy-done.10
  124.2 1.2 copy-done.16
  125.4 4.3 %pick_rows.4.refs_1_.refs_2_.refs_12_ = bf16[1792,640]{1,0:T(8,128)(2,1)S(1)} custom-call(s32[3]{0:T(128)S(1)} %pad_add_fusion.4.scalar_ref, bf16[272,1792]{1,0:T(8,128)(2,1)} %join_columns.2.refs_6_.refs_0_, bf16[272,1792]{1,0:T(8,128)(2,1)} %collective-permute-done.9.refs_1_, bf16[272,1792]{1,0:T(8,128)(2,1)} %collective-permute-done.10.refs_2_, ...), custom_call_target="tpu_custom_call" | custom-call | flops 1 | bytes 1 | tf_op jit(solution)/shard_map/pick_rows/pallas_call | solution.py:48
  129.7 1.4 copy-done.1
  131.8 2.9 %collective-permute-start.15 = (bf16[640,512]{1,0:T(8,128)(2,1)S(1)}, bf16[640,512]{1,0:T(8,128)(2,1)}, u32[]{:S(2)}, u32[]{:S(2)}) collective-permute-start(bf16[640,512]{1,0:T(8,128)(2,1)S(1)} %copy-done.19), channel_id=1, source_target_pairs={{0,8},{12,4},{1,9},{13,5},{2,10},{14,6},{3,11},{15,7},{16,24},{28,... | collective-permute-start | bytes 1966088 | tf_op jit(solution)/shard_map/ppermute | solution.py:485
  134.7 1.6 collective-permute-start.16
  136.3 2.1 collective-permute-start.17
  138.4 7.9 %for_end.3.refs_4_ = bf16[896,1024]{1,0:T(8,128)(2,1)} custom-call(s32[1]{0:T(128)} %constant.31.clone.1.scalar_ref, bf16[1792,640]{1,0:T(8,128)(2,1)} %copy-done.2, bf16[1792,640]{1,0:T(8,128)(2,1)} %copy-done.1, bf16[1792,640]{1,0:T(8,128)(2,1)} %copy-done.1, bf16[320,1024]{1,0:T(8,128)(2,1)} %get-tuple-element.36.refs_2_.refs_4_.refs_3_, ...), custom_call_target="tpu_custom_call" | custom-call | flops 1 | bytes 1 | tf_op jit(solution)/shard_map/for_end/pallas_call | solution.py:48
  146.3 1.5 collective-permute-start.26
  147.8 1.5 copy-done.11
  149.3 5.9 %pick_rows.5.refs_9_.refs_1_.refs_2_.refs_3_ = bf16[2688,640]{1,0:T(8,128)(2,1)S(1)} custom-call(s32[4]{0:T(128)S(1)} %pad_add_fusion.5.scalar_ref, bf16[272,2688]{1,0:T(8,128)(2,1)} %join_columns.3.refs_9_.refs_0_, bf16[272,2688]{1,0:T(8,128)(2,1)} %collective-permute-done.18.refs_1_, bf16[272,2688]{1,0:T(8,128)(2,1)} %collective-permute-done.19.refs_2_, ...), custom_call_target="tpu_custom_call" | custom-call | flops 1 | bytes 1 | tf_op jit(solution)/shard_map/pick_rows/pallas_call | solution.py:48
  155.3 1.7 copy-done
  157.0 5.2 %collective-permute-done.17.refs_7_ = bf16[640,512]{1,0:T(8,128)(2,1)} collective-permute-done((bf16[640,512]{1,0:T(8,128)(2,1)S(1)}, bf16[640,512]{1,0:T(8,128)(2,1)}, u32[]{:S(2)}, u32[]{:S(2)}) %collective-permute-start.17) | collective-permute-done | bytes 655392 | tf_op jit(solution)/shard_map/ppermute | solution.py:485
  162.2 1.5 copy-done.4
  163.7 4.4 %all-to-all-start.1 = ((bf16[4,160,1536]{2,1,0:T(8,128)(2,1)}), bf16[4,160,1536]{2,1,0:T(8,128)(2,1)}, u32[]{:S(2)}, u32[]{:S(2)}) async-start(bf16[4,160,1536]{2,1,0:T(8,128)(2,1)} %bitcast.33), calls=%async_computation.1 | async-start | bytes 3932160 | tf_op jit(solution)/shard_map/all_to_all | solution.py:488
  168.1 6.5 %collective-permute-start.22 = (bf16[640,512]{1,0:T(8,128)(2,1)}, bf16[640,512]{1,0:T(8,128)(2,1)}, u32[]{:S(2)}, u32[]{:S(2)}) collective-permute-start(bf16[640,512]{1,0:T(8,128)(2,1)} %get-tuple-element.46.refs_4_.refs_3_), channel_id=1, source_target_pairs={{0,8},{12,4},{1,9},{13,5},{2,10},{14,6},{3,11},{15,7},{16,24},{28,... | collective-permute-start | bytes 1966088 | tf_op jit(solution)/shard_map/ppermute | solution.py:485
  174.6 1.5 collective-permute-start.23
  176.1 2.3 collective-permute-start.24
  178.4 5.2 %for_end.4.refs_2_ = bf16[896,512]{1,0:T(8,128)(2,1)} custom-call(s32[1]{0:T(128)} %constant.31.clone.1.scalar_ref, bf16[1792,640]{1,0:T(8,128)(2,1)} %copy-done.2, bf16[1792,640]{1,0:T(8,128)(2,1)} %copy-done.1, bf16[1792,640]{1,0:T(8,128)(2,1)} %copy-done.1, bf16[640,512]{1,0:T(8,128)(2,1)} %get-tuple-element.42.refs_3_.refs_4_, ...), custom_call_target="tpu_custom_call" | custom-call | flops 1 | bytes 1 | tf_op jit(solution)/shard_map/for_end/pallas_call | solution.py:48
  183.7 2.1 combine.2.refs_13_
  185.8 1.6 collective-permute-start.21
  187.3 2.9 %collective-permute-done.26.refs_12_ = bf16[896,1024]{1,0:T(8,128)(2,1)} collective-permute-done((bf16[896,1024]{1,0:T(8,128)(2,1)}, bf16[896,1024]{1,0:T(8,128)(2,1)}, u32[]{:S(2)}, u32[]{:S(2)}) %collective-permute-start.26) | collective-permute-done | bytes 1835040 | tf_op jit(solution)/shard_map/ppermute | solution.py:497
  190.2 1.3 collective-permute-start.25
  191.5 9.8 %for_own.3.refs_9_ = bf16[896,1024]{1,0:T(8,128)(2,1)} custom-call(s32[1]{0:T(128)} %constant.31.clone.1.scalar_ref, bf16[1792,640]{1,0:T(8,128)(2,1)} %copy-done.2, bf16[2688,640]{1,0:T(8,128)(2,1)} %copy-done, bf16[2688,640]{1,0:T(8,128)(2,1)} %copy-done, bf16[2688,640]{1,0:T(8,128)(2,1)} %copy-done, ...), custom_call_target="tpu_custom_call" | custom-call | flops 1 | bytes 1 | tf_op jit(solution)/shard_map/for_own/pallas_call | solution.py:48
  201.4 1.4 collective-permute-done.24.refs_7_
  202.8 5.2 %for_end.5.refs_2_ = bf16[896,512]{1,0:T(8,128)(2,1)} custom-call(s32[1]{0:T(128)} %constant.31.clone.1.scalar_ref, bf16[1792,640]{1,0:T(8,128)(2,1)} %copy-done.2, bf16[1792,640]{1,0:T(8,128)(2,1)} %copy-done.1, bf16[1792,640]{1,0:T(8,128)(2,1)} %copy-done.1, bf16[640,512]{1,0:T(8,128)(2,1)} %get-tuple-element.46.refs_4_.refs_3_, ...), custom_call_target="tpu_custom_call" | custom-call | flops 1 | bytes 1 | tf_op jit(solution)/shard_map/for_end/pallas_call | solution.py:48
  208.0 1.3 collective-permute-start.28
  209.3 1.2 copy-done.13
  210.5 3.2 %combine.3.refs_9_ = bf16[256,1536]{1,0:T(8,128)(2,1)S(1)} custom-call(s32[1]{0:T(128)} %constant.31.clone.1.scalar_ref, s32[2,256]{1,0:T(2,128)S(1)} %bitcast.36, bf16[640,1536]{1,0:T(8,128)(2,1)} %bitcast.22.refs_1_, bf16[896,512]{1,0:T(8,128)(2,1)S(1)} %copy-done.13), custom_call_target="tpu_custom_call" | custom-call | flops 1 | bytes 1 | tf_op jit(solution)/shard_map/combine/pallas_call | solution.py:48
  213.7 1.6 collective-permute-start.27
  215.3 6.4 %for_own.4.refs_8_.refs_2_ = bf16[896,1024]{1,0:T(8,128)(2,1)} custom-call(s32[1]{0:T(128)} %constant.31.clone.1.scalar_ref, bf16[1792,640]{1,0:T(8,128)(2,1)} %copy-done.2, bf16[2688,640]{1,0:T(8,128)(2,1)} %copy-done, bf16[2688,640]{1,0:T(8,128)(2,1)} %copy-done, bf16[2688,640]{1,0:T(8,128)(2,1)} %copy-done, ...), custom_call_target="tpu_custom_call" | custom-call | flops 1 | bytes 1 | tf_op jit(solution)/shard_map/for_own/pallas_call | solution.py:48
  221.7 6.2 %for_own.5.refs_0_ = f32[896,512]{1,0:T(8,128)} custom-call(s32[1]{0:T(128)} %constant.31.clone.1.scalar_ref, bf16[1792,640]{1,0:T(8,128)(2,1)} %copy-done.2, bf16[2688,640]{1,0:T(8,128)(2,1)} %copy-done, bf16[2688,640]{1,0:T(8,128)(2,1)} %copy-done, bf16[2688,640]{1,0:T(8,128)(2,1)} %copy-done, bf16[640,512]{1,0:T(8,128)(2,1)} %get-tuple-element.46.refs_4_.refs_3_, ...), custom_call_target="tpu_custom_call" | custom-call | flops 1 | bytes 1 | tf_op jit(solution)/shard_map/for_own/pallas_call | solution.py:48
  227.9 5.4 %collective-permute-done.28.refs_1_ = bf16[896,512]{1,0:T(8,128)(2,1)} collective-permute-done((bf16[896,512]{1,0:T(8,128)(2,1)}, bf16[896,512]{1,0:T(8,128)(2,1)}, u32[]{:S(2)}, u32[]{:S(2)}) %collective-permute-start.28) | collective-permute-done | bytes 917536 | tf_op jit(solution)/shard_map/ppermute | solution.py:497
  233.3 2.8 %finish.1 = bf16[896,1024]{1,0:T(8,128)(2,1)} custom-call(s32[1]{0:T(128)} %constant.31.clone.1.scalar_ref, f32[896,512]{1,0:T(8,128)} %for_own.5.refs_0_, bf16[896,512]{1,0:T(8,128)(2,1)} %collective-permute-done.28.refs_1_, bf16[896,1024]{1,0:T(8,128)(2,1)} %for_own.4.refs_8_.refs_2_), custom_call_target="tpu_custom_call", output_to_operand_aliasing={{}: (3, {})} | custom-call | flops 1 | bytes 1 | tf_op jit(solution)/shard_map/finish/pallas_call | solution.py:48
  236.1 1.4 maximum_bitcast_fusion
  (65 shorter events, 3.9 us)
Async XLA Ops:
  0.7 1.5 copy-start.3
  2.2 0.7 copy-start.17
  6.0 13.4 %collective-permute-start.4 = (bf16[272,3584]{1,0:T(8,128)(2,1)}, bf16[272,3584]{1,0:T(8,128)(2,1)S(1)}, u32[]{:S(2)}, u32[]{:S(2)}) collective-permute-start(bf16[272,3584]{1,0:T(8,128)(2,1)} %get-tuple-element.26.refs_0_.refs_4_), channel_id=1, source_target_pairs={{0,1},{1,0},{2,3},{3,2},{4,5},{5,4},{6,7},{7,6},{8,9},{9,8},{10,11... | collective-permute-start | bytes 5849096 | tf_op jit(solution)/shard_map/ppermute | solution.py:479
  6.4 46.0 %collective-permute-start = (bf16[272,3584]{1,0:T(8,128)(2,1)}, bf16[272,3584]{1,0:T(8,128)(2,1)}, u32[]{:S(2)}, u32[]{:S(2)}) collective-permute-start(bf16[272,3584]{1,0:T(8,128)(2,1)} %get-tuple-element.26.refs_0_.refs_4_), channel_id=1, source_target_pairs={{0,2},{1,3},{2,0},{3,1},{4,6},{5,7},{6,4},{7,5},{8,10},{9,11},{10,... | collective-permute-start | bytes 5849096 | tf_op jit(solution)/shard_map/ppermute | solution.py:482
  9.0 36.9 %collective-permute-start.1 = (bf16[272,1792]{1,0:T(8,128)(2,1)}, bf16[272,1792]{1,0:T(8,128)(2,1)S(1)}, u32[]{:S(2)}, u32[]{:S(2)}) collective-permute-start(bf16[272,1792]{1,0:T(8,128)(2,1)} %get-tuple-element.27), channel_id=1, source_target_pairs={{0,8},{12,4},{1,9},{13,5},{2,10},{14,6},{3,11},{15,7},{16,24},{28,... | collective-permute-start | bytes 2924552 | tf_op jit(solution)/shard_map/ppermute | solution.py:485
  13.5 32.4 %collective-permute-start.3 = (bf16[272,1792]{1,0:T(8,128)(2,1)}, bf16[272,1792]{1,0:T(8,128)(2,1)}, u32[]{:S(2)}, u32[]{:S(2)}) collective-permute-start(bf16[272,1792]{1,0:T(8,128)(2,1)} %get-tuple-element.29), channel_id=1, source_target_pairs={{4,8},{8,4},{5,9},{9,5},{6,10},{10,6},{7,11},{11,7},{20,24},{24,20... | collective-permute-start | bytes 2924552 | tf_op jit(solution)/shard_map/ppermute | solution.py:485
  15.2 30.7 %collective-permute-start.2 = (bf16[272,896]{1,0:T(8,128)(2,1)}, bf16[272,896]{1,0:T(8,128)(2,1)}, u32[]{:S(2)}, u32[]{:S(2)}) collective-permute-start(bf16[272,896]{1,0:T(8,128)(2,1)} %get-tuple-element.28), channel_id=1, source_target_pairs={{0,4},{12,8},{1,5},{13,9},{2,6},{14,10},{3,7},{15,11},{16,20},{28,... | collective-permute-start | bytes 1462280 | tf_op jit(solution)/shard_map/ppermute | solution.py:485
  19.4 1.4 copy-start.8
  52.4 16.5 %collective-permute-start.5 = (bf16[272,3584]{1,0:T(8,128)(2,1)}, bf16[272,3584]{1,0:T(8,128)(2,1)S(1)}, u32[]{:S(2)}, u32[]{:S(2)}) collective-permute-start(bf16[272,3584]{1,0:T(8,128)(2,1)} %collective-permute-done.refs_5_.refs_0_.refs_2_.refs_6_), channel_id=1, source_target_pairs={{0,1},{1,0},{2,3},{3,2},{4,5},{5,4},{6,7},{7,6},{8,9},{9,8},{10,11... | collective-permute-start | bytes 5849096 | tf_op jit(solution)/shard_map/ppermute | solution.py:479
  54.5 39.6 %collective-permute-start.10 = (bf16[272,1792]{1,0:T(8,128)(2,1)}, bf16[272,1792]{1,0:T(8,128)(2,1)}, u32[]{:S(2)}, u32[]{:S(2)}) collective-permute-start(bf16[272,1792]{1,0:T(8,128)(2,1)} %join_columns.2.refs_6_.refs_0_), channel_id=1, source_target_pairs={{0,2},{1,3},{2,0},{3,1},{4,6},{5,7},{6,4},{7,5},{8,10},{9,11},{10,... | collective-permute-start | bytes 2924552 | tf_op jit(solution)/shard_map/ppermute | solution.py:482
  56.2 37.9 %collective-permute-start.6 = (bf16[320,1024]{1,0:T(8,128)(2,1)}, bf16[320,1024]{1,0:T(8,128)(2,1)}, u32[]{:S(2)}, u32[]{:S(2)}) collective-permute-start(bf16[320,1024]{1,0:T(8,128)(2,1)} %get-tuple-element.36.refs_2_.refs_4_.refs_3_), channel_id=1, source_target_pairs={{0,8},{12,4},{1,9},{13,5},{2,10},{14,6},{3,11},{15,7},{16,24},{28,... | collective-permute-start | bytes 1966088 | tf_op jit(solution)/shard_map/ppermute | solution.py:485
  64.6 29.5 %collective-permute-start.7 = (bf16[320,1024]{1,0:T(8,128)(2,1)}, bf16[320,1024]{1,0:T(8,128)(2,1)}, u32[]{:S(2)}, u32[]{:S(2)}) collective-permute-start(bf16[320,1024]{1,0:T(8,128)(2,1)} %get-tuple-element.36.refs_2_.refs_4_.refs_3_), channel_id=1, source_target_pairs={{0,4},{12,8},{1,5},{13,9},{2,6},{14,10},{3,7},{15,11},{16,20},{28,... | collective-permute-start | bytes 1966088 | tf_op jit(solution)/shard_map/ppermute | solution.py:485
  66.7 27.4 %collective-permute-start.8 = (bf16[320,1024]{1,0:T(8,128)(2,1)}, bf16[320,1024]{1,0:T(8,128)(2,1)}, u32[]{:S(2)}, u32[]{:S(2)}) collective-permute-start(bf16[320,1024]{1,0:T(8,128)(2,1)} %get-tuple-element.36.refs_2_.refs_4_.refs_3_), channel_id=1, source_target_pairs={{4,8},{8,4},{5,9},{9,5},{6,10},{10,6},{7,11},{11,7},{20,24},{24,20... | collective-permute-start | bytes 1966088 | tf_op jit(solution)/shard_map/ppermute | solution.py:485
  68.9 1.3 copy-start.6
  83.7 1.5 copy-start.7
  85.2 1.5 copy-start.9
  90.9 3.1 %copy-start.2 = (bf16[1792,640]{1,0:T(8,128)(2,1)}, bf16[1792,640]{1,0:T(8,128)(2,1)S(1)}, u32[]{:S(2)}) copy-start(bf16[1792,640]{1,0:T(8,128)(2,1)S(1)} %pick_rows.3.refs_3_.refs_0_) | copy-start | bytes 6881284
  94.1 8.6 %collective-permute-start.11 = (bf16[272,1792]{1,0:T(8,128)(2,1)}, bf16[272,1792]{1,0:T(8,128)(2,1)S(1)}, u32[]{:S(2)}, u32[]{:S(2)}) collective-permute-start(bf16[272,1792]{1,0:T(8,128)(2,1)} %collective-permute-done.10.refs_2_), channel_id=1, source_target_pairs={{0,1},{1,0},{2,3},{3,2},{4,5},{5,4},{6,7},{7,6},{8,9},{9,8},{10,11... | collective-permute-start | bytes 2924552 | tf_op jit(solution)/shard_map/ppermute | solution.py:479
  94.2 28.5 %collective-permute-start.9 = (bf16[272,1792]{1,0:T(8,128)(2,1)}, bf16[272,1792]{1,0:T(8,128)(2,1)}, u32[]{:S(2)}, u32[]{:S(2)}) collective-permute-start(bf16[272,1792]{1,0:T(8,128)(2,1)} %join_columns.2.refs_6_.refs_0_), channel_id=1, source_target_pairs={{0,1},{1,0},{2,3},{3,2},{4,5},{5,4},{6,7},{7,6},{8,9},{9,8},{10,11... | collective-permute-start | bytes 2924552 | tf_op jit(solution)/shard_map/ppermute | solution.py:479
  94.7 37.0 %collective-permute-start.19 = (bf16[272,2688]{1,0:T(8,128)(2,1)}, bf16[272,2688]{1,0:T(8,128)(2,1)}, u32[]{:S(2)}, u32[]{:S(2)}) collective-permute-start(bf16[272,2688]{1,0:T(8,128)(2,1)} %join_columns.3.refs_9_.refs_0_), channel_id=1, source_target_pairs={{0,2},{1,3},{2,0},{3,1},{4,6},{5,7},{6,4},{7,5},{8,10},{9,11},{10,... | collective-permute-start | bytes 4386824 | tf_op jit(solution)/shard_map/ppermute | solution.py:482
  96.2 34.9 %collective-permute-start.12 = (bf16[320,1024]{1,0:T(8,128)(2,1)}, bf16[320,1024]{1,0:T(8,128)(2,1)}, u32[]{:S(2)}, u32[]{:S(2)}) collective-permute-start(bf16[320,1024]{1,0:T(8,128)(2,1)} %get-tuple-element.41.refs_8_.refs_2_.refs_4_.refs_5_), channel_id=1, source_target_pairs={{0,8},{12,4},{1,9},{13,5},{2,10},{14,6},{3,11},{15,7},{16,24},{28,... | collective-permute-start | bytes 1966088 | tf_op jit(solution)/shard_map/ppermute | solution.py:485
  100.6 30.5 %collective-permute-start.13 = (bf16[320,1024]{1,0:T(8,128)(2,1)}, bf16[320,1024]{1,0:T(8,128)(2,1)}, u32[]{:S(2)}, u32[]{:S(2)}) collective-permute-start(bf16[320,1024]{1,0:T(8,128)(2,1)} %get-tuple-element.41.refs_8_.refs_2_.refs_4_.refs_5_), channel_id=1, source_target_pairs={{0,4},{12,8},{1,5},{13,9},{2,6},{14,10},{3,7},{15,11},{16,20},{28,... | collective-permute-start | bytes 1966088 | tf_op jit(solution)/shard_map/ppermute | solution.py:485
  102.7 0.9 copy-start.15
  103.7 27.5 %collective-permute-start.14 = (bf16[320,1024]{1,0:T(8,128)(2,1)}, bf16[320,1024]{1,0:T(8,128)(2,1)}, u32[]{:S(2)}, u32[]{:S(2)}) collective-permute-start(bf16[320,1024]{1,0:T(8,128)(2,1)} %get-tuple-element.41.refs_8_.refs_2_.refs_4_.refs_5_), channel_id=1, source_target_pairs={{4,8},{8,4},{5,9},{9,5},{6,10},{10,6},{7,11},{11,7},{20,24},{24,20... | collective-permute-start | bytes 1966088 | tf_op jit(solution)/shard_map/ppermute | solution.py:485
  119.0 43.2 %all-to-all-start = ((bf16[4,160,2048]{2,1,0:T(8,128)(2,1)}), bf16[4,160,2048]{2,1,0:T(8,128)(2,1)S(1)}, u32[]{:S(2)}, u32[]{:S(2)}) async-start(bf16[4,160,2048]{2,1,0:T(8,128)(2,1)} %bitcast.49), calls=%async_computation | async-start | bytes 5242880 | tf_op jit(solution)/shard_map/all_to_all | solution.py:488
  122.7 1.5 copy-start.10
  124.2 1.2 copy-start.16
  125.4 6.3 %copy-start.19 = (bf16[640,512]{1,0:T(8,128)(2,1)S(1)}, bf16[640,512]{1,0:T(8,128)(2,1)}, u32[]{:S(2)}) copy-start(bf16[640,512]{1,0:T(8,128)(2,1)} %get-tuple-element.42.refs_3_.refs_4_) | copy-start | bytes 1966084
  129.7 1.4 copy-start.1
  131.1 15.1 %collective-permute-start.18 = (bf16[272,2688]{1,0:T(8,128)(2,1)}, bf16[272,2688]{1,0:T(8,128)(2,1)}, u32[]{:S(2)}, u32[]{:S(2)}) collective-permute-start(bf16[272,2688]{1,0:T(8,128)(2,1)} %join_columns.3.refs_9_.refs_0_), channel_id=1, source_target_pairs={{0,1},{1,0},{2,3},{3,2},{4,5},{5,4},{6,7},{7,6},{8,9},{9,8},{10,11... | collective-permute-start | bytes 4386824 | tf_op jit(solution)/shard_map/ppermute | solution.py:479
  131.7 16.2 %collective-permute-start.20 = (bf16[272,2688]{1,0:T(8,128)(2,1)}, bf16[272,2688]{1,0:T(8,128)(2,1)}, u32[]{:S(2)}, u32[]{:S(2)}) collective-permute-start(bf16[272,2688]{1,0:T(8,128)(2,1)} %collective-permute-done.19.refs_2_), channel_id=1, source_target_pairs={{0,1},{1,0},{2,3},{3,2},{4,5},{5,4},{6,7},{7,6},{8,9},{9,8},{10,11... | collective-permute-start | bytes 4386824 | tf_op jit(solution)/shard_map/ppermute | solution.py:479
  131.8 25.2 %collective-permute-start.15 = (bf16[640,512]{1,0:T(8,128)(2,1)S(1)}, bf16[640,512]{1,0:T(8,128)(2,1)}, u32[]{:S(2)}, u32[]{:S(2)}) collective-permute-start(bf16[640,512]{1,0:T(8,128)(2,1)S(1)} %copy-done.19), channel_id=1, source_target_pairs={{0,8},{12,4},{1,9},{13,5},{2,10},{14,6},{3,11},{15,7},{16,24},{28,... | collective-permute-start | bytes 1966088 | tf_op jit(solution)/shard_map/ppermute | solution.py:485
  134.7 22.3 %collective-permute-start.16 = (bf16[640,512]{1,0:T(8,128)(2,1)S(1)}, bf16[640,512]{1,0:T(8,128)(2,1)}, u32[]{:S(2)}, u32[]{:S(2)}) collective-permute-start(bf16[640,512]{1,0:T(8,128)(2,1)S(1)} %copy-done.19), channel_id=1, source_target_pairs={{4,8},{8,4},{5,9},{9,5},{6,10},{10,6},{7,11},{11,7},{20,24},{24,20... | collective-permute-start | bytes 1966088 | tf_op jit(solution)/shard_map/ppermute | solution.py:485
  136.3 25.9 %collective-permute-start.17 = (bf16[640,512]{1,0:T(8,128)(2,1)S(1)}, bf16[640,512]{1,0:T(8,128)(2,1)}, u32[]{:S(2)}, u32[]{:S(2)}) collective-permute-start(bf16[640,512]{1,0:T(8,128)(2,1)S(1)} %copy-done.19), channel_id=1, source_target_pairs={{0,4},{12,8},{1,5},{13,9},{2,6},{14,10},{3,7},{15,11},{16,20},{28,... | collective-permute-start | bytes 1966088 | tf_op jit(solution)/shard_map/ppermute | solution.py:485
  146.3 44.0 %collective-permute-start.26 = (bf16[896,1024]{1,0:T(8,128)(2,1)}, bf16[896,1024]{1,0:T(8,128)(2,1)}, u32[]{:S(2)}, u32[]{:S(2)}) collective-permute-start(bf16[896,1024]{1,0:T(8,128)(2,1)} %for_end.3.refs_4_), channel_id=1, source_target_pairs={{4,0},{8,12},{5,1},{9,13},{6,2},{10,14},{7,3},{11,15},{20,16},{24,... | collective-permute-start | bytes 5505032 | tf_op jit(solution)/shard_map/ppermute | solution.py:497
  147.8 1.5 copy-start.11
  155.2 1.7 copy-start
  162.2 1.5 copy-start.4
  163.7 45.6 %all-to-all-start.1 = ((bf16[4,160,1536]{2,1,0:T(8,128)(2,1)}), bf16[4,160,1536]{2,1,0:T(8,128)(2,1)}, u32[]{:S(2)}, u32[]{:S(2)}) async-start(bf16[4,160,1536]{2,1,0:T(8,128)(2,1)} %bitcast.33), calls=%async_computation.1 | async-start | bytes 3932160 | tf_op jit(solution)/shard_map/all_to_all | solution.py:488
  168.1 15.5 %copy-start.5 = (bf16[4,160,2048]{2,1,0:T(8,128)(2,1)S(1)}, bf16[4,160,2048]{2,1,0:T(8,128)(2,1)}, u32[]{:S(2)}) copy-start(bf16[4,160,2048]{2,1,0:T(8,128)(2,1)} %copy-done.4) | copy-start | bytes 7864324
  168.1 15.5 %copy-start.18 = (s32[1,256,2]{1,2,0:T(2,128)S(1)}, s32[1,256,2]{1,2,0:T(2,128)}, u32[]{:S(2)}) copy-start(s32[1,256,2]{1,2,0:T(2,128)} %param.6) | copy-start | bytes 6148
  168.1 33.2 %collective-permute-start.22 = (bf16[640,512]{1,0:T(8,128)(2,1)}, bf16[640,512]{1,0:T(8,128)(2,1)}, u32[]{:S(2)}, u32[]{:S(2)}) collective-permute-start(bf16[640,512]{1,0:T(8,128)(2,1)} %get-tuple-element.46.refs_4_.refs_3_), channel_id=1, source_target_pairs={{0,8},{12,4},{1,9},{13,5},{2,10},{14,6},{3,11},{15,7},{16,24},{28,... | collective-permute-start | bytes 1966088 | tf_op jit(solution)/shard_map/ppermute | solution.py:485
  174.6 26.8 %collective-permute-start.23 = (bf16[640,512]{1,0:T(8,128)(2,1)}, bf16[640,512]{1,0:T(8,128)(2,1)}, u32[]{:S(2)}, u32[]{:S(2)}) collective-permute-start(bf16[640,512]{1,0:T(8,128)(2,1)} %get-tuple-element.46.refs_4_.refs_3_), channel_id=1, source_target_pairs={{4,8},{8,4},{5,9},{9,5},{6,10},{10,6},{7,11},{11,7},{20,24},{24,20... | collective-permute-start | bytes 1966088 | tf_op jit(solution)/shard_map/ppermute | solution.py:485
  176.1 26.6 %collective-permute-start.24 = (bf16[640,512]{1,0:T(8,128)(2,1)}, bf16[640,512]{1,0:T(8,128)(2,1)}, u32[]{:S(2)}, u32[]{:S(2)}) collective-permute-start(bf16[640,512]{1,0:T(8,128)(2,1)} %get-tuple-element.46.refs_4_.refs_3_), channel_id=1, source_target_pairs={{0,4},{12,8},{1,5},{13,9},{2,6},{14,10},{3,7},{15,11},{16,20},{28,... | collective-permute-start | bytes 1966088 | tf_op jit(solution)/shard_map/ppermute | solution.py:485
  185.8 5.8 %copy-start.12 = (bf16[256,2048]{1,0:T(8,128)(2,1)}, bf16[256,2048]{1,0:T(8,128)(2,1)S(1)}, u32[]{:S(2)}) copy-start(bf16[256,2048]{1,0:T(8,128)(2,1)S(1)} %combine.2.refs_13_) | copy-start | bytes 3145732
  185.8 42.2 %collective-permute-start.21 = (bf16[256,2048]{1,0:T(8,128)(2,1)S(1)}, bf16[256,2048]{1,0:T(8,128)(2,1)S(1)}, u32[]{:S(2)}, u32[]{:S(2)}) collective-permute-start(bf16[256,2048]{1,0:T(8,128)(2,1)S(1)} %combine.2.refs_13_), channel_id=1, source_target_pairs={{0,16},{16,0},{1,17},{17,1},{2,18},{18,2},{3,19},{19,3},{4,20},{20... | collective-permute-start | bytes 3145736 | tf_op jit(solution)/shard_map/ppermute | solution.py:494
  190.2 25.1 %collective-permute-start.25 = (bf16[896,512]{1,0:T(8,128)(2,1)}, bf16[896,512]{1,0:T(8,128)(2,1)}, u32[]{:S(2)}, u32[]{:S(2)}) collective-permute-start(bf16[896,512]{1,0:T(8,128)(2,1)} %for_end.4.refs_2_), channel_id=1, source_target_pairs={{4,0},{8,12},{5,1},{9,13},{6,2},{10,14},{7,3},{11,15},{20,16},{24,... | collective-permute-start | bytes 2752520 | tf_op jit(solution)/shard_map/ppermute | solution.py:497
  208.0 25.3 %collective-permute-start.28 = (bf16[896,512]{1,0:T(8,128)(2,1)}, bf16[896,512]{1,0:T(8,128)(2,1)}, u32[]{:S(2)}, u32[]{:S(2)}) collective-permute-start(bf16[896,512]{1,0:T(8,128)(2,1)} %for_end.5.refs_2_), channel_id=1, source_target_pairs={{4,0},{8,12},{5,1},{9,13},{6,2},{10,14},{7,3},{11,15},{20,16},{24,... | collective-permute-start | bytes 2752520 | tf_op jit(solution)/shard_map/ppermute | solution.py:497
  209.3 1.2 copy-start.13
  213.7 1.6 copy-start.14
  213.7 22.4 %collective-permute-start.27 = (bf16[256,1536]{1,0:T(8,128)(2,1)S(1)}, bf16[256,1536]{1,0:T(8,128)(2,1)S(1)}, u32[]{:S(2)}, u32[]{:S(2)}) collective-permute-start(bf16[256,1536]{1,0:T(8,128)(2,1)S(1)} %combine.3.refs_9_), channel_id=1, source_target_pairs={{0,16},{16,0},{1,17},{17,1},{2,18},{18,2},{3,19},{19,3},{4,20},{20... | collective-permute-start | bytes 2359304 | tf_op jit(solution)/shard_map/ppermute | solution.py:494
